TPU v7x, 256 devices: a whole 4x4x8 slice. The times are simulated.
256 devices in a mesh: dp: 8 (over z), phase: 4 (over y), dom: 8 (over x, core).
Axes of the slice: x: 4, y: 4, z: 8, core: 2. Of those that a mesh axis runs over, the one named last changes fastest.
Arguments:
- initial: bfloat16 [32, 2048, 256], P('dp', 'dom'), may hold values from -6 to 6
- block_cols: int32 [32, 16, 5], P('dp', 'dom'), may hold values from 0 to 15, as said below
- block_tiles: bfloat16 [32, 16, 5, 128, 128], P('dp', 'dom')
- layer_weights: bfloat16 [4, 256, 256], P('phase'), may hold values from -0.375 to 0.375
- cotangent: bfloat16 [32, 2048, 256], P('dp', 'dom'), may hold values from -6 to 6
Outputs:
- grad_initial: float32 [32, 2048, 256], P(('dp', 'phase'), 'dom')
- grad_weights: float32 [4, 256, 256], P('phase')
Inputs may be any that keep to these rules, and one draw needn't show every extreme that they name: `block_cols`: in every span the matrix P_c is symmetric, and slot 0 of each block row names that block row itself.
All inputs are finite; a program needn't handle non-finite values.
Results may differ from a plain program's by a relative error of at most 0.008.
Values may be sent and summed in bfloat16 or wider, within the bound.
No kernel may reach another device: no remote copies, remote signals or barrier semaphores. Data moves between devices by JAX's collectives and lax.ppermute only.
A program may use at most 64 MiB of HBM per device.

v0:
```python
import math

import jax
import jax.numpy as jnp
from jax import lax
from jax.sharding import PartitionSpec as P

alpha_mix = 0.1
theta_coef = 0.5


def from_behind(block, axis, distance):
    devices = range(lax.axis_size(axis))
    route = [(i - distance, i) for i in devices if i - distance in devices]
    return lax.ppermute(block, axis, route)


def gelu_tanh(inputs):
    return jax.nn.gelu(inputs, approximate=True)


def pick_blocks(gathered, cols_m, block_rows):
    blocks = gathered.reshape(-1, block_rows, gathered.shape[-1])
    return blocks[cols_m]


def apply_tiles(tiles_m, picked):
    result = jnp.einsum("ikrc,ikch->irh", tiles_m, picked, preferred_element_type=jnp.float32)
    return result.reshape(-1, result.shape[-1])


def local(initial, block_cols, block_tiles, layer_weights, cotangent):
    spans_here, rows_here, feat_width = initial.shape
    block_rows = block_tiles.shape[-1]
    layers_here = layer_weights.shape[0]
    phases = lax.axis_size("phase")
    phase_now = lax.axis_index("phase")
    tick_count = spans_here + phases - 1
    grad_scale = 1.0 / math.sqrt(
        spans_here * lax.axis_size("dp") * rows_here * lax.axis_size("dom")
    )
    layer_ids = phase_now * layers_here + jnp.arange(layers_here, dtype=jnp.int32)
    beta_table = jnp.log(theta_coef / (layer_ids.astype(jnp.float32) + 1.0) + 1.0)

    def layer_forward(hidden_state, start_m, tiles_m, cols_m, weight, beta_now):
        gathered = lax.all_gather(hidden_state, "dom", axis=0, tiled=True)
        aggregated = apply_tiles(tiles_m, pick_blocks(gathered, cols_m, block_rows))
        mix_rows = (
            (1.0 - alpha_mix) * aggregated + alpha_mix * start_m.astype(jnp.float32)
        ).astype(jnp.bfloat16)
        pre_act = (1.0 - beta_now) * mix_rows.astype(jnp.float32) + beta_now * jnp.dot(
            mix_rows, weight, preferred_element_type=jnp.float32
        )
        return (mix_rows, pre_act, gelu_tanh(pre_act).astype(jnp.bfloat16))

    def forward_tick(tick_now, carry):
        incoming, saved_mix, saved_pre = carry
        span_id = tick_now - phase_now
        is_valid = (span_id >= 0) & (span_id < spans_here)
        slot_index = jnp.clip(span_id, 0, spans_here - 1)
        start_m = initial[slot_index]
        tiles_m = block_tiles[slot_index]
        cols_m = block_cols[slot_index]
        hidden_state = jnp.where(phase_now == 0, start_m, incoming)
        mix_rows, pre_act, hidden_state = layer_forward(
            hidden_state, start_m, tiles_m, cols_m, layer_weights[0], beta_table[0]
        )
        saved_mix = saved_mix.at[slot_index, 0].set(
            jnp.where(is_valid, mix_rows, saved_mix[slot_index, 0])
        )
        saved_pre = saved_pre.at[slot_index, 0].set(
            jnp.where(is_valid, pre_act, saved_pre[slot_index, 0])
        )
        incoming = from_behind(hidden_state, "phase", 1)
        return (incoming, saved_mix, saved_pre)

    first_in = jnp.zeros((rows_here, feat_width), jnp.bfloat16)
    mix_store = jnp.zeros((spans_here, layers_here, rows_here, feat_width), jnp.bfloat16)
    pre_store = jnp.zeros((spans_here, layers_here, rows_here, feat_width), jnp.float32)
    _, mix_store, pre_store = lax.fori_loop(
        0, tick_count, forward_tick, (first_in, mix_store, pre_store)
    )

    def layer_backward(hidden_grad, mix_rows, pre_act, tiles_m, cols_m, weight, beta_now):
        _, pullback = jax.vjp(gelu_tanh, pre_act)
        grad_pre = pullback(hidden_grad.astype(jnp.float32))[0].astype(jnp.bfloat16)
        weight_term = beta_now * jnp.einsum(
            "nh,ng->hg", mix_rows, grad_pre, preferred_element_type=jnp.float32
        )
        grad_mix = (
            (1.0 - beta_now) * grad_pre.astype(jnp.float32)
            + beta_now
            * jnp.einsum("ng,hg->nh", grad_pre, weight, preferred_element_type=jnp.float32)
        ).astype(jnp.bfloat16)
        gathered = lax.all_gather(grad_mix, "dom", axis=0, tiled=True)
        spread = apply_tiles(tiles_m, pick_blocks(gathered, cols_m, block_rows))
        grad_prev = ((1.0 - alpha_mix) * spread).astype(jnp.bfloat16)
        return (weight_term, grad_mix, grad_prev)

    def backward_tick(tick_now, carry):
        incoming, grad_start, grad_acc = carry
        span_id = tick_now - (phases - 1 - phase_now)
        is_valid = (span_id >= 0) & (span_id < spans_here)
        slot_index = jnp.clip(span_id, 0, spans_here - 1)
        weight_mask = is_valid.astype(jnp.float32)
        tiles_m = block_tiles[slot_index]
        cols_m = block_cols[slot_index]
        hidden_grad = jnp.where(phase_now == phases - 1, cotangent[slot_index], incoming)
        local_sum = jnp.zeros((rows_here, feat_width), jnp.float32)
        for layer_idx in reversed(range(layers_here)):
            weight_term, grad_mix, hidden_grad = layer_backward(
                hidden_grad,
                mix_store[slot_index, layer_idx],
                pre_store[slot_index, layer_idx],
                tiles_m,
                cols_m,
                layer_weights[layer_idx],
                beta_table[layer_idx],
            )
            weight_term = weight_term * (weight_mask * grad_scale)
            weight_term = lax.psum(weight_term, ("dp", "dom"))
            grad_acc = grad_acc.at[layer_idx].add(weight_term)
            local_sum = alpha_mix * grad_mix.astype(jnp.float32)
        local_sum = local_sum + jnp.where(phase_now == 0, hidden_grad.astype(jnp.float32), 0.0)
        grad_start = grad_start.at[slot_index].add(weight_mask * local_sum)
        incoming = from_behind(hidden_grad, "phase", -1)
        return (incoming, grad_start, grad_acc)

    start_grads = jnp.zeros((spans_here, rows_here, feat_width), jnp.float32)
    weight_grads = jnp.zeros((layers_here, feat_width, feat_width), jnp.float32)
    _, start_grads, weight_grads = lax.fori_loop(
        0, tick_count, backward_tick, (first_in, start_grads, weight_grads)
    )
    grad_initial = lax.psum_scatter(start_grads, "phase", scatter_dimension=0, tiled=True)
    return (grad_initial, weight_grads)


def solution(mesh):
    placed = (
        P("dp", "dom", None),
        P("dp", "dom", None),
        P("dp", "dom", None, None, None),
        P("phase", None, None),
        P("dp", "dom", None),
    )
    return jax.shard_map(
        local,
        mesh=mesh,
        in_specs=placed,
        out_specs=(P(("dp", "phase"), "dom", None), P("phase", None, None)),
        check_vma=False,
    )
```

profile of v0, /device:TPU:1, one launch (start us, length us, event | category | flops | bytes accessed | tf_op | source)
XLA Modules:
  0.0 1652.6 jit_solution(5714047633703269271)
XLA Ops:
  9.2 283.3 %while.43 = (s32[]{:T(128)}, bf16[256,256]{1,0:T(8,128)(2,1)S(1)}, bf16[4,1,256,256]{3,2,1,0:T(8,128)(2,1)}, f32[4,1,256,256]{3,2,1,0:T(8,128)S(1)}, f32[]{:T(12...) while((s32[]{:T(128)}, bf16[256,256]{1,0:T(8,128)(2,1)S(1)}, ...), condition=%wide.region_2.3_spmd, body=%wide.region_0.2_spmd.sunk | while | flops 119473208 | bytes 11081819 | solution.py:80
  10.9 31.9 %all-gather.3.cloned.1.call-done = bf16[2048,256]{1,0:T(8,128)(2,1)} async-done(((bf16[256,256]{1,0:T(8,128)(2,1)}), bf16[2048,256]{1,0:T(8,128)(2,1)}) %all-gather.3.cloned.1.call-update) | async-done | bytes 1048592 | tf_op jit(solution)/shard_map/while/body/eval_jaxpr/all_gather | solution.py:46
  46.2 3.1 collective-permute-start
  50.0 2.3 fusion.70
  54.0 28.9 %all-gather.3.cloned.1.call-done = bf16[2048,256]{1,0:T(8,128)(2,1)} async-done(((bf16[256,256]{1,0:T(8,128)(2,1)}), bf16[2048,256]{1,0:T(8,128)(2,1)}) %all-gather.3.cloned.1.call-update) | async-done | bytes 1048592 | tf_op jit(solution)/shard_map/while/body/eval_jaxpr/all_gather | solution.py:46
  86.3 3.1 collective-permute-start
  90.2 2.3 fusion.70
  94.2 28.9 %all-gather.3.cloned.1.call-done = bf16[2048,256]{1,0:T(8,128)(2,1)} async-done(((bf16[256,256]{1,0:T(8,128)(2,1)}), bf16[2048,256]{1,0:T(8,128)(2,1)}) %all-gather.3.cloned.1.call-update) | async-done | bytes 1048592 | tf_op jit(solution)/shard_map/while/body/eval_jaxpr/all_gather | solution.py:46
  126.5 3.1 collective-permute-start
  130.4 2.3 fusion.70
  134.3 28.6 %all-gather.3.cloned.1.call-done = bf16[2048,256]{1,0:T(8,128)(2,1)} async-done(((bf16[256,256]{1,0:T(8,128)(2,1)}), bf16[2048,256]{1,0:T(8,128)(2,1)}) %all-gather.3.cloned.1.call-update) | async-done | bytes 1048592 | tf_op jit(solution)/shard_map/while/body/eval_jaxpr/all_gather | solution.py:46
  166.4 3.1 collective-permute-start
  170.2 2.3 fusion.70
  174.2 28.6 %all-gather.3.cloned.1.call-done = bf16[2048,256]{1,0:T(8,128)(2,1)} async-done(((bf16[256,256]{1,0:T(8,128)(2,1)}), bf16[2048,256]{1,0:T(8,128)(2,1)}) %all-gather.3.cloned.1.call-update) | async-done | bytes 1048592 | tf_op jit(solution)/shard_map/while/body/eval_jaxpr/all_gather | solution.py:46
  206.2 3.1 collective-permute-start
  210.1 2.3 fusion.70
  214.1 28.6 %all-gather.3.cloned.1.call-done = bf16[2048,256]{1,0:T(8,128)(2,1)} async-done(((bf16[256,256]{1,0:T(8,128)(2,1)}), bf16[2048,256]{1,0:T(8,128)(2,1)}) %all-gather.3.cloned.1.call-update) | async-done | bytes 1048592 | tf_op jit(solution)/shard_map/while/body/eval_jaxpr/all_gather | solution.py:46
  246.1 3.1 collective-permute-start
  249.9 2.3 fusion.70
  254.0 28.9 %all-gather.3.cloned.1.call-done = bf16[2048,256]{1,0:T(8,128)(2,1)} async-done(((bf16[256,256]{1,0:T(8,128)(2,1)}), bf16[2048,256]{1,0:T(8,128)(2,1)}) %all-gather.3.cloned.1.call-update) | async-done | bytes 1048592 | tf_op jit(solution)/shard_map/while/body/eval_jaxpr/all_gather | solution.py:46
  286.3 3.1 collective-permute-start
  290.1 2.3 fusion.70
  292.5 1327.9 %while.44 = (s32[]{:T(128)}, bf16[256,256]{1,0:T(8,128)(2,1)S(1)}, f32[4,256,256]{2,1,0:T(8,128)S(1)}, f32[1,256,256]{2,1,0:T(8,128)S(1)}, s32[]{:T(128)}, /*ind...) while((s32[]{:T(128)}, bf16[256,256]{1,0:T(8,128)(2,1)S(1)}, ...), condition=%wide.region_6.7_spmd.clone, body=%wide.region_3.6_spmd.clone.sunk | while | flops 153748528 | bytes 11737306 | solution.py:131
  293.7 1.8 fusion.82
  297.4 176.9 %all-reduce.2.cloned.1.call-done = f32[1,256,256]{2,1,0:T(8,128)} async-done(((f32[1,256,256]{2,1,0:T(8,128)}), f32[1,256,256]{2,1,0:T(8,128)}) %all-reduce.2.cloned.1.call-update) | async-done | bytes 262160 | tf_op jit(solution)/shard_map/while/body/eval_jaxpr/psum | solution.py:121
  475.4 1.8 gather_fusion.1
  480.5 4.8 collective-permute-done.1
  486.4 1.8 fusion.82
  490.1 173.5 %all-reduce.2.cloned.1.call-done = f32[1,256,256]{2,1,0:T(8,128)} async-done(((f32[1,256,256]{2,1,0:T(8,128)}), f32[1,256,256]{2,1,0:T(8,128)}) %all-reduce.2.cloned.1.call-update) | async-done | bytes 262160 | tf_op jit(solution)/shard_map/while/body/eval_jaxpr/psum | solution.py:121
  664.6 1.8 gather_fusion.1
  669.7 4.8 collective-permute-done.1
  679.3 173.4 %all-reduce.2.cloned.1.call-done = f32[1,256,256]{2,1,0:T(8,128)} async-done(((f32[1,256,256]{2,1,0:T(8,128)}), f32[1,256,256]{2,1,0:T(8,128)}) %all-reduce.2.cloned.1.call-update) | async-done | bytes 262160 | tf_op jit(solution)/shard_map/while/body/eval_jaxpr/psum | solution.py:121
  853.7 1.8 gather_fusion.1
  858.8 4.8 collective-permute-done.1
  864.7 1.8 fusion.82
  868.4 173.5 %all-reduce.2.cloned.1.call-done = f32[1,256,256]{2,1,0:T(8,128)} async-done(((f32[1,256,256]{2,1,0:T(8,128)}), f32[1,256,256]{2,1,0:T(8,128)}) %all-reduce.2.cloned.1.call-update) | async-done | bytes 262160 | tf_op jit(solution)/shard_map/while/body/eval_jaxpr/psum | solution.py:121
  1043.0 1.8 gather_fusion.1
  1048.1 4.8 collective-permute-done.1
  1057.6 173.7 %all-reduce.2.cloned.1.call-done = f32[1,256,256]{2,1,0:T(8,128)} async-done(((f32[1,256,256]{2,1,0:T(8,128)}), f32[1,256,256]{2,1,0:T(8,128)}) %all-reduce.2.cloned.1.call-update) | async-done | bytes 262160 | tf_op jit(solution)/shard_map/while/body/eval_jaxpr/psum | solution.py:121
  1232.4 1.8 gather_fusion.1
  1237.4 4.8 collective-permute-done.1
  1247.0 173.6 %all-reduce.2.cloned.1.call-done = f32[1,256,256]{2,1,0:T(8,128)} async-done(((f32[1,256,256]{2,1,0:T(8,128)}), f32[1,256,256]{2,1,0:T(8,128)}) %all-reduce.2.cloned.1.call-update) | async-done | bytes 262160 | tf_op jit(solution)/shard_map/while/body/eval_jaxpr/psum | solution.py:121
  1421.6 1.8 gather_fusion.1
  1426.7 4.8 collective-permute-done.1
  1436.3 173.3 %all-reduce.2.cloned.1.call-done = f32[1,256,256]{2,1,0:T(8,128)} async-done(((f32[1,256,256]{2,1,0:T(8,128)}), f32[1,256,256]{2,1,0:T(8,128)}) %all-reduce.2.cloned.1.call-update) | async-done | bytes 262160 | tf_op jit(solution)/shard_map/while/body/eval_jaxpr/psum | solution.py:121
  1610.6 1.8 gather_fusion.1
  1615.7 4.8 collective-permute-done.1
  1621.5 24.0 %reduce-scatter.2.cloned.1.call-done = f32[1,256,256]{2,1,0:T(8,128)} async-done(((f32[4,256,256]{2,1,0:T(8,128)}), f32[1,256,256]{2,1,0:T(8,128)}) %reduce-scatter.2.cloned.1.call-update) | async-done | bytes 262160 | tf_op jit(solution)/shard_map/reduce_scatter | solution.py:134
  (250 shorter events, 99.6 us)
Async XLA Ops:
  8.0 1.1 copy-start.6
  8.0 1.1 copy-start
  8.0 1.1 copy-start.4
  9.2 283.4 %copy-start.5 = (s32[3]{0:T(128)S(1)}, s32[3]{0:T(128)}, u32[]{:S(2)}) copy-start(s32[3]{0:T(128)} %constant.446.clone.2) | copy-start | bytes 40
  9.2 33.6 %all-gather.3.cloned.1.call-start = ((), (), s32[]{:S(2)}) async-start(), calls=%async_computation.2 | async-start | bytes 1179648 | tf_op jit(solution)/shard_map/while/body/eval_jaxpr/all_gather | solution.py:46
  46.2 6.2 collective-permute-start
  52.3 30.6 %all-gather.3.cloned.1.call-start = ((), (), s32[]{:S(2)}) async-start(), calls=%async_computation.2 | async-start | bytes 1179648 | tf_op jit(solution)/shard_map/while/body/eval_jaxpr/all_gather | solution.py:46
  86.3 6.2 collective-permute-start
  92.5 30.6 %all-gather.3.cloned.1.call-start = ((), (), s32[]{:S(2)}) async-start(), calls=%async_computation.2 | async-start | bytes 1179648 | tf_op jit(solution)/shard_map/while/body/eval_jaxpr/all_gather | solution.py:46
  126.5 6.2 collective-permute-start
  132.7 30.3 %all-gather.3.cloned.1.call-start = ((), (), s32[]{:S(2)}) async-start(), calls=%async_computation.2 | async-start | bytes 1179648 | tf_op jit(solution)/shard_map/while/body/eval_jaxpr/all_gather | solution.py:46
  166.4 6.2 collective-permute-start
  172.5 30.3 %all-gather.3.cloned.1.call-start = ((), (), s32[]{:S(2)}) async-start(), calls=%async_computation.2 | async-start | bytes 1179648 | tf_op jit(solution)/shard_map/while/body/eval_jaxpr/all_gather | solution.py:46
  206.2 6.2 collective-permute-start
  212.4 30.3 %all-gather.3.cloned.1.call-start = ((), (), s32[]{:S(2)}) async-start(), calls=%async_computation.2 | async-start | bytes 1179648 | tf_op jit(solution)/shard_map/while/body/eval_jaxpr/all_gather | solution.py:46
  246.1 6.2 collective-permute-start
  252.3 30.6 %all-gather.3.cloned.1.call-start = ((), (), s32[]{:S(2)}) async-start(), calls=%async_computation.2 | async-start | bytes 1179648 | tf_op jit(solution)/shard_map/while/body/eval_jaxpr/all_gather | solution.py:46
  286.3 6.2 collective-permute-start
  292.6 181.8 %all-reduce.2.cloned.1.call-start = ((), (), s32[]{:S(2)}) async-start(), calls=%async_computation.4 | async-start | bytes 524288 | tf_op jit(solution)/shard_map/while/body/eval_jaxpr/psum | solution.py:121
  295.6 179.8 %all-gather.5.cloned.1.call-start = ((), (), s32[]{:S(2)}) async-start(), calls=%async_computation.3 | async-start | bytes 1179648 | tf_op jit(solution)/shard_map/while/body/eval_jaxpr/all_gather | solution.py:95
  475.4 4.5 copy-start.1
  478.5 6.8 collective-permute-start.1
  485.3 178.3 %all-reduce.2.cloned.1.call-start = ((), (), s32[]{:S(2)}) async-start(), calls=%async_computation.4 | async-start | bytes 524288 | tf_op jit(solution)/shard_map/while/body/eval_jaxpr/psum | solution.py:121
  488.3 176.3 %all-gather.5.cloned.1.call-start = ((), (), s32[]{:S(2)}) async-start(), calls=%async_computation.3 | async-start | bytes 1179648 | tf_op jit(solution)/shard_map/while/body/eval_jaxpr/all_gather | solution.py:95
  664.6 4.5 copy-start.1
  667.7 6.8 collective-permute-start.1
  674.5 178.2 %all-reduce.2.cloned.1.call-start = ((), (), s32[]{:S(2)}) async-start(), calls=%async_computation.4 | async-start | bytes 524288 | tf_op jit(solution)/shard_map/while/body/eval_jaxpr/psum | solution.py:121
  677.5 176.3 %all-gather.5.cloned.1.call-start = ((), (), s32[]{:S(2)}) async-start(), calls=%async_computation.3 | async-start | bytes 1179648 | tf_op jit(solution)/shard_map/while/body/eval_jaxpr/all_gather | solution.py:95
  853.7 4.5 copy-start.1
  856.8 6.8 collective-permute-start.1
  863.6 178.3 %all-reduce.2.cloned.1.call-start = ((), (), s32[]{:S(2)}) async-start(), calls=%async_computation.4 | async-start | bytes 524288 | tf_op jit(solution)/shard_map/while/body/eval_jaxpr/psum | solution.py:121
  866.6 176.4 %all-gather.5.cloned.1.call-start = ((), (), s32[]{:S(2)}) async-start(), calls=%async_computation.3 | async-start | bytes 1179648 | tf_op jit(solution)/shard_map/while/body/eval_jaxpr/all_gather | solution.py:95
  1042.9 4.5 copy-start.1
  1046.1 6.8 collective-permute-start.1
  1052.9 178.4 %all-reduce.2.cloned.1.call-start = ((), (), s32[]{:S(2)}) async-start(), calls=%async_computation.4 | async-start | bytes 524288 | tf_op jit(solution)/shard_map/while/body/eval_jaxpr/psum | solution.py:121
  1055.8 176.5 %all-gather.5.cloned.1.call-start = ((), (), s32[]{:S(2)}) async-start(), calls=%async_computation.3 | async-start | bytes 1179648 | tf_op jit(solution)/shard_map/while/body/eval_jaxpr/all_gather | solution.py:95
  1232.3 4.5 copy-start.1
  1235.5 6.8 collective-permute-start.1
  1242.2 178.4 %all-reduce.2.cloned.1.call-start = ((), (), s32[]{:S(2)}) async-start(), calls=%async_computation.4 | async-start | bytes 524288 | tf_op jit(solution)/shard_map/while/body/eval_jaxpr/psum | solution.py:121
  1245.2 176.4 %all-gather.5.cloned.1.call-start = ((), (), s32[]{:S(2)}) async-start(), calls=%async_computation.3 | async-start | bytes 1179648 | tf_op jit(solution)/shard_map/while/body/eval_jaxpr/all_gather | solution.py:95
  1421.6 4.5 copy-start.1
  1424.7 6.8 collective-permute-start.1
  1431.5 178.0 %all-reduce.2.cloned.1.call-start = ((), (), s32[]{:S(2)}) async-start(), calls=%async_computation.4 | async-start | bytes 524288 | tf_op jit(solution)/shard_map/while/body/eval_jaxpr/psum | solution.py:121
  1434.5 176.1 %all-gather.5.cloned.1.call-start = ((), (), s32[]{:S(2)}) async-start(), calls=%async_computation.3 | async-start | bytes 1179648 | tf_op jit(solution)/shard_map/while/body/eval_jaxpr/all_gather | solution.py:95
  1610.6 4.5 copy-start.1
  1613.7 6.8 collective-permute-start.1
  1620.5 25.0 %copy-start.3 = (f32[1,256,256]{2,1,0:T(8,128)}, f32[1,256,256]{2,1,0:T(8,128)S(1)}, u32[]{:S(2)}) copy-start(f32[1,256,256]{2,1,0:T(8,128)S(1)} %get-tuple-element.655) | copy-start | bytes 786436
  1620.5 25.0 %reduce-scatter.2.cloned.1.call-start = ((), (), s32[]{:S(2)}) async-start(), calls=%async_computation.1 | async-start | bytes 1310720 | tf_op jit(solution)/shard_map/reduce_scatter | solution.py:134
  (2 other events, 2.1 us)
Sparse Core Ops, SparseCore 0:
  12.6 30.0 all-gather.2
  55.7 27.1 all-gather.2
  95.9 27.1 all-gather.2
  135.8 27.1 all-gather.2
  175.6 27.1 all-gather.2
  215.5 27.1 all-gather.2
  255.7 27.1 all-gather.2
  297.9 176.4 all-reduce.1
  490.6 172.9 all-reduce.1
  679.5 173.1 all-reduce.1
  868.9 172.9 all-reduce.1
  1057.8 173.4 all-reduce.1
  1247.5 173.0 all-reduce.1
  1436.5 173.0 all-reduce.1
  1624.1 21.3 reduce-scatter.1
Sparse Core Ops, SparseCore 1:
  298.7 27.1 all-gather.4
  491.3 23.5 all-gather.4
  680.5 23.5 all-gather.4
  870.0 23.5 all-gather.4
  1059.2 23.5 all-gather.4
  1248.6 23.5 all-gather.4
  1437.6 23.5 all-gather.4
where the time goes:
time: 1660 us; the launch traced here: 1650 us
  waiting for transfers between devices  1480 us (89%)
  other arithmetic  56.6 us (3%)
  matrix products  38.5 us (2%)
  starting transfers between devices  31.3 us (2%)
  local copies, waits for them, and re-layouts  29 us (2%)
    psum x7, waiting for transfers between devices, backward_tick(): weight_term = lax.psum(weight_term, ('dp', 'dom'))  1220 us
    all_gather x7, waiting for transfers between devices, layer_forward(): gathered = lax.all_gather(hidden_state, 'dom', axis=0, tiled=True)  204 us
    ppermute x14, waiting for transfers between devices, from_behind(): return lax.ppermute(block, axis, route)  33.6 us
  transfers between devices with their start and end apart: 36, of which 22 were waited for; matrix products, arithmetic and copies ran while one was open for 3% of the time, Pallas kernels for 0%

commit v1 on v0

v1 whole, which is shorter than its diff:
```python
import functools
import math

import jax
import jax.numpy as jnp
from jax import lax
from jax.experimental import pallas as pl
from jax.experimental.pallas import tpu as pltpu
from jax.sharding import PartitionSpec as P

ALPHA = 0.1
THETA = 0.5
BLK = 128
NZB = 5
GELU_C = math.sqrt(2.0 / math.pi)
GELU_B = 0.044715
HEAD_TILES = 7
BF16 = jnp.bfloat16
F32 = jnp.float32


def pack_kernel(tiles, initial, cotangent, cols, head, tail, cot, cols_vec, sems):
    span = lax.axis_index("phase")
    lane = lax.broadcasted_iota(jnp.int32, cols_vec.shape, 1)
    vec = jnp.zeros(cols_vec.shape, F32)
    for b in range(2):
        for k in range(NZB):
            vec = jnp.where(lane == b * NZB + k, cols[span, b, k].astype(F32), vec)
    cols_vec[...] = vec.astype(BF16)
    rest = 2 * NZB - HEAD_TILES
    base = rest * BLK
    copies = [
        (tiles.at[span, pl.ds(0, HEAD_TILES)], head),
        (initial.at[span, :, pl.ds(0, BLK)], tail.at[pl.ds(base, 256)]),
        (initial.at[span, :, pl.ds(BLK, BLK)], tail.at[pl.ds(base + 256, 256)]),
        (cols_vec, tail.at[pl.ds(base + 512, 16)]),
        (cotangent.at[span], cot),
    ]
    for t in range(rest):
        copies.append((tiles.at[span, HEAD_TILES + t], tail.at[pl.ds(t * BLK, BLK)]))
    started = [pltpu.make_async_copy(a, b, sems.at[n]) for n, (a, b) in enumerate(copies)]
    for c in started:
        c.start()
    for c in started:
        c.wait()


def pack(tiles, initial, cotangent, cols):
    rest = 2 * NZB - HEAD_TILES
    any_spec = pl.BlockSpec(memory_space=pl.ANY)
    return pl.pallas_call(
        pack_kernel,
        in_specs=[any_spec, any_spec, any_spec, pl.BlockSpec(memory_space=pltpu.SMEM)],
        out_specs=[any_spec] * 3,
        out_shape=[
            jax.ShapeDtypeStruct((HEAD_TILES, BLK, BLK), BF16),
            jax.ShapeDtypeStruct((rest * BLK + 512 + 16, BLK), BF16),
            jax.ShapeDtypeStruct((256, 256), BF16),
        ],
        scratch_shapes=[pltpu.VMEM((16, BLK), BF16), pltpu.SemaphoreType.DMA((5 + rest,))],
        name="pack",
    )(tiles, initial, cotangent, cols)


def dot(a, b, dims):
    return lax.dot_general(a, b, (dims, ((), ())), preferred_element_type=F32)


def layers_kernel(scale, betas, *refs):
    heads, tails, cots, weights = refs[0:8], refs[8:16], refs[16:24], refs[24:28]
    grad_initial, grad_weights = refs[28:30]
    tiles, start, cot, weight, cols_bf, cols_int, cols, h_a, h_b, mixes, slopes, dpre, dw, sems = refs[30:]
    dom = lax.axis_index("dom")
    phase = lax.axis_index("phase")
    x, core = dom // 2, dom % 2
    rest = 2 * NZB - HEAD_TILES
    base = rest * BLK
    layers = weights_n = 4
    slots = [((x - n // 2 + 4) % 4) * 2 + (core if n % 2 == 0 else 1 - core) for n in range(8)]
    copies = []
    for n in range(8):
        s = slots[n]
        copies.append((tails[n].at[pl.ds(base + 512, 16)], cols_bf.at[pl.ds(s * 16, 16)]))
    for n in range(8):
        s = slots[n]
        copies.append((heads[n], tiles.at[pl.ds(s * 10, HEAD_TILES)]))
        for t in range(rest):
            copies.append((tails[n].at[pl.ds(t * BLK, BLK)], tiles.at[s * 10 + HEAD_TILES + t]))
        rows = pl.ds(pl.multiple_of(s * 256, 256), 256)
        copies.append((tails[n].at[pl.ds(base, 256)], start.at[rows, pl.ds(0, BLK)]))
        copies.append((tails[n].at[pl.ds(base + 256, 256)], start.at[rows, pl.ds(BLK, BLK)]))
        copies.append((cots[n], cot.at[rows]))
    for n in range(weights_n):
        copies.append((weights[n].at[0], weight.at[(phase - n + 4) % 4]))
    started = [pltpu.make_async_copy(a, b, sems.at[n]) for n, (a, b) in enumerate(copies)]
    for c in started:
        c.start()
    for c in started[:8]:
        c.wait()
    cols_int[...] = cols_bf[...].astype(F32).astype(jnp.int32)
    last = pltpu.make_async_copy(cols_int, cols, sems.at[len(copies)])
    last.start()
    last.wait()
    for c in started[8:]:
        c.wait()

    def aggregate(source, i):
        part, b = i // 2, i % 2
        blocks = []
        for k in range(NZB):
            j = cols[part * 16, b * NZB + k]
            blocks.append(source[pl.ds(pl.multiple_of(j * BLK, BLK), BLK), :])
        t = [tiles[i * NZB + k] for k in range(NZB)]
        return dot(jnp.concatenate(t, axis=1), jnp.concatenate(blocks, axis=0), ((1,), (0,)))

    nodes = start.shape[0]
    buffers = (h_a, h_b)
    source = start
    for l in range(layers):
        target = buffers[l % 2]
        beta = betas[l]

        def forward(i, _, source=source, target=target, beta=beta, l=l):
            rows = pl.ds(pl.multiple_of(i * BLK, BLK), BLK)
            agg = aggregate(source, i)
            mix = ((1.0 - ALPHA) * agg + ALPHA * start[rows, :].astype(F32)).astype(BF16)
            mixes[l, rows, :] = mix
            pre = (1.0 - beta) * mix.astype(F32) + beta * dot(mix, weight[l], ((1,), (0,)))
            square = pre * pre
            t = jnp.tanh(pre * (GELU_C + (GELU_C * GELU_B) * square))
            half = 0.5 + 0.5 * t
            hidden = pre * half
            if l < layers - 1:
                target[rows, :] = hidden.astype(BF16)
            slopes[l, rows, :] = half + hidden * (1.0 - half) * (
                2.0 * GELU_C + (6.0 * GELU_C * GELU_B) * square
            )
            return 0

        lax.fori_loop(0, nodes // BLK, forward, 0)
        source = target

    own = pl.ds(pl.multiple_of(dom * 256, 256), 256)
    source = None
    for l in reversed(range(layers)):
        target = buffers[l % 2]
        beta = betas[l]

        def backward(i, _, source=source, target=target, beta=beta, l=l):
            rows = pl.ds(pl.multiple_of(i * BLK, BLK), BLK)
            if source is None:
                back = cot[rows, :]
            else:
                back = ((1.0 - ALPHA) * aggregate(source, i)).astype(BF16)
            grad = (slopes[l, rows, :] * back.astype(F32)).astype(BF16)
            dpre[rows, :] = grad
            dmix = (1.0 - beta) * grad.astype(F32) + beta * dot(grad, weight[l], ((1,), (1,)))
            target[rows, :] = dmix.astype(BF16)
            return 0

        lax.fori_loop(0, nodes // BLK, backward, 0)
        term = ALPHA * target[own, :].astype(F32)
        grad_initial[0] = term if l == layers - 1 else grad_initial[0] + term
        dw[...] = (beta * scale) * dot(mixes[l], dpre[...], ((0,), (0,)))
        grad_weights[l] = dw[pl.ds(pl.multiple_of(dom * 32, 32), 32), :]
        source = target
    for b in range(2):
        last_back = ((1.0 - ALPHA) * aggregate(source, dom * 2 + b)).astype(BF16)
        rows = pl.ds(b * BLK, BLK)
        grad_initial[0, rows, :] = grad_initial[0, rows, :] + last_back.astype(F32)


def run_layers(scale, betas, heads, tails, cots, weights):
    any_spec = pl.BlockSpec(memory_space=pl.ANY)
    vmem = pl.BlockSpec(memory_space=pltpu.VMEM)
    nodes, width = 2048, 256
    return pl.pallas_call(
        functools.partial(layers_kernel, scale, betas),
        in_specs=[any_spec] * 28,
        out_specs=[vmem, vmem],
        out_shape=[
            jax.ShapeDtypeStruct((1, 256, width), F32),
            jax.ShapeDtypeStruct((4, 32, width), F32),
        ],
        scratch_shapes=[
            pltpu.VMEM((80, BLK, BLK), BF16),
            pltpu.VMEM((nodes, width), BF16),
            pltpu.VMEM((nodes, width), BF16),
            pltpu.VMEM((4, width, width), BF16),
            pltpu.VMEM((8 * 16, BLK), BF16),
            pltpu.VMEM((8 * 16, BLK), jnp.int32),
            pltpu.SMEM((8 * 16, BLK), jnp.int32),
            pltpu.VMEM((nodes, width), BF16),
            pltpu.VMEM((nodes, width), BF16),
            pltpu.VMEM((4, nodes, width), BF16),
            pltpu.VMEM((4, nodes, width), F32),
            pltpu.VMEM((nodes, width), BF16),
            pltpu.VMEM((width, width), F32),
            pltpu.SemaphoreType.DMA((8 * 8 + 8,)),
        ],
        compiler_params=pltpu.CompilerParams(vmem_limit_bytes=48 * 1024 * 1024),
        cost_estimate=pl.CostEstimate(flops=9_000_000_000, bytes_accessed=6_000_000, transcendentals=0),
        name="layers",
    )(*heads, *tails, *cots, *weights)


def ring(v, step):
    return lax.ppermute(v, "dom", [(i, (i + 2 * step) % 8) for i in range(8)])


def other_core(v):
    return lax.ppermute(v, "dom", [(i, i ^ 1) for i in range(8)])


def gather(v, way):
    from_left, from_right = ring(v, 1), ring(v, -1)
    far = ring(from_left, 1) if way > 0 else ring(from_right, -1)
    pieces = []
    for piece in (v, from_left, far, from_right):
        pieces += [piece, other_core(piece)]
    return pieces


def local(initial, block_cols, block_tiles, layer_weights, cotangent):
    layers = lax.axis_size("phase")
    nodes_all = 4 * 2048 * lax.axis_size("dp")
    scale = 1.0 / math.sqrt(nodes_all)
    betas = [math.log(THETA / (l + 1) + 1.0) for l in range(layers)]
    spans, rows = block_tiles.shape[:2]
    tiles = block_tiles.reshape(spans, rows * NZB, BLK, BLK)
    head, tail, cot = pack(tiles, initial, cotangent, block_cols)
    heads = gather(head, 1)
    tails = gather(tail, -1)
    weights = [layer_weights] + [
        lax.ppermute(layer_weights, "phase", [(i, (i + n) % 4) for i in range(4)]) for n in (1, 2, 3)
    ]
    cots = gather(cot, 1)
    grad_initial, parts = run_layers(scale, betas, heads, tails, cots, weights)
    parts = lax.all_to_all(parts, "phase", 0, 0, tiled=True)
    mine = jnp.sum(parts, axis=0)
    mine = jnp.broadcast_to(mine[None], (8,) + mine.shape)
    mine = jnp.sum(lax.all_to_all(mine, "dp", 0, 0, tiled=True), axis=0)
    mine = jnp.broadcast_to(mine[None], (8,) + mine.shape)
    mine = lax.all_to_all(mine, "dom", 0, 0, tiled=True)
    return grad_initial, mine.reshape(1, 256, 256)


def solution(mesh):
    placed = (
        P("dp", "dom", None),
        P("dp", "dom", None),
        P("dp", "dom", None, None, None),
        P("phase", None, None),
        P("dp", "dom", None),
    )
    return jax.shard_map(
        local,
        mesh=mesh,
        in_specs=placed,
        out_specs=(P(("dp", "phase"), "dom", None), P("phase", None, None)),
        check_vma=False,
    )
```

time: 1660 us -> 161 us (0.10)
  waiting for transfers between devices: 1480 us -> 10.1 us
  Pallas kernels: 0 us -> 78.7 us
  other arithmetic: 56.6 us -> 0.03 us
  matrix products: 38.5 us -> 0 us
  blocking collectives: 0 us -> 37.9 us
  local copies, waits for them, and re-layouts: 29 us -> 3.53 us
    psum x7 -> x0, waiting for transfers between devices: 1220 us -> none  [backward_tick(): weight_term = lax.psum(weight_term, ('dp', 'dom'))]
    all_gather x14 -> x0, waiting for transfers between devices: 205 us -> none  [the longest x7 204 us: layer_forward(): gathered = lax.all_gather(hidden_state, 'dom', axis=0, tiled=True)]
    pallas_call x0 -> x2, Pallas kernels: none -> 78.7 us  [the longest x1 58.9 us: run_layers(): pl.pallas_call(functools.partial(layers_kernel, scale, betas), in_specs=[...]
    dot_general x35 -> x0, matrix products: 38.5 us -> none  [the longest x14 17.5 us: apply_tiles(): jnp.einsum('ikrc,ikch->irh', tiles_m, picked, preferred_element_type=jnp....]
    all_to_all x0 -> x3, blocking collectives: none -> 37.9 us  [the longest x1 17.2 us: local(): mine = jnp.sum(lax.all_to_all(mine, 'dp', 0, 0, tiled=True), axis=0)]
    gather x14 -> x0, local copies, waits for them, and re-layouts: 25.6 us -> none  [pick_blocks(): return blocks[cols_m]]
    reduce_scatter x1 -> x0, waiting for transfers between devices: 24 us -> none  [local(): lax.psum_scatter(start_grads, 'phase', scatter_dimension=0, tiled=True)]
    ppermute x14 -> x24, waiting for transfers between devices: 33.6 us -> 10.1 us  [the longest x9 7.97 us: ring(): return lax.ppermute(v, 'dom', [(i, (i + 2 * step) % 8) for i in range(8)])]
  transfers between devices with their start and end apart: 36 -> 24, of which waited for: 22 -> 7; matrix products, arithmetic and copies ran while one was open for 3% -> 0% of each run, Pallas kernels for 0% -> 12%
where the time goes in v1:
time: 161 us; the launch traced here: 160 us
  Pallas kernels  78.7 us (49%)
  blocking collectives  37.9 us (24%)
  starting transfers between devices  29.5 us (18%)
  waiting for transfers between devices  10.1 us (6%)
  local copies, waits for them, and re-layouts  3.53 us (2%)
    pallas_call x1, Pallas kernels, run_layers(): pl.pallas_call(functools.partial(layers_kernel, scale, betas), in_specs=[...  58.9 us
    pallas_call x1, Pallas kernels, pack(): pl.pallas_call(pack_kernel, in_specs=[any_spec, any_spec, any_spec, pl.Bl...  19.8 us
    all_to_all x1, blocking collectives, local(): mine = jnp.sum(lax.all_to_all(mine, 'dp', 0, 0, tiled=True), axis=0)  17.2 us
    ppermute x12, starting transfers between devices, other_core(): return lax.ppermute(v, 'dom', [(i, i ^ 1) for i in range(8)])  12.7 us
    all_to_all x1, blocking collectives, local(): mine = lax.all_to_all(mine, 'dom', 0, 0, tiled=True)  12.5 us
    ppermute x9, starting transfers between devices, ring(): return lax.ppermute(v, 'dom', [(i, (i + 2 * step) % 8) for i in range(8)])  10.3 us
    all_to_all x1, blocking collectives, local(): parts = lax.all_to_all(parts, 'phase', 0, 0, tiled=True)  8.17 us
    ppermute x9, waiting for transfers between devices, ring(): return lax.ppermute(v, 'dom', [(i, (i + 2 * step) % 8) for i in range(8)])  7.97 us
  transfers between devices with their start and end apart: 24, of which 7 were waited for; matrix products, arithmetic and copies ran while one was open for 0% of the time, Pallas kernels for 12%

profile of v1, /device:TPU:1, one launch (start us, length us, event | category | flops | bytes accessed | tf_op | source)
XLA Modules:
  0.0 160.5 jit_solution(12921270346406823154)
XLA Ops:
  0.6 3.8 %collective-permute-start.22 = (bf16[1,256,256]{2,1,0:T(8,128)(2,1)}, bf16[1,256,256]{2,1,0:T(8,128)(2,1)S(1)}, u32[]{:S(2)}, u32[]{:S(2)}) collective-permute-start(bf16[1,256,256]{2,1,0:T(8,128)(2,1)} %refs_24_.1), channel_id=1, source_target_pairs={{0,16},{8,24},{16,0},{24,8},{1,17},{9,25},{17,1},{25,9},{2,18},{10... | collective-permute-start | bytes 393224 | tf_op jit(solution)/shard_map/ppermute | solution.py:235
  4.5 0.4 collective-permute-start.21
  4.9 19.8 %pack.1 = (bf16[7,128,128]{2,1,0:T(8,128)(2,1)}, bf16[912,128]{1,0:T(8,128)(2,1)}, bf16[256,256]{1,0:T(8,128)(2,1)}) custom-call(bf16[4,10,128,128]{3,2,1,0:T(8,128)(2,1)} %bitcast.2, bf16[4,256,256]{2,1,0:T(8,128)(2,1)} %initial.1, bf16[4,256,256]{2,1,0:T(8,128)(2,1)} %cotangent.1, s32[4,2,5]{2,1,0:T(2,128)} %cols.1), custom_call_target="tpu_custom_call" | custom-call | tf_op jit(solution)/shard_map/pack/pallas_call | solution.py:51
  24.7 2.6 %collective-permute-start.5 = (bf16[7,128,128]{2,1,0:T(8,128)(2,1)}, bf16[7,128,128]{2,1,0:T(8,128)(2,1)S(1)}, u32[]{:S(2)}, u32[]{:S(2)}) collective-permute-start(bf16[7,128,128]{2,1,0:T(8,128)(2,1)} %get-tuple-element.7.refs_0_), channel_id=1, source_target_pairs={{0,6},{1,7},{2,0},{3,1},{4,2},{5,3},{6,4},{7,5},{8,14},{9,15},{10,... | collective-permute-start | bytes 688136 | tf_op jit(solution)/shard_map/ppermute | solution.py:208
  27.2 2.3 %collective-permute-start.23 = (bf16[1,256,256]{2,1,0:T(8,128)(2,1)S(1)}, bf16[1,256,256]{2,1,0:T(8,128)(2,1)S(1)}, u32[]{:S(2)}, u32[]{:S(2)}) collective-permute-start(bf16[1,256,256]{2,1,0:T(8,128)(2,1)S(1)} %copy-done.2), channel_id=1, source_target_pairs={{0,24},{8,0},{16,8},{24,16},{1,25},{9,1},{17,9},{25,17},{2,26},{10... | collective-permute-start | bytes 393224 | tf_op jit(solution)/shard_map/ppermute | solution.py:235
  29.5 0.5 collective-permute-start.19
  30.0 0.0 collective-permute-done.22.refs_26_
  30.0 0.9 collective-permute-start.15
  31.0 0.0 collective-permute-done.21.refs_25_
  31.0 2.4 %collective-permute-start.14 = (bf16[256,256]{1,0:T(8,128)(2,1)}, bf16[256,256]{1,0:T(8,128)(2,1)S(1)}, u32[]{:S(2)}, u32[]{:S(2)}) collective-permute-start(bf16[256,256]{1,0:T(8,128)(2,1)} %get-tuple-element.9.refs_16_), channel_id=1, source_target_pairs={{0,1},{1,0},{2,3},{3,2},{4,5},{5,4},{6,7},{7,6},{8,9},{9,8},{10,11... | collective-permute-start | bytes 393224 | tf_op jit(solution)/shard_map/ppermute | solution.py:212
  33.3 0.0 collective-permute-done.23.refs_27_
  33.3 0.0 collective-permute-start.1
  33.3 0.7 collective-permute-done.19.refs_22_
  34.0 2.5 %collective-permute-start = (bf16[7,128,128]{2,1,0:T(8,128)(2,1)}, bf16[7,128,128]{2,1,0:T(8,128)(2,1)S(1)}, u32[]{:S(2)}, u32[]{:S(2)}) collective-permute-start(bf16[7,128,128]{2,1,0:T(8,128)(2,1)} %get-tuple-element.7.refs_0_), channel_id=1, source_target_pairs={{0,1},{1,0},{2,3},{3,2},{4,5},{5,4},{6,7},{7,6},{8,9},{9,8},{10,11... | collective-permute-start | bytes 688136 | tf_op jit(solution)/shard_map/ppermute | solution.py:212
  36.5 0.0 collective-permute-done.15.refs_18_
  36.5 3.0 %collective-permute-start.10 = (bf16[912,128]{1,0:T(8,128)(2,1)}, bf16[912,128]{1,0:T(8,128)(2,1)S(1)}, u32[]{:S(2)}, u32[]{:S(2)}) collective-permute-start(bf16[912,128]{1,0:T(8,128)(2,1)} %get-tuple-element.8.refs_8_), channel_id=1, source_target_pairs={{0,6},{1,7},{2,0},{3,1},{4,2},{5,3},{6,4},{7,5},{8,14},{9,15},{10,... | collective-permute-start | bytes 700424 | tf_op jit(solution)/shard_map/ppermute | solution.py:208
  39.5 0.0 collective-permute-done.14.refs_17_
  39.5 0.0 collective-permute-start.8
  39.5 1.8 %collective-permute-start.7 = (bf16[912,128]{1,0:T(8,128)(2,1)}, bf16[912,128]{1,0:T(8,128)(2,1)S(1)}, u32[]{:S(2)}, u32[]{:S(2)}) collective-permute-start(bf16[912,128]{1,0:T(8,128)(2,1)} %get-tuple-element.8.refs_8_), channel_id=1, source_target_pairs={{0,1},{1,0},{2,3},{3,2},{4,5},{5,4},{6,7},{7,6},{8,9},{9,8},{10,11... | collective-permute-start | bytes 700424 | tf_op jit(solution)/shard_map/ppermute | solution.py:212
  41.2 1.1 collective-permute-done.1.refs_2_
  42.3 1.1 collective-permute-start.20
  43.4 1.5 collective-permute-done.10.refs_14_
  44.9 3.3 %collective-permute-start.11 = (bf16[912,128]{1,0:T(8,128)(2,1)S(1)}, bf16[912,128]{1,0:T(8,128)(2,1)S(1)}, u32[]{:S(2)}, u32[]{:S(2)}) collective-permute-start(bf16[912,128]{1,0:T(8,128)(2,1)S(1)} %collective-permute-done.10.refs_14_), channel_id=1, source_target_pairs={{0,6},{1,7},{2,0},{3,1},{4,2},{5,3},{6,4},{7,5},{8,14},{9,15},{10,... | collective-permute-start | bytes 700424 | tf_op jit(solution)/shard_map/ppermute | solution.py:208
  48.2 0.0 collective-permute-done.8.refs_10_
  48.2 1.5 collective-permute-start.6
  49.7 0.3 collective-permute-start.16
  50.0 0.7 collective-permute-done.17.refs_20_
  50.7 1.1 collective-permute-start.18
  51.8 0.0 collective-permute-start.13
  51.8 1.0 collective-permute-done.18.refs_21_
  52.8 0.4 collective-permute-start.9
  53.2 1.0 collective-permute-start.12
  54.1 0.0 collective-permute-done.6.refs_7_
  54.1 0.0 collective-permute-start.2
  54.1 4.0 %collective-permute-done.3.refs_4_ = bf16[7,128,128]{2,1,0:T(8,128)(2,1)S(1)} collective-permute-done((bf16[7,128,128]{2,1,0:T(8,128)(2,1)S(1)}, bf16[7,128,128]{2,1,0:T(8,128)(2,1)S(1)}, u32[]{:S(2)}, u32[]{:S(2)}) %collective-permute-start.3) | collective-permute-done | bytes 229408 | tf_op jit(solution)/shard_map/ppermute | solution.py:208
  58.2 0.8 collective-permute-start.4
  58.9 0.0 collective-permute-done.2.refs_3_
  58.9 0.0 collective-permute-done.13.refs_15_
  58.9 0.0 collective-permute-done.9.refs_11_
  58.9 1.1 collective-permute-done.4.refs_5_
  60.1 0.9 copy-done
  61.0 0.9 copy-done.1
  61.9 0.9 copy-done.3
  62.8 58.9 %layers.1 = (f32[1,256,256]{2,1,0:T(8,128)}, f32[4,32,256]{2,1,0:T(8,128)S(1)}) custom-call(bf16[7,128,128]{2,1,0:T(8,128)(2,1)S(1)} %copy-done.1, bf16[7,128,128]{2,1,0:T(8,128)(2,1)S(1)} %collective-permute-done.refs_1_, bf16[7,128,128]{2,1,0:T(8,128)(2,1)S(1)} %collective-permute-done.1.refs_2_, bf16[7,128,128]{2,1,0:T(8,128)(2,1)S(1)} %collective-permute-done.2.refs_3_, ...), custom_call_target="tpu_custom_call" | custom-call | flops 8999999488 | bytes 6000000 | tf_op jit(solution)/shard_map/layers/pallas_call | solution.py:177
  121.8 8.2 %all_to_all.15 = f32[4,32,256]{2,1,0:T(8,128)S(1)} all-to-all(f32[4,32,256]{2,1,0:T(8,128)S(1)} %get-tuple-element.11), channel_id=1, replica_groups=mesh['dp'=8,'phase'=4,'dom'=8] {'phase'}, dimensions={0} | all-to-all | bytes 262144 | tf_op jit(solution)/shard_map/all_to_all | solution.py:239
  130.0 17.2 %all_to_all.16 = f32[8,32,256]{2,1,0:T(8,128)S(1)} all-to-all(f32[8,32,256]{2,1,0:T(8,128)S(1)} %broadcast_in_dim.4), channel_id=1, replica_groups=mesh['dp'=8,'phase'=4,'dom'=8] {'dp'}, dimensions={0} | all-to-all | bytes 524288 | tf_op jit(solution)/shard_map/all_to_all | solution.py:242
  147.2 12.5 %all_to_all.17 = f32[8,32,256]{2,1,0:T(8,128)S(1)} all-to-all(f32[8,32,256]{2,1,0:T(8,128)S(1)} %broadcast_in_dim.5), channel_id=1, replica_groups=mesh['dp'=8,'phase'=4,'dom'=8] {'dom'}, dimensions={0} | all-to-all | bytes 524288 | tf_op jit(solution)/shard_map/all_to_all | solution.py:244
  159.8 0.7 copy.8
  (18 shorter events, 0.1 us)
Async XLA Ops:
  0.6 26.6 %copy-start.2 = (bf16[1,256,256]{2,1,0:T(8,128)(2,1)S(1)}, bf16[1,256,256]{2,1,0:T(8,128)(2,1)}, u32[]{:S(2)}) copy-start(bf16[1,256,256]{2,1,0:T(8,128)(2,1)} %refs_24_.1) | copy-start | bytes 393220
  0.6 29.4 %collective-permute-start.22 = (bf16[1,256,256]{2,1,0:T(8,128)(2,1)}, bf16[1,256,256]{2,1,0:T(8,128)(2,1)S(1)}, u32[]{:S(2)}, u32[]{:S(2)}) collective-permute-start(bf16[1,256,256]{2,1,0:T(8,128)(2,1)} %refs_24_.1), channel_id=1, source_target_pairs={{0,16},{8,24},{16,0},{24,8},{1,17},{9,25},{17,1},{25,9},{2,18},{10... | collective-permute-start | bytes 393224 | tf_op jit(solution)/shard_map/ppermute | solution.py:235
  4.5 26.5 %collective-permute-start.21 = (bf16[1,256,256]{2,1,0:T(8,128)(2,1)}, bf16[1,256,256]{2,1,0:T(8,128)(2,1)S(1)}, u32[]{:S(2)}, u32[]{:S(2)}) collective-permute-start(bf16[1,256,256]{2,1,0:T(8,128)(2,1)} %refs_24_.1), channel_id=1, source_target_pairs={{0,8},{8,16},{16,24},{24,0},{1,9},{9,17},{17,25},{25,1},{2,10},{10... | collective-permute-start | bytes 393224 | tf_op jit(solution)/shard_map/ppermute | solution.py:235
  24.7 14.8 %collective-permute-start.5 = (bf16[7,128,128]{2,1,0:T(8,128)(2,1)}, bf16[7,128,128]{2,1,0:T(8,128)(2,1)S(1)}, u32[]{:S(2)}, u32[]{:S(2)}) collective-permute-start(bf16[7,128,128]{2,1,0:T(8,128)(2,1)} %get-tuple-element.7.refs_0_), channel_id=1, source_target_pairs={{0,6},{1,7},{2,0},{3,1},{4,2},{5,3},{6,4},{7,5},{8,14},{9,15},{10,... | collective-permute-start | bytes 688136 | tf_op jit(solution)/shard_map/ppermute | solution.py:208
  27.2 6.1 %collective-permute-start.23 = (bf16[1,256,256]{2,1,0:T(8,128)(2,1)S(1)}, bf16[1,256,256]{2,1,0:T(8,128)(2,1)S(1)}, u32[]{:S(2)}, u32[]{:S(2)}) collective-permute-start(bf16[1,256,256]{2,1,0:T(8,128)(2,1)S(1)} %copy-done.2), channel_id=1, source_target_pairs={{0,24},{8,0},{16,8},{24,16},{1,25},{9,1},{17,9},{25,17},{2,26},{10... | collective-permute-start | bytes 393224 | tf_op jit(solution)/shard_map/ppermute | solution.py:235
  29.5 4.5 %collective-permute-start.19 = (bf16[256,256]{1,0:T(8,128)(2,1)}, bf16[256,256]{1,0:T(8,128)(2,1)S(1)}, u32[]{:S(2)}, u32[]{:S(2)}) collective-permute-start(bf16[256,256]{1,0:T(8,128)(2,1)} %get-tuple-element.9.refs_16_), channel_id=1, source_target_pairs={{0,6},{1,7},{2,0},{3,1},{4,2},{5,3},{6,4},{7,5},{8,14},{9,15},{10,... | collective-permute-start | bytes 393224 | tf_op jit(solution)/shard_map/ppermute | solution.py:208
  30.0 6.4 %collective-permute-start.15 = (bf16[256,256]{1,0:T(8,128)(2,1)}, bf16[256,256]{1,0:T(8,128)(2,1)S(1)}, u32[]{:S(2)}, u32[]{:S(2)}) collective-permute-start(bf16[256,256]{1,0:T(8,128)(2,1)} %get-tuple-element.9.refs_16_), channel_id=1, source_target_pairs={{0,2},{1,3},{2,4},{3,5},{4,6},{5,7},{6,0},{7,1},{8,10},{9,11},{10,... | collective-permute-start | bytes 393224 | tf_op jit(solution)/shard_map/ppermute | solution.py:208
  31.0 8.5 %collective-permute-start.14 = (bf16[256,256]{1,0:T(8,128)(2,1)}, bf16[256,256]{1,0:T(8,128)(2,1)S(1)}, u32[]{:S(2)}, u32[]{:S(2)}) collective-permute-start(bf16[256,256]{1,0:T(8,128)(2,1)} %get-tuple-element.9.refs_16_), channel_id=1, source_target_pairs={{0,1},{1,0},{2,3},{3,2},{4,5},{5,4},{6,7},{7,6},{8,9},{9,8},{10,11... | collective-permute-start | bytes 393224 | tf_op jit(solution)/shard_map/ppermute | solution.py:212
  33.3 9.0 %collective-permute-start.1 = (bf16[7,128,128]{2,1,0:T(8,128)(2,1)}, bf16[7,128,128]{2,1,0:T(8,128)(2,1)S(1)}, u32[]{:S(2)}, u32[]{:S(2)}) collective-permute-start(bf16[7,128,128]{2,1,0:T(8,128)(2,1)} %get-tuple-element.7.refs_0_), channel_id=1, source_target_pairs={{0,2},{1,3},{2,4},{3,5},{4,6},{5,7},{6,0},{7,1},{8,10},{9,11},{10,... | collective-permute-start | bytes 688136 | tf_op jit(solution)/shard_map/ppermute | solution.py:208
  34.0 9.4 %collective-permute-start = (bf16[7,128,128]{2,1,0:T(8,128)(2,1)}, bf16[7,128,128]{2,1,0:T(8,128)(2,1)S(1)}, u32[]{:S(2)}, u32[]{:S(2)}) collective-permute-start(bf16[7,128,128]{2,1,0:T(8,128)(2,1)} %get-tuple-element.7.refs_0_), channel_id=1, source_target_pairs={{0,1},{1,0},{2,3},{3,2},{4,5},{5,4},{6,7},{7,6},{8,9},{9,8},{10,11... | collective-permute-start | bytes 688136 | tf_op jit(solution)/shard_map/ppermute | solution.py:212
  36.5 8.4 %collective-permute-start.10 = (bf16[912,128]{1,0:T(8,128)(2,1)}, bf16[912,128]{1,0:T(8,128)(2,1)S(1)}, u32[]{:S(2)}, u32[]{:S(2)}) collective-permute-start(bf16[912,128]{1,0:T(8,128)(2,1)} %get-tuple-element.8.refs_8_), channel_id=1, source_target_pairs={{0,6},{1,7},{2,0},{3,1},{4,2},{5,3},{6,4},{7,5},{8,14},{9,15},{10,... | collective-permute-start | bytes 700424 | tf_op jit(solution)/shard_map/ppermute | solution.py:208
  39.5 8.7 %collective-permute-start.8 = (bf16[912,128]{1,0:T(8,128)(2,1)}, bf16[912,128]{1,0:T(8,128)(2,1)S(1)}, u32[]{:S(2)}, u32[]{:S(2)}) collective-permute-start(bf16[912,128]{1,0:T(8,128)(2,1)} %get-tuple-element.8.refs_8_), channel_id=1, source_target_pairs={{0,2},{1,3},{2,4},{3,5},{4,6},{5,7},{6,0},{7,1},{8,10},{9,11},{10,... | collective-permute-start | bytes 700424 | tf_op jit(solution)/shard_map/ppermute | solution.py:208
  39.5 10.2 %collective-permute-start.7 = (bf16[912,128]{1,0:T(8,128)(2,1)}, bf16[912,128]{1,0:T(8,128)(2,1)S(1)}, u32[]{:S(2)}, u32[]{:S(2)}) collective-permute-start(bf16[912,128]{1,0:T(8,128)(2,1)} %get-tuple-element.8.refs_8_), channel_id=1, source_target_pairs={{0,1},{1,0},{2,3},{3,2},{4,5},{5,4},{6,7},{7,6},{8,9},{9,8},{10,11... | collective-permute-start | bytes 700424 | tf_op jit(solution)/shard_map/ppermute | solution.py:212
  42.3 7.4 %collective-permute-start.20 = (bf16[256,256]{1,0:T(8,128)(2,1)S(1)}, bf16[256,256]{1,0:T(8,128)(2,1)S(1)}, u32[]{:S(2)}, u32[]{:S(2)}) collective-permute-start(bf16[256,256]{1,0:T(8,128)(2,1)S(1)} %collective-permute-done.19.refs_22_), channel_id=1, source_target_pairs={{0,1},{1,0},{2,3},{3,2},{4,5},{5,4},{6,7},{7,6},{8,9},{9,8},{10,11... | collective-permute-start | bytes 393224 | tf_op jit(solution)/shard_map/ppermute | solution.py:212
  43.4 7.3 %collective-permute-start.17 = (bf16[256,256]{1,0:T(8,128)(2,1)S(1)}, bf16[256,256]{1,0:T(8,128)(2,1)S(1)}, u32[]{:S(2)}, u32[]{:S(2)}) collective-permute-start(bf16[256,256]{1,0:T(8,128)(2,1)S(1)} %collective-permute-done.15.refs_18_), channel_id=1, source_target_pairs={{0,2},{1,3},{2,4},{3,5},{4,6},{5,7},{6,0},{7,1},{8,10},{9,11},{10,... | collective-permute-start | bytes 393224 | tf_op jit(solution)/shard_map/ppermute | solution.py:208
  44.9 8.3 %collective-permute-start.11 = (bf16[912,128]{1,0:T(8,128)(2,1)S(1)}, bf16[912,128]{1,0:T(8,128)(2,1)S(1)}, u32[]{:S(2)}, u32[]{:S(2)}) collective-permute-start(bf16[912,128]{1,0:T(8,128)(2,1)S(1)} %collective-permute-done.10.refs_14_), channel_id=1, source_target_pairs={{0,6},{1,7},{2,0},{3,1},{4,2},{5,3},{6,4},{7,5},{8,14},{9,15},{10,... | collective-permute-start | bytes 700424 | tf_op jit(solution)/shard_map/ppermute | solution.py:208
  48.2 5.9 %collective-permute-start.6 = (bf16[7,128,128]{2,1,0:T(8,128)(2,1)S(1)}, bf16[7,128,128]{2,1,0:T(8,128)(2,1)S(1)}, u32[]{:S(2)}, u32[]{:S(2)}) collective-permute-start(bf16[7,128,128]{2,1,0:T(8,128)(2,1)S(1)} %collective-permute-done.5.refs_6_), channel_id=1, source_target_pairs={{0,1},{1,0},{2,3},{3,2},{4,5},{5,4},{6,7},{7,6},{8,9},{9,8},{10,11... | collective-permute-start | bytes 688136 | tf_op jit(solution)/shard_map/ppermute | solution.py:212
  49.7 8.4 %collective-permute-start.3 = (bf16[7,128,128]{2,1,0:T(8,128)(2,1)S(1)}, bf16[7,128,128]{2,1,0:T(8,128)(2,1)S(1)}, u32[]{:S(2)}, u32[]{:S(2)}) collective-permute-start(bf16[7,128,128]{2,1,0:T(8,128)(2,1)S(1)} %collective-permute-done.1.refs_2_), channel_id=1, source_target_pairs={{0,2},{1,3},{2,4},{3,5},{4,6},{5,7},{6,0},{7,1},{8,10},{9,11},{10,... | collective-permute-start | bytes 688136 | tf_op jit(solution)/shard_map/ppermute | solution.py:208
  49.7 2.1 %collective-permute-start.16 = (bf16[256,256]{1,0:T(8,128)(2,1)S(1)}, bf16[256,256]{1,0:T(8,128)(2,1)S(1)}, u32[]{:S(2)}, u32[]{:S(2)}) collective-permute-start(bf16[256,256]{1,0:T(8,128)(2,1)S(1)} %collective-permute-done.15.refs_18_), channel_id=1, source_target_pairs={{0,1},{1,0},{2,3},{3,2},{4,5},{5,4},{6,7},{7,6},{8,9},{9,8},{10,11... | collective-permute-start | bytes 393224 | tf_op jit(solution)/shard_map/ppermute | solution.py:212
  50.7 2.1 %collective-permute-start.18 = (bf16[256,256]{1,0:T(8,128)(2,1)S(1)}, bf16[256,256]{1,0:T(8,128)(2,1)S(1)}, u32[]{:S(2)}, u32[]{:S(2)}) collective-permute-start(bf16[256,256]{1,0:T(8,128)(2,1)S(1)} %collective-permute-done.17.refs_20_), channel_id=1, source_target_pairs={{0,1},{1,0},{2,3},{3,2},{4,5},{5,4},{6,7},{7,6},{8,9},{9,8},{10,11... | collective-permute-start | bytes 393224 | tf_op jit(solution)/shard_map/ppermute | solution.py:212
  51.8 7.1 %collective-permute-start.13 = (bf16[912,128]{1,0:T(8,128)(2,1)S(1)}, bf16[912,128]{1,0:T(8,128)(2,1)S(1)}, u32[]{:S(2)}, u32[]{:S(2)}) collective-permute-start(bf16[912,128]{1,0:T(8,128)(2,1)S(1)} %collective-permute-done.10.refs_14_), channel_id=1, source_target_pairs={{0,1},{1,0},{2,3},{3,2},{4,5},{5,4},{6,7},{7,6},{8,9},{9,8},{10,11... | collective-permute-start | bytes 700424 | tf_op jit(solution)/shard_map/ppermute | solution.py:212
  52.8 6.2 %collective-permute-start.9 = (bf16[912,128]{1,0:T(8,128)(2,1)S(1)}, bf16[912,128]{1,0:T(8,128)(2,1)S(1)}, u32[]{:S(2)}, u32[]{:S(2)}) collective-permute-start(bf16[912,128]{1,0:T(8,128)(2,1)S(1)} %collective-permute-done.8.refs_10_), channel_id=1, source_target_pairs={{0,1},{1,0},{2,3},{3,2},{4,5},{5,4},{6,7},{7,6},{8,9},{9,8},{10,11... | collective-permute-start | bytes 700424 | tf_op jit(solution)/shard_map/ppermute | solution.py:212
  53.2 6.9 %collective-permute-start.12 = (bf16[912,128]{1,0:T(8,128)(2,1)S(1)}, bf16[912,128]{1,0:T(8,128)(2,1)S(1)}, u32[]{:S(2)}, u32[]{:S(2)}) collective-permute-start(bf16[912,128]{1,0:T(8,128)(2,1)S(1)} %collective-permute-done.11.refs_12_), channel_id=1, source_target_pairs={{0,1},{1,0},{2,3},{3,2},{4,5},{5,4},{6,7},{7,6},{8,9},{9,8},{10,11... | collective-permute-start | bytes 700424 | tf_op jit(solution)/shard_map/ppermute | solution.py:212
  54.1 4.8 %collective-permute-start.2 = (bf16[7,128,128]{2,1,0:T(8,128)(2,1)S(1)}, bf16[7,128,128]{2,1,0:T(8,128)(2,1)S(1)}, u32[]{:S(2)}, u32[]{:S(2)}) collective-permute-start(bf16[7,128,128]{2,1,0:T(8,128)(2,1)S(1)} %collective-permute-done.1.refs_2_), channel_id=1, source_target_pairs={{0,1},{1,0},{2,3},{3,2},{4,5},{5,4},{6,7},{7,6},{8,9},{9,8},{10,11... | collective-permute-start | bytes 688136 | tf_op jit(solution)/shard_map/ppermute | solution.py:212
  58.2 1.9 %collective-permute-start.4 = (bf16[7,128,128]{2,1,0:T(8,128)(2,1)S(1)}, bf16[7,128,128]{2,1,0:T(8,128)(2,1)S(1)}, u32[]{:S(2)}, u32[]{:S(2)}) collective-permute-start(bf16[7,128,128]{2,1,0:T(8,128)(2,1)S(1)} %collective-permute-done.3.refs_4_), channel_id=1, source_target_pairs={{0,1},{1,0},{2,3},{3,2},{4,5},{5,4},{6,7},{7,6},{8,9},{9,8},{10,11... | collective-permute-start | bytes 688136 | tf_op jit(solution)/shard_map/ppermute | solution.py:212
  60.1 0.9 copy-start
  61.0 0.9 copy-start.1
  61.9 0.9 copy-start.3

commit v2 on v1

v2 whole, which is shorter than its diff:
```python
import functools
import math

import jax
import jax.numpy as jnp
from jax import lax
from jax.experimental import pallas as pl
from jax.experimental.pallas import tpu as pltpu
from jax.sharding import PartitionSpec as P

ALPHA = 0.1
THETA = 0.5
BLK = 128
NZB = 5
GELU_C = math.sqrt(2.0 / math.pi)
GELU_B = 0.044715
HEAD_TILES = 7
TAIL_START = (2 * NZB - HEAD_TILES) * BLK
TAIL_COLS = TAIL_START + 512
CHUNK = 4
BF16 = jnp.bfloat16
F32 = jnp.float32


def pack_kernel(tiles, initial, cotangent, cols, head, tail, cot, start, sems):
    span = lax.axis_index("phase")
    rest = 2 * NZB - HEAD_TILES
    copies = [
        (tiles.at[span, pl.ds(0, HEAD_TILES)], head),
        (initial.at[span], start),
        (cotangent.at[span], cot),
    ]
    for t in range(rest):
        copies.append((tiles.at[span, HEAD_TILES + t], tail.at[pl.ds(t * BLK, BLK)]))
    started = [pltpu.make_async_copy(a, b, sems.at[n]) for n, (a, b) in enumerate(copies)]
    for c in started:
        c.start()
    lane = lax.broadcasted_iota(jnp.int32, (16, BLK), 1)
    vec = jnp.zeros((16, BLK), F32)
    for b in range(2):
        for k in range(NZB):
            vec = jnp.where(lane == b * NZB + k, cols[span, b, k].astype(F32), vec)
    tail[TAIL_COLS : TAIL_COLS + 16, :] = vec.astype(BF16)
    for c in started:
        c.wait()
    tail[TAIL_START : TAIL_START + 256, :] = start[:, :BLK]
    tail[TAIL_START + 256 : TAIL_START + 512, :] = start[:, BLK:]


def pack(tiles, initial, cotangent, cols):
    rest = 2 * NZB - HEAD_TILES
    any_spec = pl.BlockSpec(memory_space=pl.ANY)
    vmem = pl.BlockSpec(memory_space=pltpu.VMEM)
    return pl.pallas_call(
        pack_kernel,
        in_specs=[any_spec, any_spec, any_spec, pl.BlockSpec(memory_space=pltpu.SMEM)],
        out_specs=[vmem] * 3,
        out_shape=[
            jax.ShapeDtypeStruct((HEAD_TILES, BLK, BLK), BF16),
            jax.ShapeDtypeStruct((TAIL_COLS + 16, BLK), BF16),
            jax.ShapeDtypeStruct((256, 256), BF16),
        ],
        scratch_shapes=[pltpu.VMEM((256, 256), BF16), pltpu.SemaphoreType.DMA((3 + rest,))],
        name="pack",
    )(tiles, initial, cotangent, cols)


def dot(a, b, dims):
    return lax.dot_general(a, b, (dims, ((), ())), preferred_element_type=F32)


def layers_kernel(scale, betas, *refs):
    heads, tails, cots, weights = refs[0:8], refs[8:16], refs[16:24], refs[24:28]
    grad_initial, grad_weights = refs[28:30]
    start, weight, cols_int, cols, hidden, mixes, slopes, dpre, dw, sem = refs[30:]
    dom = lax.axis_index("dom")
    phase = lax.axis_index("phase")
    x, core = dom // 2, dom % 2
    layers = len(weights)
    for n in range(8):
        j = tails[n][TAIL_COLS : TAIL_COLS + 16, :].astype(F32).astype(jnp.int32)
        chip = lax.bitwise_and(x - lax.shift_right_logical(j, 2) + 4, 3)
        side = lax.bitwise_xor(lax.bitwise_and(lax.shift_right_logical(j, 1), 1), core)
        place = chip * 4 + side * 2 + lax.bitwise_and(j, 1)
        cols_int[n : n + 1, :] = (place * BLK)[:1]
    to_scalars = pltpu.make_async_copy(cols_int, cols, sem)
    to_scalars.start()
    for n in range(8):
        for half in range(2):
            part = tails[n][TAIL_START + 256 * half : TAIL_START + 256 * (half + 1), :]
            lanes = slice(BLK * half, BLK * (half + 1))
            hidden[0, 256 * n : 256 * (n + 1), lanes] = part
            start[256 * n : 256 * (n + 1), lanes] = ALPHA * part.astype(F32)
    for n in range(layers):
        weight[(phase - n + layers) % layers] = weights[n][0]
    to_scalars.wait()

    def tile(i, k):
        n, t = i // 2, (i % 2) * NZB + k
        if t < HEAD_TILES:
            return heads[n][t]
        return tails[n][(t - HEAD_TILES) * BLK : (t - HEAD_TILES + 1) * BLK, :]

    def aggregate(src, i):
        blocks = [hidden[src, i * BLK : (i + 1) * BLK, :]]
        for k in range(1, NZB):
            j = pl.multiple_of(cols[i // 2, (i % 2) * NZB + k], BLK)
            blocks.append(hidden[src, pl.ds(j, BLK), :])
        lhs = jnp.concatenate([tile(i, k) for k in range(NZB)], axis=1)
        return (1.0 - ALPHA) * dot(lhs, jnp.concatenate(blocks, axis=0), ((1,), (0,)))

    chunks = start.shape[0] // (CHUNK * BLK)

    def pipeline(first, second, third):
        held = {}
        for s in range(chunks + 2):
            if s < chunks:
                first(s)
            if 0 <= s - 1 < chunks:
                held[s - 1] = second(s - 1)
            if 0 <= s - 2 < chunks:
                third(s - 2, held.pop(s - 2))

    def pick(values, l):
        out = jnp.float32(values[0])
        for n in range(1, len(values)):
            out = jnp.where(l == n, jnp.float32(values[n]), out)
        return out

    def rows_of(c):
        return slice(c * CHUNK * BLK, (c + 1) * CHUNK * BLK)

    def forward(l, _):
        src, dst = l % 2, (l + 1) % 2
        beta = pick(betas, l)
        w = weight[l]

        def first(c):
            for i in range(c * CHUNK, (c + 1) * CHUNK):
                rows = slice(i * BLK, (i + 1) * BLK)
                mixes[l, rows, :] = (aggregate(src, i) + start[rows, :]).astype(BF16)

        def second(c):
            return dot(mixes[l, rows_of(c), :], w, ((1,), (0,)))

        def third(c, product):
            rows = rows_of(c)
            pre = (1.0 - beta) * mixes[l, rows, :].astype(F32) + beta * product
            square = pre * pre
            t = jnp.tanh(pre * (GELU_C + (GELU_C * GELU_B) * square))
            half = 0.5 + 0.5 * t
            out = pre * half
            hidden[dst, rows, :] = out.astype(BF16)
            slopes[l, rows, :] = half + out * (1.0 - half) * (
                2.0 * GELU_C + (6.0 * GELU_C * GELU_B) * square
            )

        pipeline(first, second, third)
        return 0

    def backward(step, _, top=False):
        l = layers - 1 - step
        src, dst = step % 2, (step + 1) % 2
        beta = pick(betas, l)
        w = weight[l]

        def first(c):
            for i in range(c * CHUNK, (c + 1) * CHUNK):
                rows = slice(i * BLK, (i + 1) * BLK)
                if top:
                    back = cots[i // 2][(i % 2) * BLK : (i % 2 + 1) * BLK, :]
                else:
                    back = aggregate(src, i).astype(BF16)
                dpre[rows, :] = (slopes[l, rows, :] * back.astype(F32)).astype(BF16)

        def second(c):
            return dot(dpre[rows_of(c), :], w, ((1,), (1,)))

        def third(c, product):
            rows = rows_of(c)
            dmix = (1.0 - beta) * dpre[rows, :].astype(F32) + beta * product
            hidden[dst, rows, :] = dmix.astype(BF16)

        pipeline(first, second, third)
        term = ALPHA * hidden[dst, 0:256, :].astype(F32)
        grad_initial[0] = term if top else grad_initial[0] + term
        dw[...] = (beta * scale) * dot(mixes[l], dpre[...], ((0,), (0,)))
        grad_weights[l] = dw[pl.ds(pl.multiple_of(dom * 32, 32), 32), :]
        return 0

    lax.fori_loop(0, layers, forward, 0)
    backward(0, 0, top=True)
    lax.fori_loop(1, layers, backward, 0)
    for b in range(2):
        rows = slice(b * BLK, (b + 1) * BLK)
        back = aggregate(layers % 2, b).astype(BF16)
        grad_initial[0, rows, :] = grad_initial[0, rows, :] + back.astype(F32)


def run_layers(scale, betas, heads, tails, cots, weights):
    vmem = pl.BlockSpec(memory_space=pltpu.VMEM)
    nodes, width = 2048, 256
    return pl.pallas_call(
        functools.partial(layers_kernel, scale, betas),
        in_specs=[vmem] * 28,
        out_specs=[vmem, vmem],
        out_shape=[
            jax.ShapeDtypeStruct((1, 256, width), F32),
            jax.ShapeDtypeStruct((4, 32, width), F32),
        ],
        scratch_shapes=[
            pltpu.VMEM((nodes, width), F32),
            pltpu.VMEM((4, width, width), BF16),
            pltpu.VMEM((8, BLK), jnp.int32),
            pltpu.SMEM((8, BLK), jnp.int32),
            pltpu.VMEM((2, nodes, width), BF16),
            pltpu.VMEM((4, nodes, width), BF16),
            pltpu.VMEM((4, nodes, width), F32),
            pltpu.VMEM((nodes, width), BF16),
            pltpu.VMEM((width, width), F32),
            pltpu.SemaphoreType.DMA,
        ],
        compiler_params=pltpu.CompilerParams(vmem_limit_bytes=40 * 1024 * 1024),
        cost_estimate=pl.CostEstimate(flops=9_000_000_000, bytes_accessed=6_000_000, transcendentals=0),
        name="layers",
    )(*heads, *tails, *cots, *weights)


def ring(v, step):
    return lax.ppermute(v, "dom", [(i, (i + 2 * step) % 8) for i in range(8)])


def other_core(v):
    return lax.ppermute(v, "dom", [(i, i ^ 1) for i in range(8)])


def both_cores(pieces):
    out = []
    for piece in pieces:
        out += [piece, other_core(piece)]
    return out


def local(initial, block_cols, block_tiles, layer_weights, cotangent):
    layers = lax.axis_size("phase")
    nodes_all = 4 * 2048 * lax.axis_size("dp")
    scale = 1.0 / math.sqrt(nodes_all)
    betas = [math.log(THETA / (l + 1) + 1.0) for l in range(layers)]
    spans, rows = block_tiles.shape[:2]
    tiles = block_tiles.reshape(spans, rows * NZB, BLK, BLK)
    head, tail, cot = pack(tiles, initial, cotangent, block_cols)
    head_left, head_right = ring(head, 1), ring(head, -1)
    tail_left, tail_right = ring(tail, 1), ring(tail, -1)
    heads = both_cores([head, head_left, ring(head_left, 1), head_right])
    tails = both_cores([tail, tail_left, ring(tail_right, -1), tail_right])
    weights = [layer_weights] + [
        lax.ppermute(layer_weights, "phase", [(i, (i + n) % 4) for i in range(4)]) for n in (1, 2, 3)
    ]
    cot, head_left, tail_right = lax.optimization_barrier((cot, head_left, tail_right))
    cot_left, cot_right = ring(cot, 1), ring(cot, -1)
    cots = both_cores([cot, cot_left, ring(cot_left, 1), cot_right])
    grad_initial, parts = run_layers(scale, betas, heads, tails, cots, weights)
    parts = lax.all_to_all(parts, "phase", 0, 0, tiled=True)
    mine = jnp.sum(parts, axis=0)
    mine = jnp.broadcast_to(mine[None], (8,) + mine.shape)
    mine = jnp.sum(lax.all_to_all(mine, "dp", 0, 0, tiled=True), axis=0)
    mine = jnp.broadcast_to(mine[None], (8,) + mine.shape)
    mine = lax.all_to_all(mine, "dom", 0, 0, tiled=True)
    return grad_initial, mine.reshape(1, 256, 256)


def solution(mesh):
    placed = (
        P("dp", "dom", None),
        P("dp", "dom", None),
        P("dp", "dom", None, None, None),
        P("phase", None, None),
        P("dp", "dom", None),
    )
    return jax.shard_map(
        local,
        mesh=mesh,
        in_specs=placed,
        out_specs=(P(("dp", "phase"), "dom", None), P("phase", None, None)),
        check_vma=False,
    )
```

time: 161 us -> 103 us (0.64)
  Pallas kernels: 78.7 us -> 19.5 us
  waiting for transfers between devices: 10.1 us -> 13.2 us
    pallas_call x1, Pallas kernels: 58.9 us -> 16.7 us  [run_layers(): pl.pallas_call(functools.partial(layers_kernel, scale, betas), in_specs=[...]
    pallas_call x1, Pallas kernels: 19.8 us -> 2.79 us  [pack(): pl.pallas_call(pack_kernel, in_specs=[any_spec, any_spec, any_spec, pl.Bl...]
    ppermute x3, starting transfers between devices: 6.51 us -> 3.97 us  [local(): lax.ppermute(layer_weights, 'phase', [(i, (i + n) % 4) for i in range(4)])]
    ppermute x9, waiting for transfers between devices: 7.97 us -> 10.3 us  [ring(): return lax.ppermute(v, 'dom', [(i, (i + 2 * step) % 8) for i in range(8)])]
    ppermute x3, waiting for transfers between devices: 0.01 us -> 1.91 us  [local(): lax.ppermute(layer_weights, 'phase', [(i, (i + n) % 4) for i in range(4)])]
  transfers between devices with their start and end apart: 24 -> 24, of which waited for: 7 -> 6; matrix products, arithmetic and copies ran while one was open for 0% -> 0% of each run, Pallas kernels for 12% -> 0%
where the time goes in v2:
time: 103 us
  blocking collectives  36.9 us (36%)
  starting transfers between devices  29.2 us (28%)
  Pallas kernels  19.5 us (19%)
  waiting for transfers between devices  13.2 us (13%)
  local copies, waits for them, and re-layouts  3.53 us (3%)
    all_to_all x1, blocking collectives, local(): mine = jnp.sum(lax.all_to_all(mine, 'dp', 0, 0, tiled=True), axis=0)  17.1 us
    pallas_call x1, Pallas kernels, run_layers(): pl.pallas_call(functools.partial(layers_kernel, scale, betas), in_specs=[...  16.7 us
    ppermute x12, starting transfers between devices, other_core(): return lax.ppermute(v, 'dom', [(i, i ^ 1) for i in range(8)])  13.5 us
    all_to_all x1, blocking collectives, local(): mine = lax.all_to_all(mine, 'dom', 0, 0, tiled=True)  12.5 us
    ppermute x9, starting transfers between devices, ring(): return lax.ppermute(v, 'dom', [(i, (i + 2 * step) % 8) for i in range(8)])  11.7 us
    ppermute x9, waiting for transfers between devices, ring(): return lax.ppermute(v, 'dom', [(i, (i + 2 * step) % 8) for i in range(8)])  10.3 us
    all_to_all x1, blocking collectives, local(): parts = lax.all_to_all(parts, 'phase', 0, 0, tiled=True)  7.21 us
    ppermute x3, starting transfers between devices, local(): lax.ppermute(layer_weights, 'phase', [(i, (i + n) % 4) for i in range(4)])  3.97 us
  transfers between devices with their start and end apart: 24, of which 6 were waited for; matrix products, arithmetic and copies ran while one was open for 0% of the time, Pallas kernels for 0%

profile of v2, /device:TPU:1, one launch (start us, length us, event | category | flops | bytes accessed | tf_op | source)
XLA Modules:
  0.0 103.0 jit_solution(1531912901964400578)
XLA Ops:
  0.6 2.8 %pack.1 = (bf16[7,128,128]{2,1,0:T(8,128)(2,1)}, bf16[912,128]{1,0:T(8,128)(2,1)}, bf16[256,256]{1,0:T(8,128)(2,1)}) custom-call(bf16[4,10,128,128]{3,2,1,0:T(8,128)(2,1)} %bitcast.2, bf16[4,256,256]{2,1,0:T(8,128)(2,1)} %initial.1, bf16[4,256,256]{2,1,0:T(8,128)(2,1)} %cotangent.1, s32[4,2,5]{2,1,0:T(2,128)} %cols.1), custom_call_target="tpu_custom_call" | custom-call | tf_op jit(solution)/shard_map/pack/pallas_call | solution.py:54
  3.4 3.4 %collective-permute-start.10 = (bf16[912,128]{1,0:T(8,128)(2,1)}, bf16[912,128]{1,0:T(8,128)(2,1)S(1)}, u32[]{:S(2)}, u32[]{:S(2)}) collective-permute-start(bf16[912,128]{1,0:T(8,128)(2,1)} %get-tuple-element.9.refs_8_), channel_id=1, source_target_pairs={{0,6},{1,7},{2,0},{3,1},{4,2},{5,3},{6,4},{7,5},{8,14},{9,15},{10,... | collective-permute-start | bytes 700424 | tf_op jit(solution)/shard_map/ppermute | solution.py:230
  6.8 0.0 collective-permute-start.1
  6.8 2.9 %collective-permute-start.22 = (bf16[1,256,256]{2,1,0:T(8,128)(2,1)S(1)}, bf16[1,256,256]{2,1,0:T(8,128)(2,1)S(1)}, u32[]{:S(2)}, u32[]{:S(2)}) collective-permute-start(bf16[1,256,256]{2,1,0:T(8,128)(2,1)S(1)} %copy-done.2), channel_id=1, source_target_pairs={{0,16},{8,24},{16,0},{24,8},{1,17},{9,25},{17,1},{25,9},{2,18},{10... | collective-permute-start | bytes 393224 | tf_op jit(solution)/shard_map/ppermute | solution.py:257
  9.8 0.4 collective-permute-start.21
  10.1 2.7 %collective-permute-start.5 = (bf16[7,128,128]{2,1,0:T(8,128)(2,1)}, bf16[7,128,128]{2,1,0:T(8,128)(2,1)S(1)}, u32[]{:S(2)}, u32[]{:S(2)}) collective-permute-start(bf16[7,128,128]{2,1,0:T(8,128)(2,1)} %get-tuple-element.8.refs_0_), channel_id=1, source_target_pairs={{0,6},{1,7},{2,0},{3,1},{4,2},{5,3},{6,4},{7,5},{8,14},{9,15},{10,... | collective-permute-start | bytes 688136 | tf_op jit(solution)/shard_map/ppermute | solution.py:230
  12.8 3.4 %collective-permute-start = (bf16[7,128,128]{2,1,0:T(8,128)(2,1)}, bf16[7,128,128]{2,1,0:T(8,128)(2,1)S(1)}, u32[]{:S(2)}, u32[]{:S(2)}) collective-permute-start(bf16[7,128,128]{2,1,0:T(8,128)(2,1)} %get-tuple-element.8.refs_0_), channel_id=1, source_target_pairs={{0,1},{1,0},{2,3},{3,2},{4,5},{5,4},{6,7},{7,6},{8,9},{9,8},{10,11... | collective-permute-start | bytes 688136 | tf_op jit(solution)/shard_map/ppermute | solution.py:234
  16.3 0.6 collective-permute-done.21.refs_25_
  16.8 0.7 collective-permute-start.23
  17.5 1.8 %collective-permute-start.7 = (bf16[912,128]{1,0:T(8,128)(2,1)}, bf16[912,128]{1,0:T(8,128)(2,1)S(1)}, u32[]{:S(2)}, u32[]{:S(2)}) collective-permute-start(bf16[912,128]{1,0:T(8,128)(2,1)} %get-tuple-element.9.refs_8_), channel_id=1, source_target_pairs={{0,1},{1,0},{2,3},{3,2},{4,5},{5,4},{6,7},{7,6},{8,9},{9,8},{10,11... | collective-permute-start | bytes 700424 | tf_op jit(solution)/shard_map/ppermute | solution.py:234
  19.3 1.4 %collective-permute-done.23.refs_27_ = bf16[1,256,256]{2,1,0:T(8,128)(2,1)S(1)} collective-permute-done((bf16[1,256,256]{2,1,0:T(8,128)(2,1)S(1)}, bf16[1,256,256]{2,1,0:T(8,128)(2,1)S(1)}, u32[]{:S(2)}, u32[]{:S(2)}) %collective-permute-start.23) | collective-permute-done | bytes 131104 | tf_op jit(solution)/shard_map/ppermute | solution.py:257
  20.6 2.7 %collective-permute-start.19 = (bf16[256,256]{1,0:T(8,128)(2,1)}, bf16[256,256]{1,0:T(8,128)(2,1)S(1)}, u32[]{:S(2)}, u32[]{:S(2)}) collective-permute-start(bf16[256,256]{1,0:T(8,128)(2,1)} %get-tuple-element.11.refs_16_), channel_id=1, source_target_pairs={{0,6},{1,7},{2,0},{3,1},{4,2},{5,3},{6,4},{7,5},{8,14},{9,15},{10,... | collective-permute-start | bytes 393224 | tf_op jit(solution)/shard_map/ppermute | solution.py:230
  23.3 3.0 %collective-permute-start.6 = (bf16[7,128,128]{2,1,0:T(8,128)(2,1)S(1)}, bf16[7,128,128]{2,1,0:T(8,128)(2,1)S(1)}, u32[]{:S(2)}, u32[]{:S(2)}) collective-permute-start(bf16[7,128,128]{2,1,0:T(8,128)(2,1)S(1)} %collective-permute-done.5.refs_6_), channel_id=1, source_target_pairs={{0,1},{1,0},{2,3},{3,2},{4,5},{5,4},{6,7},{7,6},{8,9},{9,8},{10,11... | collective-permute-start | bytes 688136 | tf_op jit(solution)/shard_map/ppermute | solution.py:234
  26.4 0.0 collective-permute-done.refs_1_
  26.4 0.0 collective-permute-start.15
  26.4 0.0 collective-permute-done.8.refs_10_
  26.4 0.2 collective-permute-start.14
  26.6 0.0 collective-permute-done.7.refs_9_
  26.6 0.3 collective-permute-start.3
  26.9 0.0 collective-permute-done.19.refs_22_
  26.9 2.6 %collective-permute-start.11 = (bf16[912,128]{1,0:T(8,128)(2,1)S(1)}, bf16[912,128]{1,0:T(8,128)(2,1)S(1)}, u32[]{:S(2)}, u32[]{:S(2)}) collective-permute-start(bf16[912,128]{1,0:T(8,128)(2,1)S(1)} %collective-permute-done.10.refs_14_), channel_id=1, source_target_pairs={{0,6},{1,7},{2,0},{3,1},{4,2},{5,3},{6,4},{7,5},{8,14},{9,15},{10,... | collective-permute-start | bytes 700424 | tf_op jit(solution)/shard_map/ppermute | solution.py:230
  29.5 3.4 %collective-permute-done.15.refs_18_ = bf16[256,256]{1,0:T(8,128)(2,1)S(1)} collective-permute-done((bf16[256,256]{1,0:T(8,128)(2,1)}, bf16[256,256]{1,0:T(8,128)(2,1)S(1)}, u32[]{:S(2)}, u32[]{:S(2)}) %collective-permute-start.15) | collective-permute-done | bytes 131104 | tf_op jit(solution)/shard_map/ppermute | solution.py:230
  32.8 1.3 %collective-permute-start.2 = (bf16[7,128,128]{2,1,0:T(8,128)(2,1)S(1)}, bf16[7,128,128]{2,1,0:T(8,128)(2,1)S(1)}, u32[]{:S(2)}, u32[]{:S(2)}) collective-permute-start(bf16[7,128,128]{2,1,0:T(8,128)(2,1)S(1)} %collective-permute-done.1.refs_2_), channel_id=1, source_target_pairs={{0,1},{1,0},{2,3},{3,2},{4,5},{5,4},{6,7},{7,6},{8,9},{9,8},{10,11... | collective-permute-start | bytes 688136 | tf_op jit(solution)/shard_map/ppermute | solution.py:234
  34.2 0.0 collective-permute-done.14.refs_17_
  34.2 0.0 collective-permute-start.13
  34.2 0.0 collective-permute-done.6.refs_7_
  34.2 0.5 collective-permute-start.9
  34.7 3.1 %collective-permute-done.3.refs_4_ = bf16[7,128,128]{2,1,0:T(8,128)(2,1)S(1)} collective-permute-done((bf16[7,128,128]{2,1,0:T(8,128)(2,1)S(1)}, bf16[7,128,128]{2,1,0:T(8,128)(2,1)S(1)}, u32[]{:S(2)}, u32[]{:S(2)}) %collective-permute-start.3) | collective-permute-done | bytes 229408 | tf_op jit(solution)/shard_map/ppermute | solution.py:230
  37.8 0.0 collective-permute-start.17
  37.8 0.0 collective-permute-done.11.refs_12_
  37.8 0.9 collective-permute-start.12
  38.6 0.0 collective-permute-done.2.refs_3_
  38.6 0.1 collective-permute-start.4
  38.7 0.0 collective-permute-done.13.refs_15_
  38.7 0.4 collective-permute-start.16
  39.1 0.0 collective-permute-done.9.refs_11_
  39.2 0.1 collective-permute-start.20
  39.3 3.9 %collective-permute-done.17.refs_20_ = bf16[256,256]{1,0:T(8,128)(2,1)S(1)} collective-permute-done((bf16[256,256]{1,0:T(8,128)(2,1)S(1)}, bf16[256,256]{1,0:T(8,128)(2,1)S(1)}, u32[]{:S(2)}, u32[]{:S(2)}) %collective-permute-start.17) | collective-permute-done | bytes 131104 | tf_op jit(solution)/shard_map/ppermute | solution.py:230
  43.1 1.8 %collective-permute-start.18 = (bf16[256,256]{1,0:T(8,128)(2,1)S(1)}, bf16[256,256]{1,0:T(8,128)(2,1)S(1)}, u32[]{:S(2)}, u32[]{:S(2)}) collective-permute-start(bf16[256,256]{1,0:T(8,128)(2,1)S(1)} %collective-permute-done.17.refs_20_), channel_id=1, source_target_pairs={{0,1},{1,0},{2,3},{3,2},{4,5},{5,4},{6,7},{7,6},{8,9},{9,8},{10,11... | collective-permute-start | bytes 393224 | tf_op jit(solution)/shard_map/ppermute | solution.py:234
  44.9 1.0 collective-permute-done.18.refs_21_
  45.9 0.9 copy-done
  46.8 0.9 copy-done.1
  47.8 0.9 copy-done.3
  48.7 16.7 %layers.1 = (f32[1,256,256]{2,1,0:T(8,128)}, f32[4,32,256]{2,1,0:T(8,128)S(1)}) custom-call(bf16[7,128,128]{2,1,0:T(8,128)(2,1)S(1)} %copy-done.1, bf16[7,128,128]{2,1,0:T(8,128)(2,1)S(1)} %collective-permute-done.refs_1_, bf16[7,128,128]{2,1,0:T(8,128)(2,1)S(1)} %collective-permute-done.1.refs_2_, bf16[7,128,128]{2,1,0:T(8,128)(2,1)S(1)} %collective-permute-done.2.refs_3_, ...), custom_call_target="tpu_custom_call" | custom-call | flops 8999999488 | bytes 6000000 | tf_op jit(solution)/shard_map/layers/pallas_call | solution.py:203
  65.4 7.2 %all_to_all.15 = f32[4,32,256]{2,1,0:T(8,128)S(1)} all-to-all(f32[4,32,256]{2,1,0:T(8,128)S(1)} %get-tuple-element.13), channel_id=1, replica_groups=mesh['dp'=8,'phase'=4,'dom'=8] {'phase'}, dimensions={0} | all-to-all | bytes 262144 | tf_op jit(solution)/shard_map/all_to_all | solution.py:263
  72.6 17.1 %all_to_all.16 = f32[8,32,256]{2,1,0:T(8,128)S(1)} all-to-all(f32[8,32,256]{2,1,0:T(8,128)S(1)} %broadcast_in_dim.4), channel_id=1, replica_groups=mesh['dp'=8,'phase'=4,'dom'=8] {'dp'}, dimensions={0} | all-to-all | bytes 524288 | tf_op jit(solution)/shard_map/all_to_all | solution.py:266
  89.8 12.5 %all_to_all.17 = f32[8,32,256]{2,1,0:T(8,128)S(1)} all-to-all(f32[8,32,256]{2,1,0:T(8,128)S(1)} %broadcast_in_dim.5), channel_id=1, replica_groups=mesh['dp'=8,'phase'=4,'dom'=8] {'dom'}, dimensions={0} | all-to-all | bytes 524288 | tf_op jit(solution)/shard_map/all_to_all | solution.py:268
  102.3 0.7 copy.8
  (18 shorter events, 0.1 us)
Async XLA Ops:
  0.6 6.2 %copy-start.2 = (bf16[1,256,256]{2,1,0:T(8,128)(2,1)S(1)}, bf16[1,256,256]{2,1,0:T(8,128)(2,1)}, u32[]{:S(2)}) copy-start(bf16[1,256,256]{2,1,0:T(8,128)(2,1)} %refs_24_.1) | copy-start | bytes 393220
  3.4 14.0 %collective-permute-start.10 = (bf16[912,128]{1,0:T(8,128)(2,1)}, bf16[912,128]{1,0:T(8,128)(2,1)S(1)}, u32[]{:S(2)}, u32[]{:S(2)}) collective-permute-start(bf16[912,128]{1,0:T(8,128)(2,1)} %get-tuple-element.9.refs_8_), channel_id=1, source_target_pairs={{0,6},{1,7},{2,0},{3,1},{4,2},{5,3},{6,4},{7,5},{8,14},{9,15},{10,... | collective-permute-start | bytes 700424 | tf_op jit(solution)/shard_map/ppermute | solution.py:230
  6.8 10.0 %collective-permute-start.1 = (bf16[7,128,128]{2,1,0:T(8,128)(2,1)}, bf16[7,128,128]{2,1,0:T(8,128)(2,1)S(1)}, u32[]{:S(2)}, u32[]{:S(2)}) collective-permute-start(bf16[7,128,128]{2,1,0:T(8,128)(2,1)} %get-tuple-element.8.refs_0_), channel_id=1, source_target_pairs={{0,2},{1,3},{2,4},{3,5},{4,6},{5,7},{6,0},{7,1},{8,10},{9,11},{10,... | collective-permute-start | bytes 688136 | tf_op jit(solution)/shard_map/ppermute | solution.py:230
  6.8 6.0 %collective-permute-start.22 = (bf16[1,256,256]{2,1,0:T(8,128)(2,1)S(1)}, bf16[1,256,256]{2,1,0:T(8,128)(2,1)S(1)}, u32[]{:S(2)}, u32[]{:S(2)}) collective-permute-start(bf16[1,256,256]{2,1,0:T(8,128)(2,1)S(1)} %copy-done.2), channel_id=1, source_target_pairs={{0,16},{8,24},{16,0},{24,8},{1,17},{9,25},{17,1},{25,9},{2,18},{10... | collective-permute-start | bytes 393224 | tf_op jit(solution)/shard_map/ppermute | solution.py:257
  9.8 7.1 %collective-permute-start.21 = (bf16[1,256,256]{2,1,0:T(8,128)(2,1)S(1)}, bf16[1,256,256]{2,1,0:T(8,128)(2,1)S(1)}, u32[]{:S(2)}, u32[]{:S(2)}) collective-permute-start(bf16[1,256,256]{2,1,0:T(8,128)(2,1)S(1)} %copy-done.2), channel_id=1, source_target_pairs={{0,8},{8,16},{16,24},{24,0},{1,9},{9,17},{17,25},{25,1},{2,10},{10... | collective-permute-start | bytes 393224 | tf_op jit(solution)/shard_map/ppermute | solution.py:257
  10.1 13.2 %collective-permute-start.5 = (bf16[7,128,128]{2,1,0:T(8,128)(2,1)}, bf16[7,128,128]{2,1,0:T(8,128)(2,1)S(1)}, u32[]{:S(2)}, u32[]{:S(2)}) collective-permute-start(bf16[7,128,128]{2,1,0:T(8,128)(2,1)} %get-tuple-element.8.refs_0_), channel_id=1, source_target_pairs={{0,6},{1,7},{2,0},{3,1},{4,2},{5,3},{6,4},{7,5},{8,14},{9,15},{10,... | collective-permute-start | bytes 688136 | tf_op jit(solution)/shard_map/ppermute | solution.py:230
  12.8 13.5 %collective-permute-start = (bf16[7,128,128]{2,1,0:T(8,128)(2,1)}, bf16[7,128,128]{2,1,0:T(8,128)(2,1)S(1)}, u32[]{:S(2)}, u32[]{:S(2)}) collective-permute-start(bf16[7,128,128]{2,1,0:T(8,128)(2,1)} %get-tuple-element.8.refs_0_), channel_id=1, source_target_pairs={{0,1},{1,0},{2,3},{3,2},{4,5},{5,4},{6,7},{7,6},{8,9},{9,8},{10,11... | collective-permute-start | bytes 688136 | tf_op jit(solution)/shard_map/ppermute | solution.py:234
  16.8 9.6 %collective-permute-start.8 = (bf16[912,128]{1,0:T(8,128)(2,1)}, bf16[912,128]{1,0:T(8,128)(2,1)S(1)}, u32[]{:S(2)}, u32[]{:S(2)}) collective-permute-start(bf16[912,128]{1,0:T(8,128)(2,1)} %get-tuple-element.9.refs_8_), channel_id=1, source_target_pairs={{0,2},{1,3},{2,4},{3,5},{4,6},{5,7},{6,0},{7,1},{8,10},{9,11},{10,... | collective-permute-start | bytes 700424 | tf_op jit(solution)/shard_map/ppermute | solution.py:230
  16.8 3.8 %collective-permute-start.23 = (bf16[1,256,256]{2,1,0:T(8,128)(2,1)S(1)}, bf16[1,256,256]{2,1,0:T(8,128)(2,1)S(1)}, u32[]{:S(2)}, u32[]{:S(2)}) collective-permute-start(bf16[1,256,256]{2,1,0:T(8,128)(2,1)S(1)} %copy-done.2), channel_id=1, source_target_pairs={{0,24},{8,0},{16,8},{24,16},{1,25},{9,1},{17,9},{25,17},{2,26},{10... | collective-permute-start | bytes 393224 | tf_op jit(solution)/shard_map/ppermute | solution.py:257
  17.5 9.1 %collective-permute-start.7 = (bf16[912,128]{1,0:T(8,128)(2,1)}, bf16[912,128]{1,0:T(8,128)(2,1)S(1)}, u32[]{:S(2)}, u32[]{:S(2)}) collective-permute-start(bf16[912,128]{1,0:T(8,128)(2,1)} %get-tuple-element.9.refs_8_), channel_id=1, source_target_pairs={{0,1},{1,0},{2,3},{3,2},{4,5},{5,4},{6,7},{7,6},{8,9},{9,8},{10,11... | collective-permute-start | bytes 700424 | tf_op jit(solution)/shard_map/ppermute | solution.py:234
  20.6 6.3 %collective-permute-start.19 = (bf16[256,256]{1,0:T(8,128)(2,1)}, bf16[256,256]{1,0:T(8,128)(2,1)S(1)}, u32[]{:S(2)}, u32[]{:S(2)}) collective-permute-start(bf16[256,256]{1,0:T(8,128)(2,1)} %get-tuple-element.11.refs_16_), channel_id=1, source_target_pairs={{0,6},{1,7},{2,0},{3,1},{4,2},{5,3},{6,4},{7,5},{8,14},{9,15},{10,... | collective-permute-start | bytes 393224 | tf_op jit(solution)/shard_map/ppermute | solution.py:230
  23.3 10.9 %collective-permute-start.6 = (bf16[7,128,128]{2,1,0:T(8,128)(2,1)S(1)}, bf16[7,128,128]{2,1,0:T(8,128)(2,1)S(1)}, u32[]{:S(2)}, u32[]{:S(2)}) collective-permute-start(bf16[7,128,128]{2,1,0:T(8,128)(2,1)S(1)} %collective-permute-done.5.refs_6_), channel_id=1, source_target_pairs={{0,1},{1,0},{2,3},{3,2},{4,5},{5,4},{6,7},{7,6},{8,9},{9,8},{10,11... | collective-permute-start | bytes 688136 | tf_op jit(solution)/shard_map/ppermute | solution.py:234
  26.4 6.5 %collective-permute-start.15 = (bf16[256,256]{1,0:T(8,128)(2,1)}, bf16[256,256]{1,0:T(8,128)(2,1)S(1)}, u32[]{:S(2)}, u32[]{:S(2)}) collective-permute-start(bf16[256,256]{1,0:T(8,128)(2,1)} %get-tuple-element.11.refs_16_), channel_id=1, source_target_pairs={{0,2},{1,3},{2,4},{3,5},{4,6},{5,7},{6,0},{7,1},{8,10},{9,11},{10,... | collective-permute-start | bytes 393224 | tf_op jit(solution)/shard_map/ppermute | solution.py:230
  26.4 7.8 %collective-permute-start.14 = (bf16[256,256]{1,0:T(8,128)(2,1)}, bf16[256,256]{1,0:T(8,128)(2,1)S(1)}, u32[]{:S(2)}, u32[]{:S(2)}) collective-permute-start(bf16[256,256]{1,0:T(8,128)(2,1)} %get-tuple-element.11.refs_16_), channel_id=1, source_target_pairs={{0,1},{1,0},{2,3},{3,2},{4,5},{5,4},{6,7},{7,6},{8,9},{9,8},{10,11... | collective-permute-start | bytes 393224 | tf_op jit(solution)/shard_map/ppermute | solution.py:234
  26.6 11.2 %collective-permute-start.3 = (bf16[7,128,128]{2,1,0:T(8,128)(2,1)S(1)}, bf16[7,128,128]{2,1,0:T(8,128)(2,1)S(1)}, u32[]{:S(2)}, u32[]{:S(2)}) collective-permute-start(bf16[7,128,128]{2,1,0:T(8,128)(2,1)S(1)} %collective-permute-done.1.refs_2_), channel_id=1, source_target_pairs={{0,2},{1,3},{2,4},{3,5},{4,6},{5,7},{6,0},{7,1},{8,10},{9,11},{10,... | collective-permute-start | bytes 688136 | tf_op jit(solution)/shard_map/ppermute | solution.py:230
  26.9 10.9 %collective-permute-start.11 = (bf16[912,128]{1,0:T(8,128)(2,1)S(1)}, bf16[912,128]{1,0:T(8,128)(2,1)S(1)}, u32[]{:S(2)}, u32[]{:S(2)}) collective-permute-start(bf16[912,128]{1,0:T(8,128)(2,1)S(1)} %collective-permute-done.10.refs_14_), channel_id=1, source_target_pairs={{0,6},{1,7},{2,0},{3,1},{4,2},{5,3},{6,4},{7,5},{8,14},{9,15},{10,... | collective-permute-start | bytes 700424 | tf_op jit(solution)/shard_map/ppermute | solution.py:230
  32.8 5.8 %collective-permute-start.2 = (bf16[7,128,128]{2,1,0:T(8,128)(2,1)S(1)}, bf16[7,128,128]{2,1,0:T(8,128)(2,1)S(1)}, u32[]{:S(2)}, u32[]{:S(2)}) collective-permute-start(bf16[7,128,128]{2,1,0:T(8,128)(2,1)S(1)} %collective-permute-done.1.refs_2_), channel_id=1, source_target_pairs={{0,1},{1,0},{2,3},{3,2},{4,5},{5,4},{6,7},{7,6},{8,9},{9,8},{10,11... | collective-permute-start | bytes 688136 | tf_op jit(solution)/shard_map/ppermute | solution.py:234
  34.2 4.6 %collective-permute-start.13 = (bf16[912,128]{1,0:T(8,128)(2,1)S(1)}, bf16[912,128]{1,0:T(8,128)(2,1)S(1)}, u32[]{:S(2)}, u32[]{:S(2)}) collective-permute-start(bf16[912,128]{1,0:T(8,128)(2,1)S(1)} %collective-permute-done.10.refs_14_), channel_id=1, source_target_pairs={{0,1},{1,0},{2,3},{3,2},{4,5},{5,4},{6,7},{7,6},{8,9},{9,8},{10,11... | collective-permute-start | bytes 700424 | tf_op jit(solution)/shard_map/ppermute | solution.py:234
  34.2 5.0 %collective-permute-start.9 = (bf16[912,128]{1,0:T(8,128)(2,1)S(1)}, bf16[912,128]{1,0:T(8,128)(2,1)S(1)}, u32[]{:S(2)}, u32[]{:S(2)}) collective-permute-start(bf16[912,128]{1,0:T(8,128)(2,1)S(1)} %collective-permute-done.8.refs_10_), channel_id=1, source_target_pairs={{0,1},{1,0},{2,3},{3,2},{4,5},{5,4},{6,7},{7,6},{8,9},{9,8},{10,11... | collective-permute-start | bytes 700424 | tf_op jit(solution)/shard_map/ppermute | solution.py:234
  37.8 5.4 %collective-permute-start.17 = (bf16[256,256]{1,0:T(8,128)(2,1)S(1)}, bf16[256,256]{1,0:T(8,128)(2,1)S(1)}, u32[]{:S(2)}, u32[]{:S(2)}) collective-permute-start(bf16[256,256]{1,0:T(8,128)(2,1)S(1)} %collective-permute-done.15.refs_18_), channel_id=1, source_target_pairs={{0,2},{1,3},{2,4},{3,5},{4,6},{5,7},{6,0},{7,1},{8,10},{9,11},{10,... | collective-permute-start | bytes 393224 | tf_op jit(solution)/shard_map/ppermute | solution.py:230
  37.8 8.1 %collective-permute-start.12 = (bf16[912,128]{1,0:T(8,128)(2,1)S(1)}, bf16[912,128]{1,0:T(8,128)(2,1)S(1)}, u32[]{:S(2)}, u32[]{:S(2)}) collective-permute-start(bf16[912,128]{1,0:T(8,128)(2,1)S(1)} %collective-permute-done.11.refs_12_), channel_id=1, source_target_pairs={{0,1},{1,0},{2,3},{3,2},{4,5},{5,4},{6,7},{7,6},{8,9},{9,8},{10,11... | collective-permute-start | bytes 700424 | tf_op jit(solution)/shard_map/ppermute | solution.py:234
  38.6 7.2 %collective-permute-start.4 = (bf16[7,128,128]{2,1,0:T(8,128)(2,1)S(1)}, bf16[7,128,128]{2,1,0:T(8,128)(2,1)S(1)}, u32[]{:S(2)}, u32[]{:S(2)}) collective-permute-start(bf16[7,128,128]{2,1,0:T(8,128)(2,1)S(1)} %collective-permute-done.3.refs_4_), channel_id=1, source_target_pairs={{0,1},{1,0},{2,3},{3,2},{4,5},{5,4},{6,7},{7,6},{8,9},{9,8},{10,11... | collective-permute-start | bytes 688136 | tf_op jit(solution)/shard_map/ppermute | solution.py:234
  38.7 6.2 %collective-permute-start.16 = (bf16[256,256]{1,0:T(8,128)(2,1)S(1)}, bf16[256,256]{1,0:T(8,128)(2,1)S(1)}, u32[]{:S(2)}, u32[]{:S(2)}) collective-permute-start(bf16[256,256]{1,0:T(8,128)(2,1)S(1)} %collective-permute-done.15.refs_18_), channel_id=1, source_target_pairs={{0,1},{1,0},{2,3},{3,2},{4,5},{5,4},{6,7},{7,6},{8,9},{9,8},{10,11... | collective-permute-start | bytes 393224 | tf_op jit(solution)/shard_map/ppermute | solution.py:234
  39.2 5.7 %collective-permute-start.20 = (bf16[256,256]{1,0:T(8,128)(2,1)S(1)}, bf16[256,256]{1,0:T(8,128)(2,1)S(1)}, u32[]{:S(2)}, u32[]{:S(2)}) collective-permute-start(bf16[256,256]{1,0:T(8,128)(2,1)S(1)} %collective-permute-done.19.refs_22_), channel_id=1, source_target_pairs={{0,1},{1,0},{2,3},{3,2},{4,5},{5,4},{6,7},{7,6},{8,9},{9,8},{10,11... | collective-permute-start | bytes 393224 | tf_op jit(solution)/shard_map/ppermute | solution.py:234
  43.1 2.7 %collective-permute-start.18 = (bf16[256,256]{1,0:T(8,128)(2,1)S(1)}, bf16[256,256]{1,0:T(8,128)(2,1)S(1)}, u32[]{:S(2)}, u32[]{:S(2)}) collective-permute-start(bf16[256,256]{1,0:T(8,128)(2,1)S(1)} %collective-permute-done.17.refs_20_), channel_id=1, source_target_pairs={{0,1},{1,0},{2,3},{3,2},{4,5},{5,4},{6,7},{7,6},{8,9},{9,8},{10,11... | collective-permute-start | bytes 393224 | tf_op jit(solution)/shard_map/ppermute | solution.py:234
  45.9 0.9 copy-start
  46.8 0.9 copy-start.1
  47.8 0.9 copy-start.3

commit v3 on v2

v3 whole, which is shorter than its diff:
```python
import functools
import math

import jax
import jax.numpy as jnp
from jax import lax
from jax.experimental import pallas as pl
from jax.experimental.pallas import tpu as pltpu
from jax.sharding import PartitionSpec as P

ALPHA = 0.1
THETA = 0.5
BLK = 128
NZB = 5
GELU_C = math.sqrt(2.0 / math.pi)
GELU_B = 0.044715
ROWS = 2 * BLK
TILE_ROWS = 2 * NZB * BLK
CUT = 9 * BLK
START = TILE_ROWS
COT = START + 2 * ROWS
COLS = COT + 2 * ROWS
PIECE = COLS + 16
CHUNK = 4
LAG = 8
GELU_C = math.sqrt(2.0 / math.pi)
GELU_B = 0.044715
HEAD_TILES = 7
TAIL_START = (2 * NZB - HEAD_TILES) * BLK
TAIL_COLS = TAIL_START + 512
CHUNK = 4
LAG = 8
BF16 = jnp.bfloat16
F32 = jnp.float32


def pack_kernel(tiles, initial, cotangent, cols, piece, start, cot, sems):
    span = lax.axis_index("phase")
    copies = [(initial.at[span], start), (cotangent.at[span], cot)]
    for t in range(2 * NZB):
        copies.append((tiles.at[span, t], piece.at[pl.ds(t * BLK, BLK)]))
    started = [pltpu.make_async_copy(a, b, sems.at[n]) for n, (a, b) in enumerate(copies)]
    for c in started:
        c.start()
    lane = lax.broadcasted_iota(jnp.int32, (16, BLK), 1)
    vec = jnp.zeros((16, BLK), F32)
    for b in range(2):
        for k in range(NZB):
            vec = jnp.where(lane == b * NZB + k, cols[span, b, k].astype(F32), vec)
    piece[COLS : COLS + 16, :] = vec.astype(BF16)
    for c in started:
        c.wait()
    for base, array in ((START, start), (COT, cot)):
        piece[base : base + ROWS, :] = array[:, :BLK]
        piece[base + ROWS : base + 2 * ROWS, :] = array[:, BLK:]


def pack(tiles, initial, cotangent, cols):
    any_spec = pl.BlockSpec(memory_space=pl.ANY)
    return pl.pallas_call(
        pack_kernel,
        in_specs=[any_spec, any_spec, any_spec, pl.BlockSpec(memory_space=pltpu.SMEM)],
        out_specs=pl.BlockSpec(memory_space=pltpu.VMEM),
        out_shape=pltpu.VMEM((PIECE, BLK), BF16),
        scratch_shapes=[
            pltpu.VMEM((ROWS, 2 * BLK), BF16),
            pltpu.VMEM((ROWS, 2 * BLK), BF16),
            pltpu.SemaphoreType.DMA((2 + 2 * NZB,)),
        ],
        name="pack",
    )(*[pltpu.with_memory_space_constraint(a, pltpu.HBM) for a in (tiles, initial, cotangent)], cols)


def dot(a, b, dims):
    return lax.dot_general(a, b, (dims, ((), ())), preferred_element_type=F32)


def layers_kernel(scale, betas, layout, *refs):
    count = sum(len(p) for p in layout)
    inputs, weights = list(refs[:count]), refs[count : count + len(betas)]
    grad_initial, grad_weights = refs[count + len(betas) : count + len(betas) + 2]
    scratch = refs[count + len(betas) + 2 :]
    start, weight, cols_int, cols, hidden, mixes, slopes, dpre, dw, sem = scratch
    pieces = []
    for parts in layout:
        spots = []
        for low, high in parts:
            spots.append((low, high, inputs.pop(0)))
        pieces.append(spots)

    def piece(n, low, rows):
        for first, last, ref in pieces[n]:
            if first <= low < last:
                return ref[low - first : low - first + rows, :]

    dom = lax.axis_index("dom")
    phase = lax.axis_index("phase")
    x, core = dom // 2, dom % 2
    layers = len(weights)
    for n in range(layers):
        weight[(phase - n + layers) % layers] = weights[n][0]
    for n in range(8):
        j = piece(n, COLS, 16).astype(F32).astype(jnp.int32)
        chip = lax.bitwise_and(x - lax.shift_right_logical(j, 2) + 4, 3)
        side = lax.bitwise_xor(lax.bitwise_and(lax.shift_right_logical(j, 1), 1), core)
        place = chip * 4 + side * 2 + lax.bitwise_and(j, 1)
        cols_int[n : n + 1, :] = (place * BLK)[:1]
    to_scalars = pltpu.make_async_copy(cols_int, cols, sem)
    to_scalars.start()
    for n in range(8):
        for half in range(2):
            part = piece(n, START + ROWS * half, ROWS)
            lanes = slice(BLK * half, BLK * (half + 1))
            hidden[0, ROWS * n : ROWS * (n + 1), lanes] = part
            start[ROWS * n : ROWS * (n + 1), lanes] = ALPHA * part.astype(F32)
    to_scalars.wait()

    def tile(i, k):
        return piece(i // 2, ((i % 2) * NZB + k) * BLK, BLK)

    def aggregate(src, i):
        blocks = [hidden[src, i * BLK : (i + 1) * BLK, :]]
        for k in range(1, NZB):
            j = pl.multiple_of(cols[i // 2, (i % 2) * NZB + k], BLK)
            blocks.append(hidden[src, pl.ds(j, BLK), :])
        lhs = jnp.concatenate([tile(i, k) for k in range(NZB)], axis=1)
        return (1.0 - ALPHA) * dot(lhs, jnp.concatenate(blocks, axis=0), ((1,), (0,)))

    blocks_all = start.shape[0] // BLK

    def pipeline(first, second, third):
        held = {}
        for s in range(blocks_all + LAG):
            if s < blocks_all:
                first(s)
            if s < blocks_all + CHUNK and s >= CHUNK and s % CHUNK == 0:
                held[s // CHUNK - 1] = second(s // CHUNK - 1)
            i = s - LAG
            if 0 <= i < blocks_all:
                product = held[i // CHUNK]
                third(i, product[(i % CHUNK) * BLK : (i % CHUNK + 1) * BLK, :])

    def pick(values, l):
        out = jnp.float32(values[0])
        for n in range(1, len(values)):
            out = jnp.where(l == n, jnp.float32(values[n]), out)
        return out

    def forward(l, _):
        src, dst = l % 2, (l + 1) % 2
        beta = pick(betas, l)
        w = weight[l]

        def first(i):
            rows = slice(i * BLK, (i + 1) * BLK)
            mixes[l, rows, :] = (aggregate(src, i) + start[rows, :]).astype(BF16)

        def second(c):
            return dot(mixes[l, c * CHUNK * BLK : (c + 1) * CHUNK * BLK, :], w, ((1,), (0,)))

        def third(i, product):
            rows = slice(i * BLK, (i + 1) * BLK)
            pre = (1.0 - beta) * mixes[l, rows, :].astype(F32) + beta * product
            square = pre * pre
            t = jnp.tanh(pre * (GELU_C + (GELU_C * GELU_B) * square))
            half = 0.5 + 0.5 * t
            out = pre * half
            hidden[dst, rows, :] = out.astype(BF16)
            slopes[l, rows, :] = half + out * (1.0 - half) * (
                2.0 * GELU_C + (6.0 * GELU_C * GELU_B) * square
            )

        pipeline(first, second, third)
        return 0

    def backward(step, _, top=False):
        l = layers - 1 - step
        src, dst = step % 2, (step + 1) % 2
        beta = pick(betas, l)
        w = weight[l]

        def first(i):
            rows = slice(i * BLK, (i + 1) * BLK)
            if top:
                low = COT + (i % 2) * BLK
                back = jnp.concatenate([piece(i // 2, low, BLK), piece(i // 2, low + ROWS, BLK)], axis=1)
            else:
                back = aggregate(src, i).astype(BF16)
            dpre[rows, :] = (slopes[l, rows, :] * back.astype(F32)).astype(BF16)

        def second(c):
            return dot(dpre[c * CHUNK * BLK : (c + 1) * CHUNK * BLK, :], w, ((1,), (1,)))

        def third(i, product):
            rows = slice(i * BLK, (i + 1) * BLK)
            dmix = (1.0 - beta) * dpre[rows, :].astype(F32) + beta * product
            hidden[dst, rows, :] = dmix.astype(BF16)

        pipeline(first, second, third)
        term = ALPHA * hidden[dst, 0:256, :].astype(F32)
        grad_initial[0] = term if top else grad_initial[0] + term
        lanes = pl.ds(pl.multiple_of(dom // 4 * BLK, BLK), BLK)
        dw[...] = (beta * scale) * dot(mixes[l, :, lanes], dpre[...], ((0,), (0,)))
        grad_weights[l] = dw[pl.ds(pl.multiple_of(dom % 4 * 32, 32), 32), :].astype(BF16)
        return 0

    lax.fori_loop(0, layers, forward, 0)
    backward(0, 0, top=True)
    lax.fori_loop(1, layers, backward, 0)
    for b in range(2):
        rows = slice(b * BLK, (b + 1) * BLK)
        back = aggregate(layers % 2, b).astype(BF16)
        grad_initial[0, rows, :] = grad_initial[0, rows, :] + back.astype(F32)


def run_layers(scale, betas, pieces, weights):
    vmem = pl.BlockSpec(memory_space=pltpu.VMEM)
    layout = [[(low, high) for low, high, _ in parts] for parts in pieces]
    arrays = [a for parts in pieces for _, _, a in parts]
    nodes, width = 2048, 256
    return pl.pallas_call(
        functools.partial(layers_kernel, scale, betas, layout),
        in_specs=[vmem] * (len(arrays) + len(weights)),
        out_specs=[vmem, vmem],
        out_shape=[
            jax.ShapeDtypeStruct((1, 256, width), F32),
            jax.ShapeDtypeStruct((4, 32, width), BF16),
        ],
        scratch_shapes=[
            pltpu.VMEM((nodes, width), F32),
            pltpu.VMEM((4, width, width), BF16),
            pltpu.VMEM((8, BLK), jnp.int32),
            pltpu.SMEM((8, BLK), jnp.int32),
            pltpu.VMEM((2, nodes, width), BF16),
            pltpu.VMEM((4, nodes, width), BF16),
            pltpu.VMEM((4, nodes, width), F32),
            pltpu.VMEM((nodes, width), BF16),
            pltpu.VMEM((BLK, width), F32),
            pltpu.SemaphoreType.DMA,
        ],
        compiler_params=pltpu.CompilerParams(vmem_limit_bytes=40 * 1024 * 1024),
        cost_estimate=pl.CostEstimate(flops=9_000_000_000, bytes_accessed=6_000_000, transcendentals=0),
        name="layers",
    )(*arrays, *weights)


def ring(v, step):
    return lax.ppermute(v, "dom", [(i, (i + 2 * step) % 8) for i in range(8)])


def other_core(v):
    return lax.ppermute(v, "dom", [(i, i ^ 1) for i in range(8)])


def phase_weights(w):
    return [w] + [lax.ppermute(w, "phase", [(i, (i + n) % 4) for i in range(4)]) for n in (1, 2, 3)]


def whole(v):
    return [(0, PIECE, v)]


def gather_halves(own, w):
    left, right = ring(own, 1), ring(own, -1)
    w, _ = lax.optimization_barrier((w, own))
    weights = phase_weights(w)
    top, low = ring(left[:CUT], 1), ring(right[CUT:], -1)
    pieces = [whole(own), whole(other_core(own)), whole(left), whole(other_core(left))]
    pieces.append([(0, CUT, top), (CUT, PIECE, low)])
    pieces.append([(0, CUT, other_core(top)), (CUT, PIECE, other_core(low))])
    pieces += [whole(right), whole(other_core(right))]
    return pieces, weights


def local(initial, block_cols, block_tiles, layer_weights, cotangent):
    layers = lax.axis_size("phase")
    nodes_all = 4 * 2048 * lax.axis_size("dp")
    scale = 1.0 / math.sqrt(nodes_all)
    betas = [math.log(THETA / (l + 1) + 1.0) for l in range(layers)]
    spans, rows = block_tiles.shape[:2]
    tiles = block_tiles.reshape(spans, rows * NZB, BLK, BLK)
    own = pack(tiles, initial, cotangent, block_cols)
    pieces, weights = gather_halves(own, layer_weights)
    grad_initial, parts = run_layers(scale, betas, pieces, weights)
    parts = lax.all_to_all(parts, "phase", 0, 0, tiled=True)
    mine = jnp.sum(parts.astype(F32), axis=0).astype(BF16)
    mine = jnp.broadcast_to(mine[None], (8,) + mine.shape)
    mine = jnp.sum(lax.all_to_all(mine, "dp", 0, 0, tiled=True).astype(F32), axis=0)
    mine = jnp.broadcast_to(mine[None], (8,) + mine.shape)
    mine = lax.all_to_all(mine, "dom", 0, 0, tiled=True)
    return grad_initial, mine.reshape(1, 256, 256)


def solution(mesh):
    placed = (
        P("dp", "dom", None),
        P("dp", "dom", None),
        P("dp", "dom", None, None, None),
        P("phase", None, None),
        P("dp", "dom", None),
    )
    return jax.shard_map(
        local,
        mesh=mesh,
        in_specs=placed,
        out_specs=(P(("dp", "phase"), "dom", None), P("phase", None, None)),
        check_vma=False,
    )
```

time: 103 us -> 89.6 us (0.87)
  starting transfers between devices: 29.2 us -> 16.4 us
  waiting for transfers between devices: 13.2 us -> 16.8 us
  local copies, waits for them, and re-layouts: 3.53 us -> 0.78 us
  Pallas kernels: 19.5 us -> 18 us
    ppermute x12 -> x5, starting transfers between devices: 13.5 us -> 5.67 us  [other_core(): return lax.ppermute(v, 'dom', [(i, i ^ 1) for i in range(8)])]
    ppermute x9 -> x4, waiting for transfers between devices: 10.3 us -> 15.6 us  [ring(): return lax.ppermute(v, 'dom', [(i, (i + 2 * step) % 8) for i in range(8)])]
    ppermute x9 -> x4, starting transfers between devices: 11.7 us -> 6.96 us  [ring(): return lax.ppermute(v, 'dom', [(i, (i + 2 * step) % 8) for i in range(8)])]
    unnamed x9 -> x3, local copies, waits for them, and re-layouts: 3.49 us -> 0.71 us
    ppermute x3, waiting for transfers between devices: 1.91 us -> 0.01 us  [phase_weights(): lax.ppermute(w, 'phase', [(i, (i + n) % 4) for i in range(4)])]
    all_to_all x1, blocking collectives: 7.21 us -> 8.47 us  [local(): parts = lax.all_to_all(parts, 'phase', 0, 0, tiled=True)]
    all_to_all x1, blocking collectives: 17.1 us -> 16 us  [local(): lax.all_to_all(mine, 'dp', 0, 0, tiled=True).astype(F32)]
  transfers between devices with their start and end apart: 24 -> 12, of which waited for: 6 -> 4; matrix products, arithmetic and copies ran while one was open for 0% -> 0% of each run, Pallas kernels for 0% -> 0%
where the time goes in v3:
time: 89.6 us; the launch traced here: 89.3 us
  blocking collectives  36.5 us (41%)
  Pallas kernels  18 us (20%)
  waiting for transfers between devices  16.8 us (19%)
  starting transfers between devices  16.4 us (18%)
    all_to_all x1, blocking collectives, local(): lax.all_to_all(mine, 'dp', 0, 0, tiled=True).astype(F32)  16 us
    pallas_call x1, Pallas kernels, run_layers(): pl.pallas_call(functools.partial(layers_kernel, scale, betas, layout), in...  16 us
    ppermute x4, waiting for transfers between devices, ring(): return lax.ppermute(v, 'dom', [(i, (i + 2 * step) % 8) for i in range(8)])  15.6 us
    all_to_all x1, blocking collectives, local(): mine = lax.all_to_all(mine, 'dom', 0, 0, tiled=True)  12 us
    all_to_all x1, blocking collectives, local(): parts = lax.all_to_all(parts, 'phase', 0, 0, tiled=True)  8.47 us
    ppermute x4, starting transfers between devices, ring(): return lax.ppermute(v, 'dom', [(i, (i + 2 * step) % 8) for i in range(8)])  6.96 us
    ppermute x5, starting transfers between devices, other_core(): return lax.ppermute(v, 'dom', [(i, i ^ 1) for i in range(8)])  5.67 us
    ppermute x3, starting transfers between devices, phase_weights(): lax.ppermute(w, 'phase', [(i, (i + n) % 4) for i in range(4)])  3.79 us
  transfers between devices with their start and end apart: 12, of which 4 were waited for; matrix products, arithmetic and copies ran while one was open for 0% of the time, Pallas kernels for 0%

profile of v3, /device:TPU:1, one launch (start us, length us, event | category | flops | bytes accessed | tf_op | source)
XLA Modules:
  0.0 89.3 jit_solution(16922832711333927898)
XLA Ops:
  0.6 0.0 copy-start
  0.6 2.0 %pack.1.refs_0_ = bf16[2320,128]{1,0:T(8,128)(2,1)S(1)} custom-call(bf16[4,10,128,128]{3,2,1,0:T(8,128)(2,1)} %bitcast.2, bf16[4,256,256]{2,1,0:T(8,128)(2,1)} %initial.1, bf16[4,256,256]{2,1,0:T(8,128)(2,1)} %cotangent.1, s32[4,2,5]{2,1,0:T(2,128)} %cols.1), custom_call_target="tpu_custom_call" | custom-call | tf_op jit(solution)/shard_map/pack/pallas_call | solution.py:60
  2.7 3.4 %collective-permute-start.4 = (bf16[2320,128]{1,0:T(8,128)(2,1)S(1)}, bf16[2320,128]{1,0:T(8,128)(2,1)S(1)}, u32[]{:S(2)}, u32[]{:S(2)}) collective-permute-start(bf16[2320,128]{1,0:T(8,128)(2,1)S(1)} %pack.1.refs_0_), channel_id=1, source_target_pairs={{0,6},{1,7},{2,0},{3,1},{4,2},{5,3},{6,4},{7,5},{8,14},{9,15},{10,... | collective-permute-start | bytes 1781768 | tf_op jit(solution)/shard_map/ppermute | solution.py:248
  6.1 0.0 collective-permute-start.1
  6.1 0.0 copy-done
  6.1 2.7 %collective-permute-start.11 = (bf16[1,256,256]{2,1,0:T(8,128)(2,1)S(1)}, bf16[1,256,256]{2,1,0:T(8,128)(2,1)S(1)}, u32[]{:S(2)}, u32[]{:S(2)}) collective-permute-start(bf16[1,256,256]{2,1,0:T(8,128)(2,1)S(1)} %copy-done), channel_id=1, source_target_pairs={{0,24},{8,0},{16,8},{24,16},{1,25},{9,1},{17,9},{25,17},{2,26},{10... | collective-permute-start | bytes 393224 | tf_op jit(solution)/shard_map/ppermute | solution.py:256
  8.8 0.3 collective-permute-start.10
  9.2 0.7 collective-permute-start.9
  9.9 8.3 %collective-permute-done.4.refs_8_ = bf16[2320,128]{1,0:T(8,128)(2,1)S(1)} collective-permute-done((bf16[2320,128]{1,0:T(8,128)(2,1)S(1)}, bf16[2320,128]{1,0:T(8,128)(2,1)S(1)}, u32[]{:S(2)}, u32[]{:S(2)}) %collective-permute-start.4) | collective-permute-done | bytes 593952 | tf_op jit(solution)/shard_map/ppermute | solution.py:248
  18.2 3.5 %collective-permute-start.5 = (bf16[1168,128]{1,0:T(8,128)(2,1)S(1)}, bf16[1168,128]{1,0:T(8,128)(2,1)S(1)}, u32[]{:S(2)}, u32[]{:S(2)}) collective-permute-start(bf16[1168,128]{1,0:T(8,128)(2,1)S(1)} %slice.9), channel_id=1, source_target_pairs={{0,6},{1,7},{2,0},{3,1},{4,2},{5,3},{6,4},{7,5},{8,14},{9,15},{10,... | collective-permute-start | bytes 897032 | tf_op jit(solution)/shard_map/ppermute | solution.py:248
  21.7 0.0 collective-permute-done.11.refs_13_
  21.7 1.8 %collective-permute-start = (bf16[2320,128]{1,0:T(8,128)(2,1)S(1)}, bf16[2320,128]{1,0:T(8,128)(2,1)S(1)}, u32[]{:S(2)}, u32[]{:S(2)}) collective-permute-start(bf16[2320,128]{1,0:T(8,128)(2,1)S(1)} %pack.1.refs_0_), channel_id=1, source_target_pairs={{0,1},{1,0},{2,3},{3,2},{4,5},{5,4},{6,7},{7,6},{8,9},{9,8},{10,11... | collective-permute-start | bytes 1781768 | tf_op jit(solution)/shard_map/ppermute | solution.py:252
  23.5 0.0 collective-permute-done.10.refs_12_
  23.5 0.1 collective-permute-start.8
  23.6 0.0 collective-permute-done.1.refs_2_
  23.6 0.4 collective-permute-start.2
  24.0 0.0 collective-permute-done.9.refs_11_
  24.0 0.1 collective-permute-start.3
  24.1 2.4 %collective-permute-done.5.refs_5_ = bf16[1168,128]{1,0:T(8,128)(2,1)S(1)} collective-permute-done((bf16[1168,128]{1,0:T(8,128)(2,1)S(1)}, bf16[1168,128]{1,0:T(8,128)(2,1)S(1)}, u32[]{:S(2)}, u32[]{:S(2)}) %collective-permute-start.5) | collective-permute-done | bytes 299040 | tf_op jit(solution)/shard_map/ppermute | solution.py:248
  26.5 2.5 %collective-permute-start.7 = (bf16[1168,128]{1,0:T(8,128)(2,1)S(1)}, bf16[1168,128]{1,0:T(8,128)(2,1)S(1)}, u32[]{:S(2)}, u32[]{:S(2)}) collective-permute-start(bf16[1168,128]{1,0:T(8,128)(2,1)S(1)} %collective-permute-done.5.refs_5_), channel_id=1, source_target_pairs={{0,1},{1,0},{2,3},{3,2},{4,5},{5,4},{6,7},{7,6},{8,9},{9,8},{10,11... | collective-permute-start | bytes 897032 | tf_op jit(solution)/shard_map/ppermute | solution.py:252
  29.0 4.9 %collective-permute-done.3.refs_4_ = bf16[1152,128]{1,0:T(8,128)(2,1)S(1)} collective-permute-done((bf16[1152,128]{1,0:T(8,128)(2,1)S(1)}, bf16[1152,128]{1,0:T(8,128)(2,1)S(1)}, u32[]{:S(2)}, u32[]{:S(2)}) %collective-permute-start.3) | collective-permute-done | bytes 294944 | tf_op jit(solution)/shard_map/ppermute | solution.py:248
  33.9 0.9 collective-permute-start.6
  34.8 0.0 collective-permute-done.refs_1_
  34.8 1.2 %collective-permute-done.6.refs_6_ = bf16[1152,128]{1,0:T(8,128)(2,1)S(1)} collective-permute-done((bf16[1152,128]{1,0:T(8,128)(2,1)S(1)}, bf16[1152,128]{1,0:T(8,128)(2,1)S(1)}, u32[]{:S(2)}, u32[]{:S(2)}) %collective-permute-start.6) | collective-permute-done | bytes 294944 | tf_op jit(solution)/shard_map/ppermute | solution.py:252
  36.0 0.0 collective-permute-done.8.refs_9_
  36.0 0.0 collective-permute-done.2.refs_3_
  36.0 0.0 collective-permute-done.7.refs_7_
  36.0 16.0 %layers.1 = (f32[1,256,256]{2,1,0:T(8,128)}, bf16[4,32,256]{2,1,0:T(8,128)(2,1)S(1)}) custom-call(bf16[2320,128]{1,0:T(8,128)(2,1)S(1)} %pack.1.refs_0_, bf16[2320,128]{1,0:T(8,128)(2,1)S(1)} %collective-permute-done.refs_1_, bf16[2320,128]{1,0:T(8,128)(2,1)S(1)} %collective-permute-done.1.refs_2_, bf16[2320,128]{1,0:T(8,128)(2,1)S(1)} %collective-permute-done.2.refs_3_, ...), custom_call_target="tpu_custom_call" | custom-call | flops 8999999488 | bytes 6000000 | tf_op jit(solution)/shard_map/layers/pallas_call | solution.py:221
  52.0 8.5 %all_to_all.15 = bf16[4,32,256]{2,1,0:T(8,128)(2,1)S(1)} all-to-all(bf16[4,32,256]{2,1,0:T(8,128)(2,1)S(1)} %get-tuple-element.7), channel_id=1, replica_groups=mesh['dp'=8,'phase'=4,'dom'=8] {'phase'}, dimensions={0} | all-to-all | bytes 131072 | tf_op jit(solution)/shard_map/all_to_all | solution.py:285
  60.5 16.0 %all_to_all.16 = bf16[8,32,256]{2,1,0:T(8,128)(2,1)S(1)} all-to-all(bf16[8,32,256]{2,1,0:T(8,128)(2,1)S(1)} %broadcast_in_dim.4), channel_id=1, replica_groups=mesh['dp'=8,'phase'=4,'dom'=8] {'dp'}, dimensions={0} | all-to-all | bytes 262144 | tf_op jit(solution)/shard_map/all_to_all | solution.py:288
  76.6 12.0 %all_to_all.17 = f32[8,32,256]{2,1,0:T(8,128)S(1)} all-to-all(f32[8,32,256]{2,1,0:T(8,128)S(1)} %broadcast_in_dim.5), channel_id=1, replica_groups=mesh['dp'=8,'phase'=4,'dom'=8] {'dom'}, dimensions={0} | all-to-all | bytes 524288 | tf_op jit(solution)/shard_map/all_to_all | solution.py:290
  88.6 0.7 copy.8
  (6 shorter events, 0.1 us)
Async XLA Ops:
  0.6 5.4 %copy-start = (bf16[1,256,256]{2,1,0:T(8,128)(2,1)S(1)}, bf16[1,256,256]{2,1,0:T(8,128)(2,1)}, u32[]{:S(2)}) copy-start(bf16[1,256,256]{2,1,0:T(8,128)(2,1)} %refs_10_) | copy-start | bytes 393220
  2.7 15.5 %collective-permute-start.4 = (bf16[2320,128]{1,0:T(8,128)(2,1)S(1)}, bf16[2320,128]{1,0:T(8,128)(2,1)S(1)}, u32[]{:S(2)}, u32[]{:S(2)}) collective-permute-start(bf16[2320,128]{1,0:T(8,128)(2,1)S(1)} %pack.1.refs_0_), channel_id=1, source_target_pairs={{0,6},{1,7},{2,0},{3,1},{4,2},{5,3},{6,4},{7,5},{8,14},{9,15},{10,... | collective-permute-start | bytes 1781768 | tf_op jit(solution)/shard_map/ppermute | solution.py:248
  6.1 17.5 %collective-permute-start.1 = (bf16[2320,128]{1,0:T(8,128)(2,1)S(1)}, bf16[2320,128]{1,0:T(8,128)(2,1)S(1)}, u32[]{:S(2)}, u32[]{:S(2)}) collective-permute-start(bf16[2320,128]{1,0:T(8,128)(2,1)S(1)} %pack.1.refs_0_), channel_id=1, source_target_pairs={{0,2},{1,3},{2,4},{3,5},{4,6},{5,7},{6,0},{7,1},{8,10},{9,11},{10,... | collective-permute-start | bytes 1781768 | tf_op jit(solution)/shard_map/ppermute | solution.py:248
  6.1 15.6 %collective-permute-start.11 = (bf16[1,256,256]{2,1,0:T(8,128)(2,1)S(1)}, bf16[1,256,256]{2,1,0:T(8,128)(2,1)S(1)}, u32[]{:S(2)}, u32[]{:S(2)}) collective-permute-start(bf16[1,256,256]{2,1,0:T(8,128)(2,1)S(1)} %copy-done), channel_id=1, source_target_pairs={{0,24},{8,0},{16,8},{24,16},{1,25},{9,1},{17,9},{25,17},{2,26},{10... | collective-permute-start | bytes 393224 | tf_op jit(solution)/shard_map/ppermute | solution.py:256
  8.8 14.7 %collective-permute-start.10 = (bf16[1,256,256]{2,1,0:T(8,128)(2,1)S(1)}, bf16[1,256,256]{2,1,0:T(8,128)(2,1)S(1)}, u32[]{:S(2)}, u32[]{:S(2)}) collective-permute-start(bf16[1,256,256]{2,1,0:T(8,128)(2,1)S(1)} %copy-done), channel_id=1, source_target_pairs={{0,16},{8,24},{16,0},{24,8},{1,17},{9,25},{17,1},{25,9},{2,18},{10... | collective-permute-start | bytes 393224 | tf_op jit(solution)/shard_map/ppermute | solution.py:256
  9.2 14.9 %collective-permute-start.9 = (bf16[1,256,256]{2,1,0:T(8,128)(2,1)S(1)}, bf16[1,256,256]{2,1,0:T(8,128)(2,1)S(1)}, u32[]{:S(2)}, u32[]{:S(2)}) collective-permute-start(bf16[1,256,256]{2,1,0:T(8,128)(2,1)S(1)} %copy-done), channel_id=1, source_target_pairs={{0,8},{8,16},{16,24},{24,0},{1,9},{9,17},{17,25},{25,1},{2,10},{10... | collective-permute-start | bytes 393224 | tf_op jit(solution)/shard_map/ppermute | solution.py:256
  18.2 8.3 %collective-permute-start.5 = (bf16[1168,128]{1,0:T(8,128)(2,1)S(1)}, bf16[1168,128]{1,0:T(8,128)(2,1)S(1)}, u32[]{:S(2)}, u32[]{:S(2)}) collective-permute-start(bf16[1168,128]{1,0:T(8,128)(2,1)S(1)} %slice.9), channel_id=1, source_target_pairs={{0,6},{1,7},{2,0},{3,1},{4,2},{5,3},{6,4},{7,5},{8,14},{9,15},{10,... | collective-permute-start | bytes 897032 | tf_op jit(solution)/shard_map/ppermute | solution.py:248
  21.7 13.1 %collective-permute-start = (bf16[2320,128]{1,0:T(8,128)(2,1)S(1)}, bf16[2320,128]{1,0:T(8,128)(2,1)S(1)}, u32[]{:S(2)}, u32[]{:S(2)}) collective-permute-start(bf16[2320,128]{1,0:T(8,128)(2,1)S(1)} %pack.1.refs_0_), channel_id=1, source_target_pairs={{0,1},{1,0},{2,3},{3,2},{4,5},{5,4},{6,7},{7,6},{8,9},{9,8},{10,11... | collective-permute-start | bytes 1781768 | tf_op jit(solution)/shard_map/ppermute | solution.py:252
  23.5 12.5 %collective-permute-start.8 = (bf16[2320,128]{1,0:T(8,128)(2,1)S(1)}, bf16[2320,128]{1,0:T(8,128)(2,1)S(1)}, u32[]{:S(2)}, u32[]{:S(2)}) collective-permute-start(bf16[2320,128]{1,0:T(8,128)(2,1)S(1)} %collective-permute-done.4.refs_8_), channel_id=1, source_target_pairs={{0,1},{1,0},{2,3},{3,2},{4,5},{5,4},{6,7},{7,6},{8,9},{9,8},{10,11... | collective-permute-start | bytes 1781768 | tf_op jit(solution)/shard_map/ppermute | solution.py:252
  23.6 12.4 %collective-permute-start.2 = (bf16[2320,128]{1,0:T(8,128)(2,1)S(1)}, bf16[2320,128]{1,0:T(8,128)(2,1)S(1)}, u32[]{:S(2)}, u32[]{:S(2)}) collective-permute-start(bf16[2320,128]{1,0:T(8,128)(2,1)S(1)} %collective-permute-done.1.refs_2_), channel_id=1, source_target_pairs={{0,1},{1,0},{2,3},{3,2},{4,5},{5,4},{6,7},{7,6},{8,9},{9,8},{10,11... | collective-permute-start | bytes 1781768 | tf_op jit(solution)/shard_map/ppermute | solution.py:252
  24.0 9.9 %collective-permute-start.3 = (bf16[1152,128]{1,0:T(8,128)(2,1)S(1)}, bf16[1152,128]{1,0:T(8,128)(2,1)S(1)}, u32[]{:S(2)}, u32[]{:S(2)}) collective-permute-start(bf16[1152,128]{1,0:T(8,128)(2,1)S(1)} %slice.8), channel_id=1, source_target_pairs={{0,2},{1,3},{2,4},{3,5},{4,6},{5,7},{6,0},{7,1},{8,10},{9,11},{10,... | collective-permute-start | bytes 884744 | tf_op jit(solution)/shard_map/ppermute | solution.py:248
  26.5 9.5 %collective-permute-start.7 = (bf16[1168,128]{1,0:T(8,128)(2,1)S(1)}, bf16[1168,128]{1,0:T(8,128)(2,1)S(1)}, u32[]{:S(2)}, u32[]{:S(2)}) collective-permute-start(bf16[1168,128]{1,0:T(8,128)(2,1)S(1)} %collective-permute-done.5.refs_5_), channel_id=1, source_target_pairs={{0,1},{1,0},{2,3},{3,2},{4,5},{5,4},{6,7},{7,6},{8,9},{9,8},{10,11... | collective-permute-start | bytes 897032 | tf_op jit(solution)/shard_map/ppermute | solution.py:252
  33.9 2.1 %collective-permute-start.6 = (bf16[1152,128]{1,0:T(8,128)(2,1)S(1)}, bf16[1152,128]{1,0:T(8,128)(2,1)S(1)}, u32[]{:S(2)}, u32[]{:S(2)}) collective-permute-start(bf16[1152,128]{1,0:T(8,128)(2,1)S(1)} %collective-permute-done.3.refs_4_), channel_id=1, source_target_pairs={{0,1},{1,0},{2,3},{3,2},{4,5},{5,4},{6,7},{7,6},{8,9},{9,8},{10,11... | collective-permute-start | bytes 884744 | tf_op jit(solution)/shard_map/ppermute | solution.py:252

commit v4 on v3

--- a/solution.py
+++ b/solution.py
@@ -16,7 +16,6 @@
 GELU_B = 0.044715
 ROWS = 2 * BLK
 TILE_ROWS = 2 * NZB * BLK
-CUT = 9 * BLK
 START = TILE_ROWS
 COT = START + 2 * ROWS
 COLS = COT + 2 * ROWS
@@ -75,33 +74,24 @@
     return lax.dot_general(a, b, (dims, ((), ())), preferred_element_type=F32)
 
 
-def layers_kernel(scale, betas, layout, *refs):
-    count = sum(len(p) for p in layout)
-    inputs, weights = list(refs[:count]), refs[count : count + len(betas)]
-    grad_initial, grad_weights = refs[count + len(betas) : count + len(betas) + 2]
-    scratch = refs[count + len(betas) + 2 :]
-    start, weight, cols_int, cols, hidden, mixes, slopes, dpre, dw, sem = scratch
-    pieces = []
-    for parts in layout:
-        spots = []
-        for low, high in parts:
-            spots.append((low, high, inputs.pop(0)))
-        pieces.append(spots)
+def layers_kernel(scale, betas, *refs):
+    layers = len(betas)
+    pieces, weights = refs[:8], refs[8 : 8 + layers]
+    grad_initial, grad_weights = refs[8 + layers : 10 + layers]
+    start, weight, cols_int, cols, hidden, mixes, slopes, dpre, dw, sem = refs[10 + layers :]
 
     def piece(n, low, rows):
-        for first, last, ref in pieces[n]:
-            if first <= low < last:
-                return ref[low - first : low - first + rows, :]
+        return pieces[n][low : low + rows, :]
 
     dom = lax.axis_index("dom")
     phase = lax.axis_index("phase")
     x, core = dom // 2, dom % 2
-    layers = len(weights)
     for n in range(layers):
         weight[(phase - n + layers) % layers] = weights[n][0]
+    way = 1 - 2 * core
     for n in range(8):
         j = piece(n, COLS, 16).astype(F32).astype(jnp.int32)
-        chip = lax.bitwise_and(x - lax.shift_right_logical(j, 2) + 4, 3)
+        chip = lax.bitwise_and(way * (x - lax.shift_right_logical(j, 2)) + 4, 3)
         side = lax.bitwise_xor(lax.bitwise_and(lax.shift_right_logical(j, 1), 1), core)
         place = chip * 4 + side * 2 + lax.bitwise_and(j, 1)
         cols_int[n : n + 1, :] = (place * BLK)[:1]
@@ -215,12 +205,10 @@
 
 def run_layers(scale, betas, pieces, weights):
     vmem = pl.BlockSpec(memory_space=pltpu.VMEM)
-    layout = [[(low, high) for low, high, _ in parts] for parts in pieces]
-    arrays = [a for parts in pieces for _, _, a in parts]
     nodes, width = 2048, 256
     return pl.pallas_call(
-        functools.partial(layers_kernel, scale, betas, layout),
-        in_specs=[vmem] * (len(arrays) + len(weights)),
+        functools.partial(layers_kernel, scale, betas),
+        in_specs=[vmem] * (len(pieces) + len(weights)),
         out_specs=[vmem, vmem],
         out_shape=[
             jax.ShapeDtypeStruct((1, 256, width), F32),
@@ -241,11 +229,12 @@
         compiler_params=pltpu.CompilerParams(vmem_limit_bytes=40 * 1024 * 1024),
         cost_estimate=pl.CostEstimate(flops=9_000_000_000, bytes_accessed=6_000_000, transcendentals=0),
         name="layers",
-    )(*arrays, *weights)
-
-
-def ring(v, step):
-    return lax.ppermute(v, "dom", [(i, (i + 2 * step) % 8) for i in range(8)])
+    )(*pieces, *weights)
+
+
+def onward(v):
+    route = [(i, (i + 2) % 8 if i % 2 == 0 else (i - 2) % 8) for i in range(8)]
+    return lax.ppermute(v, "dom", route)
 
 
 def other_core(v):
@@ -256,19 +245,18 @@
     return [w] + [lax.ppermute(w, "phase", [(i, (i + n) % 4) for i in range(4)]) for n in (1, 2, 3)]
 
 
-def whole(v):
-    return [(0, PIECE, v)]
-
-
-def gather_halves(own, w):
-    left, right = ring(own, 1), ring(own, -1)
-    w, _ = lax.optimization_barrier((w, own))
+def across(v):
+    route = [(i, (i + 2) % 8 - 1 if i % 2 else (i - 2) % 8 + 1) for i in range(8)]
+    return lax.ppermute(v, "dom", route)
+
+
+def gather(own, w):
+    near, near_too = onward(own), across(own)
+    partner = other_core(own)
     weights = phase_weights(w)
-    top, low = ring(left[:CUT], 1), ring(right[CUT:], -1)
-    pieces = [whole(own), whole(other_core(own)), whole(left), whole(other_core(left))]
-    pieces.append([(0, CUT, top), (CUT, PIECE, low)])
-    pieces.append([(0, CUT, other_core(top)), (CUT, PIECE, other_core(low))])
-    pieces += [whole(right), whole(other_core(right))]
+    early, *weights = lax.optimization_barrier((near, *weights))
+    far = onward(early)
+    pieces = [own, partner, near, near_too, far, other_core(far), other_core(near_too), other_core(near)]
     return pieces, weights
 
 
@@ -280,7 +268,7 @@
     spans, rows = block_tiles.shape[:2]
     tiles = block_tiles.reshape(spans, rows * NZB, BLK, BLK)
     own = pack(tiles, initial, cotangent, block_cols)
-    pieces, weights = gather_halves(own, layer_weights)
+    pieces, weights = gather(own, layer_weights)
     grad_initial, parts = run_layers(scale, betas, pieces, weights)
     parts = lax.all_to_all(parts, "phase", 0, 0, tiled=True)
     mine = jnp.sum(parts.astype(F32), axis=0).astype(BF16)

time: 89.6 us -> 84.4 us (0.942)
  waiting for transfers between devices: 16.8 us -> 13.7 us
  starting transfers between devices: 16.4 us -> 15.1 us
    ppermute x4 -> x3, waiting for transfers between devices: 15.6 us -> 9.28 us  [the longest x1 5.95 us: across(): return lax.ppermute(v, 'dom', route)]
    ppermute x3, waiting for transfers between devices: 0.01 us -> 2.8 us  [phase_weights(): lax.ppermute(w, 'phase', [(i, (i + n) % 4) for i in range(4)])]
    ppermute x5 -> x4, starting transfers between devices: 5.67 us -> 3.64 us  [other_core(): return lax.ppermute(v, 'dom', [(i, i ^ 1) for i in range(8)])]
    ppermute x3, starting transfers between devices: 3.79 us -> 5.6 us  [phase_weights(): lax.ppermute(w, 'phase', [(i, (i + n) % 4) for i in range(4)])]
    ppermute x4 -> x3, starting transfers between devices: 6.96 us -> 5.86 us  [the longest x2 4.24 us: onward(): return lax.ppermute(v, 'dom', route)]
  transfers between devices with their start and end apart: 12 -> 10, of which waited for: 4 -> 5; matrix products, arithmetic and copies ran while one was open for 0% -> 0% of each run, Pallas kernels for 0% -> 0%
where the time goes in v4:
time: 84.4 us; the launch traced here: 84.2 us
  blocking collectives  35.9 us (43%)
  Pallas kernels  18.1 us (21%)
  starting transfers between devices  15.1 us (18%)
  waiting for transfers between devices  13.7 us (16%)
    pallas_call x1, Pallas kernels, run_layers(): pl.pallas_call(functools.partial(layers_kernel, scale, betas), in_specs=[...  16 us
    all_to_all x1, blocking collectives, local(): lax.all_to_all(mine, 'dp', 0, 0, tiled=True).astype(F32)  16 us
    all_to_all x1, blocking collectives, local(): mine = lax.all_to_all(mine, 'dom', 0, 0, tiled=True)  12.1 us
    all_to_all x1, blocking collectives, local(): parts = lax.all_to_all(parts, 'phase', 0, 0, tiled=True)  7.79 us
    ppermute x1, waiting for transfers between devices, across(): return lax.ppermute(v, 'dom', route)  5.95 us
    ppermute x3, starting transfers between devices, phase_weights(): lax.ppermute(w, 'phase', [(i, (i + n) % 4) for i in range(4)])  5.6 us
    ppermute x2, starting transfers between devices, onward(): return lax.ppermute(v, 'dom', route)  4.24 us
    ppermute x4, starting transfers between devices, other_core(): return lax.ppermute(v, 'dom', [(i, i ^ 1) for i in range(8)])  3.64 us
  transfers between devices with their start and end apart: 10, of which 5 were waited for; matrix products, arithmetic and copies ran while one was open for 0% of the time, Pallas kernels for 0%

profile of v4, /device:TPU:1, one launch (start us, length us, event | category | flops | bytes accessed | tf_op | source)
XLA Modules:
  0.0 84.2 jit_solution(11452378828288886154)
XLA Ops:
  0.6 0.0 copy-start
  0.6 2.0 %pack.1.refs_0_ = bf16[2320,128]{1,0:T(8,128)(2,1)S(1)} custom-call(bf16[4,10,128,128]{3,2,1,0:T(8,128)(2,1)} %bitcast.2, bf16[4,256,256]{2,1,0:T(8,128)(2,1)} %initial.1, bf16[4,256,256]{2,1,0:T(8,128)(2,1)} %cotangent.1, s32[4,2,5]{2,1,0:T(2,128)} %cols.1), custom_call_target="tpu_custom_call" | custom-call | tf_op jit(solution)/shard_map/pack/pallas_call | solution.py:59
  2.7 3.4 %collective-permute-start.1 = (bf16[2320,128]{1,0:T(8,128)(2,1)S(1)}, bf16[2320,128]{1,0:T(8,128)(2,1)S(1)}, u32[]{:S(2)}, u32[]{:S(2)}) collective-permute-start(bf16[2320,128]{1,0:T(8,128)(2,1)S(1)} %pack.1.refs_0_), channel_id=1, source_target_pairs={{0,2},{1,7},{2,4},{3,1},{4,6},{5,3},{6,0},{7,5},{8,10},{9,15},{10,... | collective-permute-start | bytes 1781768 | tf_op jit(solution)/shard_map/ppermute | solution.py:237
  6.1 0.0 copy-done
  6.1 2.9 %collective-permute-start.4 = (bf16[1,256,256]{2,1,0:T(8,128)(2,1)S(1)}, bf16[1,256,256]{2,1,0:T(8,128)(2,1)S(1)}, u32[]{:S(2)}, u32[]{:S(2)}) collective-permute-start(bf16[1,256,256]{2,1,0:T(8,128)(2,1)S(1)} %copy-done), channel_id=1, source_target_pairs={{0,16},{8,24},{16,0},{24,8},{1,17},{9,25},{17,1},{25,9},{2,18},{10... | collective-permute-start | bytes 393224 | tf_op jit(solution)/shard_map/ppermute | solution.py:245
  9.0 0.4 collective-permute-start.3
  9.4 2.3 %collective-permute-start.5 = (bf16[1,256,256]{2,1,0:T(8,128)(2,1)S(1)}, bf16[1,256,256]{2,1,0:T(8,128)(2,1)S(1)}, u32[]{:S(2)}, u32[]{:S(2)}) collective-permute-start(bf16[1,256,256]{2,1,0:T(8,128)(2,1)S(1)} %copy-done), channel_id=1, source_target_pairs={{0,24},{8,0},{16,8},{24,16},{1,25},{9,1},{17,9},{25,17},{2,26},{10... | collective-permute-start | bytes 393224 | tf_op jit(solution)/shard_map/ppermute | solution.py:245
  11.7 1.6 %collective-permute-start.2 = (bf16[2320,128]{1,0:T(8,128)(2,1)S(1)}, bf16[2320,128]{1,0:T(8,128)(2,1)S(1)}, u32[]{:S(2)}, u32[]{:S(2)}) collective-permute-start(bf16[2320,128]{1,0:T(8,128)(2,1)S(1)} %pack.1.refs_0_), channel_id=1, source_target_pairs={{0,7},{1,2},{2,1},{3,4},{4,3},{5,6},{6,5},{7,0},{8,15},{9,10},{10,... | collective-permute-start | bytes 1781768 | tf_op jit(solution)/shard_map/ppermute | solution.py:250
  13.3 0.0 collective-permute-done.4.refs_10_
  13.3 2.5 %collective-permute-done.3.refs_9_ = bf16[1,256,256]{2,1,0:T(8,128)(2,1)S(1)} collective-permute-done((bf16[1,256,256]{2,1,0:T(8,128)(2,1)S(1)}, bf16[1,256,256]{2,1,0:T(8,128)(2,1)S(1)}, u32[]{:S(2)}, u32[]{:S(2)}) %collective-permute-start.3) | collective-permute-done | bytes 131104 | tf_op jit(solution)/shard_map/ppermute | solution.py:245
  15.8 0.3 collective-permute-done.5.refs_11_
  16.1 0.0 collective-permute-done.1.refs_2_
  16.1 0.9 %collective-permute-start.6 = (bf16[2320,128]{1,0:T(8,128)(2,1)S(1)}, bf16[2320,128]{1,0:T(8,128)(2,1)S(1)}, u32[]{:S(2)}, u32[]{:S(2)}) collective-permute-start(bf16[2320,128]{1,0:T(8,128)(2,1)S(1)} %collective-permute-done.1.refs_2_), channel_id=1, source_target_pairs={{0,2},{1,7},{2,4},{3,1},{4,6},{5,3},{6,0},{7,5},{8,10},{9,15},{10,... | collective-permute-start | bytes 1781768 | tf_op jit(solution)/shard_map/ppermute | solution.py:237
  16.9 0.9 %collective-permute-start = (bf16[2320,128]{1,0:T(8,128)(2,1)S(1)}, bf16[2320,128]{1,0:T(8,128)(2,1)S(1)}, u32[]{:S(2)}, u32[]{:S(2)}) collective-permute-start(bf16[2320,128]{1,0:T(8,128)(2,1)S(1)} %pack.1.refs_0_), channel_id=1, source_target_pairs={{0,1},{1,0},{2,3},{3,2},{4,5},{5,4},{6,7},{7,6},{8,9},{9,8},{10,11... | collective-permute-start | bytes 1781768 | tf_op jit(solution)/shard_map/ppermute | solution.py:241
  17.8 0.0 collective-permute-start.9
  17.8 5.9 %collective-permute-done.2.refs_3_ = bf16[2320,128]{1,0:T(8,128)(2,1)S(1)} collective-permute-done((bf16[2320,128]{1,0:T(8,128)(2,1)S(1)}, bf16[2320,128]{1,0:T(8,128)(2,1)S(1)}, u32[]{:S(2)}, u32[]{:S(2)}) %collective-permute-start.2) | collective-permute-done | bytes 593952 | tf_op jit(solution)/shard_map/ppermute | solution.py:250
  23.8 0.6 collective-permute-start.8
  24.4 3.3 %collective-permute-done.6.refs_4_ = bf16[2320,128]{1,0:T(8,128)(2,1)S(1)} collective-permute-done((bf16[2320,128]{1,0:T(8,128)(2,1)S(1)}, bf16[2320,128]{1,0:T(8,128)(2,1)S(1)}, u32[]{:S(2)}, u32[]{:S(2)}) %collective-permute-start.6) | collective-permute-done | bytes 593952 | tf_op jit(solution)/shard_map/ppermute | solution.py:237
  27.7 2.2 %collective-permute-start.7 = (bf16[2320,128]{1,0:T(8,128)(2,1)S(1)}, bf16[2320,128]{1,0:T(8,128)(2,1)S(1)}, u32[]{:S(2)}, u32[]{:S(2)}) collective-permute-start(bf16[2320,128]{1,0:T(8,128)(2,1)S(1)} %collective-permute-done.6.refs_4_), channel_id=1, source_target_pairs={{0,1},{1,0},{2,3},{3,2},{4,5},{5,4},{6,7},{7,6},{8,9},{9,8},{10,11... | collective-permute-start | bytes 1781768 | tf_op jit(solution)/shard_map/ppermute | solution.py:241
  29.9 0.0 collective-permute-done.refs_1_
  29.9 0.0 collective-permute-done.8.refs_6_
  29.9 0.0 collective-permute-done.9.refs_7_
  29.9 1.6 %collective-permute-done.7.refs_5_ = bf16[2320,128]{1,0:T(8,128)(2,1)S(1)} collective-permute-done((bf16[2320,128]{1,0:T(8,128)(2,1)S(1)}, bf16[2320,128]{1,0:T(8,128)(2,1)S(1)}, u32[]{:S(2)}, u32[]{:S(2)}) %collective-permute-start.7) | collective-permute-done | bytes 593952 | tf_op jit(solution)/shard_map/ppermute | solution.py:241
  31.5 16.0 %layers.1 = (f32[1,256,256]{2,1,0:T(8,128)}, bf16[4,32,256]{2,1,0:T(8,128)(2,1)S(1)}) custom-call(bf16[2320,128]{1,0:T(8,128)(2,1)S(1)} %pack.1.refs_0_, bf16[2320,128]{1,0:T(8,128)(2,1)S(1)} %collective-permute-done.refs_1_, bf16[2320,128]{1,0:T(8,128)(2,1)S(1)} %collective-permute-done.1.refs_2_, bf16[2320,128]{1,0:T(8,128)(2,1)S(1)} %collective-permute-done.2.refs_3_, ...), custom_call_target="tpu_custom_call" | custom-call | flops 8999999488 | bytes 6000000 | tf_op jit(solution)/shard_map/layers/pallas_call | solution.py:209
  47.5 7.8 %all_to_all.15 = bf16[4,32,256]{2,1,0:T(8,128)(2,1)S(1)} all-to-all(bf16[4,32,256]{2,1,0:T(8,128)(2,1)S(1)} %get-tuple-element.15), channel_id=1, replica_groups=mesh['dp'=8,'phase'=4,'dom'=8] {'phase'}, dimensions={0} | all-to-all | bytes 131072 | tf_op jit(solution)/shard_map/all_to_all | solution.py:273
  55.4 16.0 %all_to_all.16 = bf16[8,32,256]{2,1,0:T(8,128)(2,1)S(1)} all-to-all(bf16[8,32,256]{2,1,0:T(8,128)(2,1)S(1)} %broadcast_in_dim.4), channel_id=1, replica_groups=mesh['dp'=8,'phase'=4,'dom'=8] {'dp'}, dimensions={0} | all-to-all | bytes 262144 | tf_op jit(solution)/shard_map/all_to_all | solution.py:276
  71.4 12.1 %all_to_all.17 = f32[8,32,256]{2,1,0:T(8,128)S(1)} all-to-all(f32[8,32,256]{2,1,0:T(8,128)S(1)} %broadcast_in_dim.5), channel_id=1, replica_groups=mesh['dp'=8,'phase'=4,'dom'=8] {'dom'}, dimensions={0} | all-to-all | bytes 524288 | tf_op jit(solution)/shard_map/all_to_all | solution.py:278
  83.5 0.7 copy.8
  (4 shorter events, 0.1 us)
Async XLA Ops:
  0.6 5.4 %copy-start = (bf16[1,256,256]{2,1,0:T(8,128)(2,1)S(1)}, bf16[1,256,256]{2,1,0:T(8,128)(2,1)}, u32[]{:S(2)}) copy-start(bf16[1,256,256]{2,1,0:T(8,128)(2,1)} %refs_8_) | copy-start | bytes 393220
  2.7 13.4 %collective-permute-start.1 = (bf16[2320,128]{1,0:T(8,128)(2,1)S(1)}, bf16[2320,128]{1,0:T(8,128)(2,1)S(1)}, u32[]{:S(2)}, u32[]{:S(2)}) collective-permute-start(bf16[2320,128]{1,0:T(8,128)(2,1)S(1)} %pack.1.refs_0_), channel_id=1, source_target_pairs={{0,2},{1,7},{2,4},{3,1},{4,6},{5,3},{6,0},{7,5},{8,10},{9,15},{10,... | collective-permute-start | bytes 1781768 | tf_op jit(solution)/shard_map/ppermute | solution.py:237
  6.1 7.2 %collective-permute-start.4 = (bf16[1,256,256]{2,1,0:T(8,128)(2,1)S(1)}, bf16[1,256,256]{2,1,0:T(8,128)(2,1)S(1)}, u32[]{:S(2)}, u32[]{:S(2)}) collective-permute-start(bf16[1,256,256]{2,1,0:T(8,128)(2,1)S(1)} %copy-done), channel_id=1, source_target_pairs={{0,16},{8,24},{16,0},{24,8},{1,17},{9,25},{17,1},{25,9},{2,18},{10... | collective-permute-start | bytes 393224 | tf_op jit(solution)/shard_map/ppermute | solution.py:245
  9.0 6.8 %collective-permute-start.3 = (bf16[1,256,256]{2,1,0:T(8,128)(2,1)S(1)}, bf16[1,256,256]{2,1,0:T(8,128)(2,1)S(1)}, u32[]{:S(2)}, u32[]{:S(2)}) collective-permute-start(bf16[1,256,256]{2,1,0:T(8,128)(2,1)S(1)} %copy-done), channel_id=1, source_target_pairs={{0,8},{8,16},{16,24},{24,0},{1,9},{9,17},{17,25},{25,1},{2,10},{10... | collective-permute-start | bytes 393224 | tf_op jit(solution)/shard_map/ppermute | solution.py:245
  9.4 6.7 %collective-permute-start.5 = (bf16[1,256,256]{2,1,0:T(8,128)(2,1)S(1)}, bf16[1,256,256]{2,1,0:T(8,128)(2,1)S(1)}, u32[]{:S(2)}, u32[]{:S(2)}) collective-permute-start(bf16[1,256,256]{2,1,0:T(8,128)(2,1)S(1)} %copy-done), channel_id=1, source_target_pairs={{0,24},{8,0},{16,8},{24,16},{1,25},{9,1},{17,9},{25,17},{2,26},{10... | collective-permute-start | bytes 393224 | tf_op jit(solution)/shard_map/ppermute | solution.py:245
  11.7 12.1 %collective-permute-start.2 = (bf16[2320,128]{1,0:T(8,128)(2,1)S(1)}, bf16[2320,128]{1,0:T(8,128)(2,1)S(1)}, u32[]{:S(2)}, u32[]{:S(2)}) collective-permute-start(bf16[2320,128]{1,0:T(8,128)(2,1)S(1)} %pack.1.refs_0_), channel_id=1, source_target_pairs={{0,7},{1,2},{2,1},{3,4},{4,3},{5,6},{6,5},{7,0},{8,15},{9,10},{10,... | collective-permute-start | bytes 1781768 | tf_op jit(solution)/shard_map/ppermute | solution.py:250
  16.1 11.6 %collective-permute-start.6 = (bf16[2320,128]{1,0:T(8,128)(2,1)S(1)}, bf16[2320,128]{1,0:T(8,128)(2,1)S(1)}, u32[]{:S(2)}, u32[]{:S(2)}) collective-permute-start(bf16[2320,128]{1,0:T(8,128)(2,1)S(1)} %collective-permute-done.1.refs_2_), channel_id=1, source_target_pairs={{0,2},{1,7},{2,4},{3,1},{4,6},{5,3},{6,0},{7,5},{8,10},{9,15},{10,... | collective-permute-start | bytes 1781768 | tf_op jit(solution)/shard_map/ppermute | solution.py:237
  16.9 12.9 %collective-permute-start = (bf16[2320,128]{1,0:T(8,128)(2,1)S(1)}, bf16[2320,128]{1,0:T(8,128)(2,1)S(1)}, u32[]{:S(2)}, u32[]{:S(2)}) collective-permute-start(bf16[2320,128]{1,0:T(8,128)(2,1)S(1)} %pack.1.refs_0_), channel_id=1, source_target_pairs={{0,1},{1,0},{2,3},{3,2},{4,5},{5,4},{6,7},{7,6},{8,9},{9,8},{10,11... | collective-permute-start | bytes 1781768 | tf_op jit(solution)/shard_map/ppermute | solution.py:241
  17.8 12.1 %collective-permute-start.9 = (bf16[2320,128]{1,0:T(8,128)(2,1)S(1)}, bf16[2320,128]{1,0:T(8,128)(2,1)S(1)}, u32[]{:S(2)}, u32[]{:S(2)}) collective-permute-start(bf16[2320,128]{1,0:T(8,128)(2,1)S(1)} %collective-permute-done.1.refs_2_), channel_id=1, source_target_pairs={{0,1},{1,0},{2,3},{3,2},{4,5},{5,4},{6,7},{7,6},{8,9},{9,8},{10,11... | collective-permute-start | bytes 1781768 | tf_op jit(solution)/shard_map/ppermute | solution.py:241
  23.8 6.1 %collective-permute-start.8 = (bf16[2320,128]{1,0:T(8,128)(2,1)S(1)}, bf16[2320,128]{1,0:T(8,128)(2,1)S(1)}, u32[]{:S(2)}, u32[]{:S(2)}) collective-permute-start(bf16[2320,128]{1,0:T(8,128)(2,1)S(1)} %collective-permute-done.2.refs_3_), channel_id=1, source_target_pairs={{0,1},{1,0},{2,3},{3,2},{4,5},{5,4},{6,7},{7,6},{8,9},{9,8},{10,11... | collective-permute-start | bytes 1781768 | tf_op jit(solution)/shard_map/ppermute | solution.py:241
  27.7 3.8 %collective-permute-start.7 = (bf16[2320,128]{1,0:T(8,128)(2,1)S(1)}, bf16[2320,128]{1,0:T(8,128)(2,1)S(1)}, u32[]{:S(2)}, u32[]{:S(2)}) collective-permute-start(bf16[2320,128]{1,0:T(8,128)(2,1)S(1)} %collective-permute-done.6.refs_4_), channel_id=1, source_target_pairs={{0,1},{1,0},{2,3},{3,2},{4,5},{5,4},{6,7},{7,6},{8,9},{9,8},{10,11... | collective-permute-start | bytes 1781768 | tf_op jit(solution)/shard_map/ppermute | solution.py:241

commit v5 on v4

--- a/solution.py
+++ b/solution.py
@@ -35,9 +35,11 @@
 
 def pack_kernel(tiles, initial, cotangent, cols, piece, start, cot, sems):
     span = lax.axis_index("phase")
-    copies = [(initial.at[span], start), (cotangent.at[span], cot)]
-    for t in range(2 * NZB):
-        copies.append((tiles.at[span, t], piece.at[pl.ds(t * BLK, BLK)]))
+    copies = [
+        (initial.at[span], start),
+        (cotangent.at[span], cot),
+        (tiles.at[span], piece.at[pl.ds(0, TILE_ROWS)]),
+    ]
     started = [pltpu.make_async_copy(a, b, sems.at[n]) for n, (a, b) in enumerate(copies)]
     for c in started:
         c.start()
@@ -47,11 +49,11 @@
         for k in range(NZB):
             vec = jnp.where(lane == b * NZB + k, cols[span, b, k].astype(F32), vec)
     piece[COLS : COLS + 16, :] = vec.astype(BF16)
-    for c in started:
-        c.wait()
-    for base, array in ((START, start), (COT, cot)):
+    for copy, base, array in ((started[0], START, start), (started[1], COT, cot)):
+        copy.wait()
         piece[base : base + ROWS, :] = array[:, :BLK]
         piece[base + ROWS : base + 2 * ROWS, :] = array[:, BLK:]
+    started[2].wait()
 
 
 def pack(tiles, initial, cotangent, cols):
@@ -64,7 +66,7 @@
         scratch_shapes=[
             pltpu.VMEM((ROWS, 2 * BLK), BF16),
             pltpu.VMEM((ROWS, 2 * BLK), BF16),
-            pltpu.SemaphoreType.DMA((2 + 2 * NZB,)),
+            pltpu.SemaphoreType.DMA((3,)),
         ],
         name="pack",
     )(*[pltpu.with_memory_space_constraint(a, pltpu.HBM) for a in (tiles, initial, cotangent)], cols)
@@ -78,7 +80,9 @@
     layers = len(betas)
     pieces, weights = refs[:8], refs[8 : 8 + layers]
     grad_initial, grad_weights = refs[8 + layers : 10 + layers]
-    start, weight, cols_int, cols, hidden, mixes, slopes, dpre, dw, sem = refs[10 + layers :]
+    start, weight, cols_int, cols, h_even, h_odd, mixes, slopes, dpre, dw, sem = refs[10 + layers :]
+
+    hidden = (h_even, h_odd)
 
     def piece(n, low, rows):
         return pieces[n][low : low + rows, :]
@@ -101,7 +105,7 @@
         for half in range(2):
             part = piece(n, START + ROWS * half, ROWS)
             lanes = slice(BLK * half, BLK * (half + 1))
-            hidden[0, ROWS * n : ROWS * (n + 1), lanes] = part
+            h_even[ROWS * n : ROWS * (n + 1), lanes] = part
             start[ROWS * n : ROWS * (n + 1), lanes] = ALPHA * part.astype(F32)
     to_scalars.wait()
 
@@ -109,10 +113,10 @@
         return piece(i // 2, ((i % 2) * NZB + k) * BLK, BLK)
 
     def aggregate(src, i):
-        blocks = [hidden[src, i * BLK : (i + 1) * BLK, :]]
+        blocks = [hidden[src][i * BLK : (i + 1) * BLK, :]]
         for k in range(1, NZB):
             j = pl.multiple_of(cols[i // 2, (i % 2) * NZB + k], BLK)
-            blocks.append(hidden[src, pl.ds(j, BLK), :])
+            blocks.append(hidden[src][pl.ds(j, BLK), :])
         lhs = jnp.concatenate([tile(i, k) for k in range(NZB)], axis=1)
         return (1.0 - ALPHA) * dot(lhs, jnp.concatenate(blocks, axis=0), ((1,), (0,)))
 
@@ -131,13 +135,15 @@
                 third(i, product[(i % CHUNK) * BLK : (i % CHUNK + 1) * BLK, :])
 
     def pick(values, l):
+        if isinstance(l, int):
+            return values[l]
         out = jnp.float32(values[0])
         for n in range(1, len(values)):
             out = jnp.where(l == n, jnp.float32(values[n]), out)
         return out
 
-    def forward(l, _):
-        src, dst = l % 2, (l + 1) % 2
+    def forward(l, src):
+        dst = 1 - src
         beta = pick(betas, l)
         w = weight[l]
 
@@ -155,7 +161,7 @@
             t = jnp.tanh(pre * (GELU_C + (GELU_C * GELU_B) * square))
             half = 0.5 + 0.5 * t
             out = pre * half
-            hidden[dst, rows, :] = out.astype(BF16)
+            hidden[dst][rows, :] = out.astype(BF16)
             slopes[l, rows, :] = half + out * (1.0 - half) * (
                 2.0 * GELU_C + (6.0 * GELU_C * GELU_B) * square
             )
@@ -163,9 +169,9 @@
         pipeline(first, second, third)
         return 0
 
-    def backward(step, _, top=False):
+    def backward(step, src, top=False):
         l = layers - 1 - step
-        src, dst = step % 2, (step + 1) % 2
+        dst = 1 - src
         beta = pick(betas, l)
         w = weight[l]
 
@@ -184,19 +190,30 @@
         def third(i, product):
             rows = slice(i * BLK, (i + 1) * BLK)
             dmix = (1.0 - beta) * dpre[rows, :].astype(F32) + beta * product
-            hidden[dst, rows, :] = dmix.astype(BF16)
+            hidden[dst][rows, :] = dmix.astype(BF16)
 
         pipeline(first, second, third)
-        term = ALPHA * hidden[dst, 0:256, :].astype(F32)
+        term = ALPHA * hidden[dst][0:256, :].astype(F32)
         grad_initial[0] = term if top else grad_initial[0] + term
-        lanes = pl.ds(pl.multiple_of(dom // 4 * BLK, BLK), BLK)
+        lanes = pl.ds(pl.multiple_of(core * BLK, BLK), BLK)
         dw[...] = (beta * scale) * dot(mixes[l, :, lanes], dpre[...], ((0,), (0,)))
-        grad_weights[l] = dw[pl.ds(pl.multiple_of(dom % 4 * 32, 32), 32), :].astype(BF16)
+        grad_weights[l] = dw[pl.ds(pl.multiple_of(x % 2 * 64, 64), 64), :].astype(BF16)
         return 0
 
-    lax.fori_loop(0, layers, forward, 0)
+    def two_forward(m, _):
+        forward(2 * m, 0)
+        forward(2 * m + 1, 1)
+        return 0
+
+    def two_backward(m, _):
+        backward(2 * m, 0)
+        backward(2 * m + 1, 1)
+        return 0
+
+    lax.fori_loop(0, layers // 2, two_forward, 0)
     backward(0, 0, top=True)
-    lax.fori_loop(1, layers, backward, 0)
+    backward(1, 1)
+    lax.fori_loop(1, layers // 2, two_backward, 0)
     for b in range(2):
         rows = slice(b * BLK, (b + 1) * BLK)
         back = aggregate(layers % 2, b).astype(BF16)
@@ -212,14 +229,15 @@
         out_specs=[vmem, vmem],
         out_shape=[
             jax.ShapeDtypeStruct((1, 256, width), F32),
-            jax.ShapeDtypeStruct((4, 32, width), BF16),
+            jax.ShapeDtypeStruct((4, 64, width), BF16),
         ],
         scratch_shapes=[
             pltpu.VMEM((nodes, width), F32),
             pltpu.VMEM((4, width, width), BF16),
             pltpu.VMEM((8, BLK), jnp.int32),
             pltpu.SMEM((8, BLK), jnp.int32),
-            pltpu.VMEM((2, nodes, width), BF16),
+            pltpu.VMEM((nodes, width), BF16),
+            pltpu.VMEM((nodes, width), BF16),
             pltpu.VMEM((4, nodes, width), BF16),
             pltpu.VMEM((4, nodes, width), F32),
             pltpu.VMEM((nodes, width), BF16),
@@ -266,7 +284,7 @@
     scale = 1.0 / math.sqrt(nodes_all)
     betas = [math.log(THETA / (l + 1) + 1.0) for l in range(layers)]
     spans, rows = block_tiles.shape[:2]
-    tiles = block_tiles.reshape(spans, rows * NZB, BLK, BLK)
+    tiles = block_tiles.reshape(spans, rows * NZB * BLK, BLK)
     own = pack(tiles, initial, cotangent, block_cols)
     pieces, weights = gather(own, layer_weights)
     grad_initial, parts = run_layers(scale, betas, pieces, weights)
@@ -274,8 +292,12 @@
     mine = jnp.sum(parts.astype(F32), axis=0).astype(BF16)
     mine = jnp.broadcast_to(mine[None], (8,) + mine.shape)
     mine = jnp.sum(lax.all_to_all(mine, "dp", 0, 0, tiled=True).astype(F32), axis=0)
-    mine = jnp.broadcast_to(mine[None], (8,) + mine.shape)
-    mine = lax.all_to_all(mine, "dom", 0, 0, tiled=True)
+    dom = lax.axis_index("dom")
+    for bit in (2, 1):
+        other = lax.ppermute(mine, "dom", [(i, i ^ bit) for i in range(8)])
+        odd = lax.bitwise_and(dom, bit) != 0
+        both = jnp.stack([jnp.where(odd, other, mine), jnp.where(odd, mine, other)])
+        mine = both.reshape(-1, both.shape[-1])
     return grad_initial, mine.reshape(1, 256, 256)
 
 

time: 84.4 us -> 82 us (0.972)
  blocking collectives: 35.9 us -> 25.1 us
  starting transfers between devices: 15.1 us -> 21.3 us
  waiting for transfers between devices: 13.7 us -> 16.6 us
    all_to_all x1 -> x0, blocking collectives: 12.1 us -> none  [local(): mine = lax.all_to_all(mine, 'dom', 0, 0, tiled=True)]
    ppermute x0 -> x2, starting transfers between devices: none -> 4.97 us  [local(): other = lax.ppermute(mine, 'dom', [(i, i ^ bit) for i in range(8)])]
    ppermute x0 -> x2, waiting for transfers between devices: none -> 4.08 us  [local(): other = lax.ppermute(mine, 'dom', [(i, i ^ bit) for i in range(8)])]
    ppermute x4, starting transfers between devices: 3.64 us -> 6.32 us  [other_core(): return lax.ppermute(v, 'dom', [(i, i ^ 1) for i in range(8)])]
    ppermute x1, waiting for transfers between devices: 5.95 us -> 3.49 us  [across(): return lax.ppermute(v, 'dom', route)]
    ppermute x3, waiting for transfers between devices: 2.8 us -> 4.02 us  [phase_weights(): lax.ppermute(w, 'phase', [(i, (i + n) % 4) for i in range(4)])]
    all_to_all x1, blocking collectives: 16 us -> 17.2 us  [local(): lax.all_to_all(mine, 'dp', 0, 0, tiled=True).astype(F32)]
    ppermute x2, starting transfers between devices: 4.24 us -> 3.39 us  [onward(): return lax.ppermute(v, 'dom', route)]
  transfers between devices with their start and end apart: 10 -> 12, of which waited for: 5 -> 6; matrix products, arithmetic and copies ran while one was open for 0% -> 0% of each run, Pallas kernels for 0% -> 0%
where the time goes in v5:
time: 82 us; the launch traced here: 81.8 us
  blocking collectives  25.1 us (31%)
  starting transfers between devices  21.3 us (26%)
  Pallas kernels  17.4 us (21%)
  waiting for transfers between devices  16.6 us (20%)
    all_to_all x1, blocking collectives, local(): lax.all_to_all(mine, 'dp', 0, 0, tiled=True).astype(F32)  17.2 us
    pallas_call x1, Pallas kernels, run_layers(): pl.pallas_call(functools.partial(layers_kernel, scale, betas), in_specs=[...  15.4 us
    all_to_all x1, blocking collectives, local(): parts = lax.all_to_all(parts, 'phase', 0, 0, tiled=True)  7.85 us
    ppermute x4, starting transfers between devices, other_core(): return lax.ppermute(v, 'dom', [(i, i ^ 1) for i in range(8)])  6.32 us
    ppermute x3, starting transfers between devices, phase_weights(): lax.ppermute(w, 'phase', [(i, (i + n) % 4) for i in range(4)])  4.99 us
    ppermute x2, starting transfers between devices, local(): other = lax.ppermute(mine, 'dom', [(i, i ^ bit) for i in range(8)])  4.97 us
    ppermute x2, waiting for transfers between devices, local(): other = lax.ppermute(mine, 'dom', [(i, i ^ bit) for i in range(8)])  4.08 us
    ppermute x3, waiting for transfers between devices, phase_weights(): lax.ppermute(w, 'phase', [(i, (i + n) % 4) for i in range(4)])  4.02 us
  transfers between devices with their start and end apart: 12, of which 6 were waited for; matrix products, arithmetic and copies ran while one was open for 0% of the time, Pallas kernels for 0%

profile of v5, /device:TPU:1, one launch (start us, length us, event | category | flops | bytes accessed | tf_op | source)
XLA Modules:
  0.0 81.8 jit_solution(17266139623318593723)
XLA Ops:
  0.6 0.0 copy-start
  0.6 2.0 %pack.1.refs_0_ = bf16[2320,128]{1,0:T(8,128)(2,1)S(1)} custom-call(bf16[4,1280,128]{2,1,0:T(8,128)(2,1)} %bitcast.13, bf16[4,256,256]{2,1,0:T(8,128)(2,1)} %initial.1, bf16[4,256,256]{2,1,0:T(8,128)(2,1)} %cotangent.1, s32[4,2,5]{2,1,0:T(2,128)} %cols.1), custom_call_target="tpu_custom_call" | custom-call | tf_op jit(solution)/shard_map/pack/pallas_call | solution.py:61
  2.6 3.4 %collective-permute-start.1 = (bf16[2320,128]{1,0:T(8,128)(2,1)S(1)}, bf16[2320,128]{1,0:T(8,128)(2,1)S(1)}, u32[]{:S(2)}, u32[]{:S(2)}) collective-permute-start(bf16[2320,128]{1,0:T(8,128)(2,1)S(1)} %pack.1.refs_0_), channel_id=1, source_target_pairs={{0,2},{1,7},{2,4},{3,1},{4,6},{5,3},{6,0},{7,5},{8,10},{9,15},{10,... | collective-permute-start | bytes 1781768 | tf_op jit(solution)/shard_map/ppermute | solution.py:255
  6.0 0.0 copy-done
  6.0 1.3 %collective-permute-start.3 = (bf16[1,256,256]{2,1,0:T(8,128)(2,1)S(1)}, bf16[1,256,256]{2,1,0:T(8,128)(2,1)S(1)}, u32[]{:S(2)}, u32[]{:S(2)}) collective-permute-start(bf16[1,256,256]{2,1,0:T(8,128)(2,1)S(1)} %copy-done), channel_id=1, source_target_pairs={{0,8},{8,16},{16,24},{24,0},{1,9},{9,17},{17,25},{25,1},{2,10},{10... | collective-permute-start | bytes 393224 | tf_op jit(solution)/shard_map/ppermute | solution.py:263
  7.3 2.6 %collective-permute-start.4 = (bf16[1,256,256]{2,1,0:T(8,128)(2,1)S(1)}, bf16[1,256,256]{2,1,0:T(8,128)(2,1)S(1)}, u32[]{:S(2)}, u32[]{:S(2)}) collective-permute-start(bf16[1,256,256]{2,1,0:T(8,128)(2,1)S(1)} %copy-done), channel_id=1, source_target_pairs={{0,16},{8,24},{16,0},{24,8},{1,17},{9,25},{17,1},{25,9},{2,18},{10... | collective-permute-start | bytes 393224 | tf_op jit(solution)/shard_map/ppermute | solution.py:263
  10.0 1.1 %collective-permute-start.5 = (bf16[1,256,256]{2,1,0:T(8,128)(2,1)S(1)}, bf16[1,256,256]{2,1,0:T(8,128)(2,1)S(1)}, u32[]{:S(2)}, u32[]{:S(2)}) collective-permute-start(bf16[1,256,256]{2,1,0:T(8,128)(2,1)S(1)} %copy-done), channel_id=1, source_target_pairs={{0,24},{8,0},{16,8},{24,16},{1,25},{9,1},{17,9},{25,17},{2,26},{10... | collective-permute-start | bytes 393224 | tf_op jit(solution)/shard_map/ppermute | solution.py:263
  11.0 1.6 %collective-permute-start.2 = (bf16[2320,128]{1,0:T(8,128)(2,1)S(1)}, bf16[2320,128]{1,0:T(8,128)(2,1)S(1)}, u32[]{:S(2)}, u32[]{:S(2)}) collective-permute-start(bf16[2320,128]{1,0:T(8,128)(2,1)S(1)} %pack.1.refs_0_), channel_id=1, source_target_pairs={{0,7},{1,2},{2,1},{3,4},{4,3},{5,6},{6,5},{7,0},{8,15},{9,10},{10,... | collective-permute-start | bytes 1781768 | tf_op jit(solution)/shard_map/ppermute | solution.py:268
  12.6 0.0 collective-permute-done.3.refs_9_
  12.6 4.0 %collective-permute-done.4.refs_10_ = bf16[1,256,256]{2,1,0:T(8,128)(2,1)S(1)} collective-permute-done((bf16[1,256,256]{2,1,0:T(8,128)(2,1)S(1)}, bf16[1,256,256]{2,1,0:T(8,128)(2,1)S(1)}, u32[]{:S(2)}, u32[]{:S(2)}) %collective-permute-start.4) | collective-permute-done | bytes 131104 | tf_op jit(solution)/shard_map/ppermute | solution.py:263
  16.7 0.0 collective-permute-done.5.refs_11_
  16.7 0.0 collective-permute-done.1.refs_2_
  16.7 0.0 collective-permute-start.6
  16.7 1.7 %collective-permute-start = (bf16[2320,128]{1,0:T(8,128)(2,1)S(1)}, bf16[2320,128]{1,0:T(8,128)(2,1)S(1)}, u32[]{:S(2)}, u32[]{:S(2)}) collective-permute-start(bf16[2320,128]{1,0:T(8,128)(2,1)S(1)} %pack.1.refs_0_), channel_id=1, source_target_pairs={{0,1},{1,0},{2,3},{3,2},{4,5},{5,4},{6,7},{7,6},{8,9},{9,8},{10,11... | collective-permute-start | bytes 1781768 | tf_op jit(solution)/shard_map/ppermute | solution.py:259
  18.4 0.0 collective-permute-start.9
  18.4 3.5 %collective-permute-done.2.refs_3_ = bf16[2320,128]{1,0:T(8,128)(2,1)S(1)} collective-permute-done((bf16[2320,128]{1,0:T(8,128)(2,1)S(1)}, bf16[2320,128]{1,0:T(8,128)(2,1)S(1)}, u32[]{:S(2)}, u32[]{:S(2)}) %collective-permute-start.2) | collective-permute-done | bytes 593952 | tf_op jit(solution)/shard_map/ppermute | solution.py:268
  21.9 1.8 %collective-permute-start.8 = (bf16[2320,128]{1,0:T(8,128)(2,1)S(1)}, bf16[2320,128]{1,0:T(8,128)(2,1)S(1)}, u32[]{:S(2)}, u32[]{:S(2)}) collective-permute-start(bf16[2320,128]{1,0:T(8,128)(2,1)S(1)} %collective-permute-done.2.refs_3_), channel_id=1, source_target_pairs={{0,1},{1,0},{2,3},{3,2},{4,5},{5,4},{6,7},{7,6},{8,9},{9,8},{10,11... | collective-permute-start | bytes 1781768 | tf_op jit(solution)/shard_map/ppermute | solution.py:259
  23.7 3.3 %collective-permute-done.6.refs_4_ = bf16[2320,128]{1,0:T(8,128)(2,1)S(1)} collective-permute-done((bf16[2320,128]{1,0:T(8,128)(2,1)S(1)}, bf16[2320,128]{1,0:T(8,128)(2,1)S(1)}, u32[]{:S(2)}, u32[]{:S(2)}) %collective-permute-start.6) | collective-permute-done | bytes 593952 | tf_op jit(solution)/shard_map/ppermute | solution.py:255
  27.0 2.8 %collective-permute-start.7 = (bf16[2320,128]{1,0:T(8,128)(2,1)S(1)}, bf16[2320,128]{1,0:T(8,128)(2,1)S(1)}, u32[]{:S(2)}, u32[]{:S(2)}) collective-permute-start(bf16[2320,128]{1,0:T(8,128)(2,1)S(1)} %collective-permute-done.6.refs_4_), channel_id=1, source_target_pairs={{0,1},{1,0},{2,3},{3,2},{4,5},{5,4},{6,7},{7,6},{8,9},{9,8},{10,11... | collective-permute-start | bytes 1781768 | tf_op jit(solution)/shard_map/ppermute | solution.py:259
  29.8 0.0 collective-permute-done.refs_1_
  29.8 0.0 collective-permute-done.9.refs_7_
  29.8 0.0 collective-permute-done.8.refs_6_
  29.8 1.6 %collective-permute-done.7.refs_5_ = bf16[2320,128]{1,0:T(8,128)(2,1)S(1)} collective-permute-done((bf16[2320,128]{1,0:T(8,128)(2,1)S(1)}, bf16[2320,128]{1,0:T(8,128)(2,1)S(1)}, u32[]{:S(2)}, u32[]{:S(2)}) %collective-permute-start.7) | collective-permute-done | bytes 593952 | tf_op jit(solution)/shard_map/ppermute | solution.py:259
  31.5 15.4 %layers.1 = (f32[1,256,256]{2,1,0:T(8,128)}, bf16[4,64,256]{2,1,0:T(8,128)(2,1)S(1)}) custom-call(bf16[2320,128]{1,0:T(8,128)(2,1)S(1)} %pack.1.refs_0_, bf16[2320,128]{1,0:T(8,128)(2,1)S(1)} %collective-permute-done.refs_1_, bf16[2320,128]{1,0:T(8,128)(2,1)S(1)} %collective-permute-done.1.refs_2_, bf16[2320,128]{1,0:T(8,128)(2,1)S(1)} %collective-permute-done.2.refs_3_, ...), custom_call_target="tpu_custom_call" | custom-call | flops 8999999488 | bytes 6000000 | tf_op jit(solution)/shard_map/layers/pallas_call | solution.py:226
  46.8 7.9 %all_to_all.10 = bf16[4,64,256]{2,1,0:T(8,128)(2,1)S(1)} all-to-all(bf16[4,64,256]{2,1,0:T(8,128)(2,1)S(1)} %get-tuple-element.15), channel_id=1, replica_groups=mesh['dp'=8,'phase'=4,'dom'=8] {'phase'}, dimensions={0} | all-to-all | bytes 262144 | tf_op jit(solution)/shard_map/all_to_all | solution.py:291
  54.7 17.2 %all_to_all.11 = bf16[8,64,256]{2,1,0:T(8,128)(2,1)S(1)} all-to-all(bf16[8,64,256]{2,1,0:T(8,128)(2,1)S(1)} %broadcast_in_dim.2), channel_id=1, replica_groups=mesh['dp'=8,'phase'=4,'dom'=8] {'dp'}, dimensions={0} | all-to-all | bytes 524288 | tf_op jit(solution)/shard_map/all_to_all | solution.py:294
  72.0 0.1 collective-permute-start.10
  72.1 3.1 %collective-permute-done.10 = f32[64,256]{1,0:T(8,128)S(1)} collective-permute-done((f32[64,256]{1,0:T(8,128)S(1)}, f32[64,256]{1,0:T(8,128)S(1)}, u32[]{:S(2)}, u32[]{:S(2)}) %collective-permute-start.10) | collective-permute-done | bytes 65568 | tf_op jit(solution)/shard_map/ppermute | solution.py:297
  75.2 4.9 %collective-permute-start.11 = (f32[128,256]{1,0:T(8,128)S(1)}, f32[128,256]{1,0:T(8,128)S(1)}, u32[]{:S(2)}, u32[]{:S(2)}) collective-permute-start(f32[128,256]{1,0:T(8,128)S(1)} %bitcast.14), channel_id=1, source_target_pairs={{0,1},{1,0},{2,3},{3,2},{4,5},{5,4},{6,7},{7,6},{8,9},{9,8},{10,11... | collective-permute-start | bytes 393224 | tf_op jit(solution)/shard_map/ppermute | solution.py:297
  80.1 1.0 %collective-permute-done.11 = f32[128,256]{1,0:T(8,128)S(1)} collective-permute-done((f32[128,256]{1,0:T(8,128)S(1)}, f32[128,256]{1,0:T(8,128)S(1)}, u32[]{:S(2)}, u32[]{:S(2)}) %collective-permute-start.11) | collective-permute-done | bytes 131104 | tf_op jit(solution)/shard_map/ppermute | solution.py:297
  81.1 0.7 pad_maximum_fusion
  (6 shorter events, 0.1 us)
Async XLA Ops:
  0.6 5.4 %copy-start = (bf16[1,256,256]{2,1,0:T(8,128)(2,1)S(1)}, bf16[1,256,256]{2,1,0:T(8,128)(2,1)}, u32[]{:S(2)}) copy-start(bf16[1,256,256]{2,1,0:T(8,128)(2,1)} %refs_8_) | copy-start | bytes 393220
  2.6 14.0 %collective-permute-start.1 = (bf16[2320,128]{1,0:T(8,128)(2,1)S(1)}, bf16[2320,128]{1,0:T(8,128)(2,1)S(1)}, u32[]{:S(2)}, u32[]{:S(2)}) collective-permute-start(bf16[2320,128]{1,0:T(8,128)(2,1)S(1)} %pack.1.refs_0_), channel_id=1, source_target_pairs={{0,2},{1,7},{2,4},{3,1},{4,6},{5,3},{6,0},{7,5},{8,10},{9,15},{10,... | collective-permute-start | bytes 1781768 | tf_op jit(solution)/shard_map/ppermute | solution.py:255
  6.0 6.6 %collective-permute-start.3 = (bf16[1,256,256]{2,1,0:T(8,128)(2,1)S(1)}, bf16[1,256,256]{2,1,0:T(8,128)(2,1)S(1)}, u32[]{:S(2)}, u32[]{:S(2)}) collective-permute-start(bf16[1,256,256]{2,1,0:T(8,128)(2,1)S(1)} %copy-done), channel_id=1, source_target_pairs={{0,8},{8,16},{16,24},{24,0},{1,9},{9,17},{17,25},{25,1},{2,10},{10... | collective-permute-start | bytes 393224 | tf_op jit(solution)/shard_map/ppermute | solution.py:263
  7.3 9.3 %collective-permute-start.4 = (bf16[1,256,256]{2,1,0:T(8,128)(2,1)S(1)}, bf16[1,256,256]{2,1,0:T(8,128)(2,1)S(1)}, u32[]{:S(2)}, u32[]{:S(2)}) collective-permute-start(bf16[1,256,256]{2,1,0:T(8,128)(2,1)S(1)} %copy-done), channel_id=1, source_target_pairs={{0,16},{8,24},{16,0},{24,8},{1,17},{9,25},{17,1},{25,9},{2,18},{10... | collective-permute-start | bytes 393224 | tf_op jit(solution)/shard_map/ppermute | solution.py:263
  10.0 6.7 %collective-permute-start.5 = (bf16[1,256,256]{2,1,0:T(8,128)(2,1)S(1)}, bf16[1,256,256]{2,1,0:T(8,128)(2,1)S(1)}, u32[]{:S(2)}, u32[]{:S(2)}) collective-permute-start(bf16[1,256,256]{2,1,0:T(8,128)(2,1)S(1)} %copy-done), channel_id=1, source_target_pairs={{0,24},{8,0},{16,8},{24,16},{1,25},{9,1},{17,9},{25,17},{2,26},{10... | collective-permute-start | bytes 393224 | tf_op jit(solution)/shard_map/ppermute | solution.py:263
  11.0 10.9 %collective-permute-start.2 = (bf16[2320,128]{1,0:T(8,128)(2,1)S(1)}, bf16[2320,128]{1,0:T(8,128)(2,1)S(1)}, u32[]{:S(2)}, u32[]{:S(2)}) collective-permute-start(bf16[2320,128]{1,0:T(8,128)(2,1)S(1)} %pack.1.refs_0_), channel_id=1, source_target_pairs={{0,7},{1,2},{2,1},{3,4},{4,3},{5,6},{6,5},{7,0},{8,15},{9,10},{10,... | collective-permute-start | bytes 1781768 | tf_op jit(solution)/shard_map/ppermute | solution.py:268
  16.7 10.4 %collective-permute-start.6 = (bf16[2320,128]{1,0:T(8,128)(2,1)S(1)}, bf16[2320,128]{1,0:T(8,128)(2,1)S(1)}, u32[]{:S(2)}, u32[]{:S(2)}) collective-permute-start(bf16[2320,128]{1,0:T(8,128)(2,1)S(1)} %collective-permute-done.1.refs_2_), channel_id=1, source_target_pairs={{0,2},{1,7},{2,4},{3,1},{4,6},{5,3},{6,0},{7,5},{8,10},{9,15},{10,... | collective-permute-start | bytes 1781768 | tf_op jit(solution)/shard_map/ppermute | solution.py:255
  16.7 13.2 %collective-permute-start = (bf16[2320,128]{1,0:T(8,128)(2,1)S(1)}, bf16[2320,128]{1,0:T(8,128)(2,1)S(1)}, u32[]{:S(2)}, u32[]{:S(2)}) collective-permute-start(bf16[2320,128]{1,0:T(8,128)(2,1)S(1)} %pack.1.refs_0_), channel_id=1, source_target_pairs={{0,1},{1,0},{2,3},{3,2},{4,5},{5,4},{6,7},{7,6},{8,9},{9,8},{10,11... | collective-permute-start | bytes 1781768 | tf_op jit(solution)/shard_map/ppermute | solution.py:259
  18.4 11.4 %collective-permute-start.9 = (bf16[2320,128]{1,0:T(8,128)(2,1)S(1)}, bf16[2320,128]{1,0:T(8,128)(2,1)S(1)}, u32[]{:S(2)}, u32[]{:S(2)}) collective-permute-start(bf16[2320,128]{1,0:T(8,128)(2,1)S(1)} %collective-permute-done.1.refs_2_), channel_id=1, source_target_pairs={{0,1},{1,0},{2,3},{3,2},{4,5},{5,4},{6,7},{7,6},{8,9},{9,8},{10,11... | collective-permute-start | bytes 1781768 | tf_op jit(solution)/shard_map/ppermute | solution.py:259
  21.9 8.0 %collective-permute-start.8 = (bf16[2320,128]{1,0:T(8,128)(2,1)S(1)}, bf16[2320,128]{1,0:T(8,128)(2,1)S(1)}, u32[]{:S(2)}, u32[]{:S(2)}) collective-permute-start(bf16[2320,128]{1,0:T(8,128)(2,1)S(1)} %collective-permute-done.2.refs_3_), channel_id=1, source_target_pairs={{0,1},{1,0},{2,3},{3,2},{4,5},{5,4},{6,7},{7,6},{8,9},{9,8},{10,11... | collective-permute-start | bytes 1781768 | tf_op jit(solution)/shard_map/ppermute | solution.py:259
  27.0 4.4 %collective-permute-start.7 = (bf16[2320,128]{1,0:T(8,128)(2,1)S(1)}, bf16[2320,128]{1,0:T(8,128)(2,1)S(1)}, u32[]{:S(2)}, u32[]{:S(2)}) collective-permute-start(bf16[2320,128]{1,0:T(8,128)(2,1)S(1)} %collective-permute-done.6.refs_4_), channel_id=1, source_target_pairs={{0,1},{1,0},{2,3},{3,2},{4,5},{5,4},{6,7},{7,6},{8,9},{9,8},{10,11... | collective-permute-start | bytes 1781768 | tf_op jit(solution)/shard_map/ppermute | solution.py:259
  72.0 3.2 %collective-permute-start.10 = (f32[64,256]{1,0:T(8,128)S(1)}, f32[64,256]{1,0:T(8,128)S(1)}, u32[]{:S(2)}, u32[]{:S(2)}) collective-permute-start(f32[64,256]{1,0:T(8,128)S(1)} %convert_reduce_fusion), channel_id=1, source_target_pairs={{0,2},{1,3},{2,0},{3,1},{4,6},{5,7},{6,4},{7,5},{8,10},{9,11},{10,... | collective-permute-start | bytes 196616 | tf_op jit(solution)/shard_map/ppermute | solution.py:297
  75.2 5.9 %collective-permute-start.11 = (f32[128,256]{1,0:T(8,128)S(1)}, f32[128,256]{1,0:T(8,128)S(1)}, u32[]{:S(2)}, u32[]{:S(2)}) collective-permute-start(f32[128,256]{1,0:T(8,128)S(1)} %bitcast.14), channel_id=1, source_target_pairs={{0,1},{1,0},{2,3},{3,2},{4,5},{5,4},{6,7},{7,6},{8,9},{9,8},{10,11... | collective-permute-start | bytes 393224 | tf_op jit(solution)/shard_map/ppermute | solution.py:297

commit v6 on v5

--- a/solution.py
+++ b/solution.py
@@ -197,7 +197,7 @@
         grad_initial[0] = term if top else grad_initial[0] + term
         lanes = pl.ds(pl.multiple_of(core * BLK, BLK), BLK)
         dw[...] = (beta * scale) * dot(mixes[l, :, lanes], dpre[...], ((0,), (0,)))
-        grad_weights[l] = dw[pl.ds(pl.multiple_of(x % 2 * 64, 64), 64), :].astype(BF16)
+        grad_weights[(l - phase + layers) % layers] = dw[pl.ds(pl.multiple_of(x % 2 * 64, 64), 64), :].astype(BF16)
         return 0
 
     def two_forward(m, _):
@@ -259,8 +259,8 @@
     return lax.ppermute(v, "dom", [(i, i ^ 1) for i in range(8)])
 
 
-def phase_weights(w):
-    return [w] + [lax.ppermute(w, "phase", [(i, (i + n) % 4) for i in range(4)]) for n in (1, 2, 3)]
+def to_phase(v, n):
+    return lax.ppermute(v, "phase", [(i, (i + n) % 4) for i in range(4)])
 
 
 def across(v):
@@ -271,7 +271,7 @@
 def gather(own, w):
     near, near_too = onward(own), across(own)
     partner = other_core(own)
-    weights = phase_weights(w)
+    weights = [w] + [to_phase(w, n) for n in (1, 2, 3)]
     early, *weights = lax.optimization_barrier((near, *weights))
     far = onward(early)
     pieces = [own, partner, near, near_too, far, other_core(far), other_core(near_too), other_core(near)]
@@ -288,8 +288,10 @@
     own = pack(tiles, initial, cotangent, block_cols)
     pieces, weights = gather(own, layer_weights)
     grad_initial, parts = run_layers(scale, betas, pieces, weights)
-    parts = lax.all_to_all(parts, "phase", 0, 0, tiled=True)
-    mine = jnp.sum(parts.astype(F32), axis=0).astype(BF16)
+    mine = parts[0].astype(F32)
+    for n in (1, 2, 3):
+        mine = mine + to_phase(parts[n], n).astype(F32)
+    mine = mine.astype(BF16)
     mine = jnp.broadcast_to(mine[None], (8,) + mine.shape)
     mine = jnp.sum(lax.all_to_all(mine, "dp", 0, 0, tiled=True).astype(F32), axis=0)
     dom = lax.axis_index("dom")

time: 82 us -> 80.1 us (0.977)
  blocking collectives: 25.1 us -> 17.3 us
  starting transfers between devices: 21.3 us -> 24.8 us
  waiting for transfers between devices: 16.6 us -> 18.8 us
    all_to_all x1 -> x0, blocking collectives: 7.85 us -> none  [local(): parts = lax.all_to_all(parts, 'phase', 0, 0, tiled=True)]
    ppermute x3 -> x6, starting transfers between devices: 4.99 us -> 8.78 us  [to_phase(): return lax.ppermute(v, 'phase', [(i, (i + n) % 4) for i in range(4)])]
    ppermute x3 -> x6, waiting for transfers between devices: 4.02 us -> 6.27 us  [to_phase(): return lax.ppermute(v, 'phase', [(i, (i + n) % 4) for i in range(4)])]
  transfers between devices with their start and end apart: 12 -> 15, of which waited for: 6 -> 9; matrix products, arithmetic and copies ran while one was open for 0% -> 0% of each run, Pallas kernels for 0% -> 0%
where the time goes in v6:
time: 80.1 us; the launch traced here: 80 us
  starting transfers between devices  24.8 us (31%)
  waiting for transfers between devices  18.8 us (23%)
  Pallas kernels  17.4 us (22%)
  blocking collectives  17.3 us (22%)
  other arithmetic  0.82 us (1%)
    all_to_all x1, blocking collectives, local(): lax.all_to_all(mine, 'dp', 0, 0, tiled=True).astype(F32)  17.3 us
    pallas_call x1, Pallas kernels, run_layers(): pl.pallas_call(functools.partial(layers_kernel, scale, betas), in_specs=[...  15.4 us
    ppermute x6, starting transfers between devices, to_phase(): return lax.ppermute(v, 'phase', [(i, (i + n) % 4) for i in range(4)])  8.78 us
    ppermute x4, starting transfers between devices, other_core(): return lax.ppermute(v, 'dom', [(i, i ^ 1) for i in range(8)])  6.32 us
    ppermute x6, waiting for transfers between devices, to_phase(): return lax.ppermute(v, 'phase', [(i, (i + n) % 4) for i in range(4)])  6.27 us
    ppermute x2, starting transfers between devices, local(): other = lax.ppermute(mine, 'dom', [(i, i ^ bit) for i in range(8)])  4.73 us
    ppermute x2, waiting for transfers between devices, local(): other = lax.ppermute(mine, 'dom', [(i, i ^ bit) for i in range(8)])  4.08 us
    ppermute x1, waiting for transfers between devices, across(): return lax.ppermute(v, 'dom', route)  3.49 us
  transfers between devices with their start and end apart: 15, of which 9 were waited for; matrix products, arithmetic and copies ran while one was open for 0% of the time, Pallas kernels for 0%

profile of v6, /device:TPU:1, one launch (start us, length us, event | category | flops | bytes accessed | tf_op | source)
XLA Modules:
  0.0 80.0 jit_solution(11004114878362862491)
XLA Ops:
  0.6 0.0 copy-start
  0.6 2.0 %pack.1.refs_0_ = bf16[2320,128]{1,0:T(8,128)(2,1)S(1)} custom-call(bf16[4,1280,128]{2,1,0:T(8,128)(2,1)} %bitcast.22, bf16[4,256,256]{2,1,0:T(8,128)(2,1)} %initial.1, bf16[4,256,256]{2,1,0:T(8,128)(2,1)} %cotangent.1, s32[4,2,5]{2,1,0:T(2,128)} %cols.1), custom_call_target="tpu_custom_call" | custom-call | tf_op jit(solution)/shard_map/pack/pallas_call | solution.py:61
  2.6 3.4 %collective-permute-start.1 = (bf16[2320,128]{1,0:T(8,128)(2,1)S(1)}, bf16[2320,128]{1,0:T(8,128)(2,1)S(1)}, u32[]{:S(2)}, u32[]{:S(2)}) collective-permute-start(bf16[2320,128]{1,0:T(8,128)(2,1)S(1)} %pack.1.refs_0_), channel_id=1, source_target_pairs={{0,2},{1,7},{2,4},{3,1},{4,6},{5,3},{6,0},{7,5},{8,10},{9,15},{10,... | collective-permute-start | bytes 1781768 | tf_op jit(solution)/shard_map/ppermute | solution.py:255
  6.0 0.0 copy-done
  6.0 1.3 %collective-permute-start.3 = (bf16[1,256,256]{2,1,0:T(8,128)(2,1)S(1)}, bf16[1,256,256]{2,1,0:T(8,128)(2,1)S(1)}, u32[]{:S(2)}, u32[]{:S(2)}) collective-permute-start(bf16[1,256,256]{2,1,0:T(8,128)(2,1)S(1)} %copy-done), channel_id=1, source_target_pairs={{0,8},{8,16},{16,24},{24,0},{1,9},{9,17},{17,25},{25,1},{2,10},{10... | collective-permute-start | bytes 393224 | tf_op jit(solution)/shard_map/ppermute | solution.py:263
  7.3 2.6 %collective-permute-start.4 = (bf16[1,256,256]{2,1,0:T(8,128)(2,1)S(1)}, bf16[1,256,256]{2,1,0:T(8,128)(2,1)S(1)}, u32[]{:S(2)}, u32[]{:S(2)}) collective-permute-start(bf16[1,256,256]{2,1,0:T(8,128)(2,1)S(1)} %copy-done), channel_id=1, source_target_pairs={{0,16},{8,24},{16,0},{24,8},{1,17},{9,25},{17,1},{25,9},{2,18},{10... | collective-permute-start | bytes 393224 | tf_op jit(solution)/shard_map/ppermute | solution.py:263
  10.0 1.1 %collective-permute-start.5 = (bf16[1,256,256]{2,1,0:T(8,128)(2,1)S(1)}, bf16[1,256,256]{2,1,0:T(8,128)(2,1)S(1)}, u32[]{:S(2)}, u32[]{:S(2)}) collective-permute-start(bf16[1,256,256]{2,1,0:T(8,128)(2,1)S(1)} %copy-done), channel_id=1, source_target_pairs={{0,24},{8,0},{16,8},{24,16},{1,25},{9,1},{17,9},{25,17},{2,26},{10... | collective-permute-start | bytes 393224 | tf_op jit(solution)/shard_map/ppermute | solution.py:263
  11.0 1.6 %collective-permute-start.2 = (bf16[2320,128]{1,0:T(8,128)(2,1)S(1)}, bf16[2320,128]{1,0:T(8,128)(2,1)S(1)}, u32[]{:S(2)}, u32[]{:S(2)}) collective-permute-start(bf16[2320,128]{1,0:T(8,128)(2,1)S(1)} %pack.1.refs_0_), channel_id=1, source_target_pairs={{0,7},{1,2},{2,1},{3,4},{4,3},{5,6},{6,5},{7,0},{8,15},{9,10},{10,... | collective-permute-start | bytes 1781768 | tf_op jit(solution)/shard_map/ppermute | solution.py:268
  12.6 0.0 collective-permute-done.3.refs_9_
  12.6 4.0 %collective-permute-done.4.refs_10_ = bf16[1,256,256]{2,1,0:T(8,128)(2,1)S(1)} collective-permute-done((bf16[1,256,256]{2,1,0:T(8,128)(2,1)S(1)}, bf16[1,256,256]{2,1,0:T(8,128)(2,1)S(1)}, u32[]{:S(2)}, u32[]{:S(2)}) %collective-permute-start.4) | collective-permute-done | bytes 131104 | tf_op jit(solution)/shard_map/ppermute | solution.py:263
  16.7 0.0 collective-permute-done.5.refs_11_
  16.7 0.0 collective-permute-done.1.refs_2_
  16.7 0.0 collective-permute-start.6
  16.7 1.7 %collective-permute-start = (bf16[2320,128]{1,0:T(8,128)(2,1)S(1)}, bf16[2320,128]{1,0:T(8,128)(2,1)S(1)}, u32[]{:S(2)}, u32[]{:S(2)}) collective-permute-start(bf16[2320,128]{1,0:T(8,128)(2,1)S(1)} %pack.1.refs_0_), channel_id=1, source_target_pairs={{0,1},{1,0},{2,3},{3,2},{4,5},{5,4},{6,7},{7,6},{8,9},{9,8},{10,11... | collective-permute-start | bytes 1781768 | tf_op jit(solution)/shard_map/ppermute | solution.py:259
  18.4 0.0 collective-permute-start.9
  18.4 3.5 %collective-permute-done.2.refs_3_ = bf16[2320,128]{1,0:T(8,128)(2,1)S(1)} collective-permute-done((bf16[2320,128]{1,0:T(8,128)(2,1)S(1)}, bf16[2320,128]{1,0:T(8,128)(2,1)S(1)}, u32[]{:S(2)}, u32[]{:S(2)}) %collective-permute-start.2) | collective-permute-done | bytes 593952 | tf_op jit(solution)/shard_map/ppermute | solution.py:268
  21.9 1.8 %collective-permute-start.8 = (bf16[2320,128]{1,0:T(8,128)(2,1)S(1)}, bf16[2320,128]{1,0:T(8,128)(2,1)S(1)}, u32[]{:S(2)}, u32[]{:S(2)}) collective-permute-start(bf16[2320,128]{1,0:T(8,128)(2,1)S(1)} %collective-permute-done.2.refs_3_), channel_id=1, source_target_pairs={{0,1},{1,0},{2,3},{3,2},{4,5},{5,4},{6,7},{7,6},{8,9},{9,8},{10,11... | collective-permute-start | bytes 1781768 | tf_op jit(solution)/shard_map/ppermute | solution.py:259
  23.7 3.3 %collective-permute-done.6.refs_4_ = bf16[2320,128]{1,0:T(8,128)(2,1)S(1)} collective-permute-done((bf16[2320,128]{1,0:T(8,128)(2,1)S(1)}, bf16[2320,128]{1,0:T(8,128)(2,1)S(1)}, u32[]{:S(2)}, u32[]{:S(2)}) %collective-permute-start.6) | collective-permute-done | bytes 593952 | tf_op jit(solution)/shard_map/ppermute | solution.py:255
  27.0 2.8 %collective-permute-start.7 = (bf16[2320,128]{1,0:T(8,128)(2,1)S(1)}, bf16[2320,128]{1,0:T(8,128)(2,1)S(1)}, u32[]{:S(2)}, u32[]{:S(2)}) collective-permute-start(bf16[2320,128]{1,0:T(8,128)(2,1)S(1)} %collective-permute-done.6.refs_4_), channel_id=1, source_target_pairs={{0,1},{1,0},{2,3},{3,2},{4,5},{5,4},{6,7},{7,6},{8,9},{9,8},{10,11... | collective-permute-start | bytes 1781768 | tf_op jit(solution)/shard_map/ppermute | solution.py:259
  29.8 0.0 collective-permute-done.refs_1_
  29.8 0.0 collective-permute-done.9.refs_7_
  29.8 0.0 collective-permute-done.8.refs_6_
  29.8 1.6 %collective-permute-done.7.refs_5_ = bf16[2320,128]{1,0:T(8,128)(2,1)S(1)} collective-permute-done((bf16[2320,128]{1,0:T(8,128)(2,1)S(1)}, bf16[2320,128]{1,0:T(8,128)(2,1)S(1)}, u32[]{:S(2)}, u32[]{:S(2)}) %collective-permute-start.7) | collective-permute-done | bytes 593952 | tf_op jit(solution)/shard_map/ppermute | solution.py:259
  31.5 15.4 %layers.1 = (f32[1,256,256]{2,1,0:T(8,128)}, bf16[4,64,256]{2,1,0:T(8,128)(2,1)S(1)}) custom-call(bf16[2320,128]{1,0:T(8,128)(2,1)S(1)} %pack.1.refs_0_, bf16[2320,128]{1,0:T(8,128)(2,1)S(1)} %collective-permute-done.refs_1_, bf16[2320,128]{1,0:T(8,128)(2,1)S(1)} %collective-permute-done.1.refs_2_, bf16[2320,128]{1,0:T(8,128)(2,1)S(1)} %collective-permute-done.2.refs_3_, ...), custom_call_target="tpu_custom_call" | custom-call | flops 8999999488 | bytes 6000000 | tf_op jit(solution)/shard_map/layers/pallas_call | solution.py:226
  46.9 0.1 collective-permute-start.10
  46.9 3.1 %collective-permute-start.11 = (bf16[64,256]{1,0:T(8,128)(2,1)S(1)}, bf16[64,256]{1,0:T(8,128)(2,1)S(1)}, u32[]{:S(2)}, u32[]{:S(2)}) collective-permute-start(bf16[64,256]{1,0:T(8,128)(2,1)S(1)} %get-tuple-element.22), channel_id=1, source_target_pairs={{0,16},{8,24},{16,0},{24,8},{1,17},{9,25},{17,1},{25,9},{2,18},{10... | collective-permute-start | bytes 98312 | tf_op jit(solution)/shard_map/ppermute | solution.py:263
  50.1 0.6 collective-permute-start.12
  50.7 0.2 collective-permute-done.10
  50.9 0.9 %collective-permute-done.11 = bf16[64,256]{1,0:T(8,128)(2,1)S(1)} collective-permute-done((bf16[64,256]{1,0:T(8,128)(2,1)S(1)}, bf16[64,256]{1,0:T(8,128)(2,1)S(1)}, u32[]{:S(2)}, u32[]{:S(2)}) %collective-permute-start.11) | collective-permute-done | bytes 32800 | tf_op jit(solution)/shard_map/ppermute | solution.py:263
  51.8 1.1 %collective-permute-done.12 = bf16[64,256]{1,0:T(8,128)(2,1)S(1)} collective-permute-done((bf16[64,256]{1,0:T(8,128)(2,1)S(1)}, bf16[64,256]{1,0:T(8,128)(2,1)S(1)}, u32[]{:S(2)}, u32[]{:S(2)}) %collective-permute-start.12) | collective-permute-done | bytes 32800 | tf_op jit(solution)/shard_map/ppermute | solution.py:263
  53.0 17.3 %all_to_all.5 = bf16[8,64,256]{2,1,0:T(8,128)(2,1)S(1)} all-to-all(bf16[8,64,256]{2,1,0:T(8,128)(2,1)S(1)} %broadcast_in_dim.2), channel_id=1, replica_groups=mesh['dp'=8,'phase'=4,'dom'=8] {'dp'}, dimensions={0} | all-to-all | bytes 524288 | tf_op jit(solution)/shard_map/all_to_all | solution.py:296
  70.3 0.1 collective-permute-start.13
  70.5 3.1 %collective-permute-done.13 = f32[64,256]{1,0:T(8,128)S(1)} collective-permute-done((f32[64,256]{1,0:T(8,128)S(1)}, f32[64,256]{1,0:T(8,128)S(1)}, u32[]{:S(2)}, u32[]{:S(2)}) %collective-permute-start.13) | collective-permute-done | bytes 65568 | tf_op jit(solution)/shard_map/ppermute | solution.py:299
  73.6 4.6 %collective-permute-start.14 = (f32[128,256]{1,0:T(8,128)S(1)}, f32[128,256]{1,0:T(8,128)S(1)}, u32[]{:S(2)}, u32[]{:S(2)}) collective-permute-start(f32[128,256]{1,0:T(8,128)S(1)} %bitcast.23), channel_id=1, source_target_pairs={{0,1},{1,0},{2,3},{3,2},{4,5},{5,4},{6,7},{7,6},{8,9},{9,8},{10,11... | collective-permute-start | bytes 393224 | tf_op jit(solution)/shard_map/ppermute | solution.py:299
  78.2 1.0 %collective-permute-done.14 = f32[128,256]{1,0:T(8,128)S(1)} collective-permute-done((f32[128,256]{1,0:T(8,128)S(1)}, f32[128,256]{1,0:T(8,128)S(1)}, u32[]{:S(2)}, u32[]{:S(2)}) %collective-permute-start.14) | collective-permute-done | bytes 131104 | tf_op jit(solution)/shard_map/ppermute | solution.py:299
  79.2 0.7 pad_maximum_fusion
  (7 shorter events, 0.1 us)
Async XLA Ops:
  0.6 5.4 %copy-start = (bf16[1,256,256]{2,1,0:T(8,128)(2,1)S(1)}, bf16[1,256,256]{2,1,0:T(8,128)(2,1)}, u32[]{:S(2)}) copy-start(bf16[1,256,256]{2,1,0:T(8,128)(2,1)} %refs_8_) | copy-start | bytes 393220
  2.6 14.0 %collective-permute-start.1 = (bf16[2320,128]{1,0:T(8,128)(2,1)S(1)}, bf16[2320,128]{1,0:T(8,128)(2,1)S(1)}, u32[]{:S(2)}, u32[]{:S(2)}) collective-permute-start(bf16[2320,128]{1,0:T(8,128)(2,1)S(1)} %pack.1.refs_0_), channel_id=1, source_target_pairs={{0,2},{1,7},{2,4},{3,1},{4,6},{5,3},{6,0},{7,5},{8,10},{9,15},{10,... | collective-permute-start | bytes 1781768 | tf_op jit(solution)/shard_map/ppermute | solution.py:255
  6.0 6.6 %collective-permute-start.3 = (bf16[1,256,256]{2,1,0:T(8,128)(2,1)S(1)}, bf16[1,256,256]{2,1,0:T(8,128)(2,1)S(1)}, u32[]{:S(2)}, u32[]{:S(2)}) collective-permute-start(bf16[1,256,256]{2,1,0:T(8,128)(2,1)S(1)} %copy-done), channel_id=1, source_target_pairs={{0,8},{8,16},{16,24},{24,0},{1,9},{9,17},{17,25},{25,1},{2,10},{10... | collective-permute-start | bytes 393224 | tf_op jit(solution)/shard_map/ppermute | solution.py:263
  7.3 9.3 %collective-permute-start.4 = (bf16[1,256,256]{2,1,0:T(8,128)(2,1)S(1)}, bf16[1,256,256]{2,1,0:T(8,128)(2,1)S(1)}, u32[]{:S(2)}, u32[]{:S(2)}) collective-permute-start(bf16[1,256,256]{2,1,0:T(8,128)(2,1)S(1)} %copy-done), channel_id=1, source_target_pairs={{0,16},{8,24},{16,0},{24,8},{1,17},{9,25},{17,1},{25,9},{2,18},{10... | collective-permute-start | bytes 393224 | tf_op jit(solution)/shard_map/ppermute | solution.py:263
  10.0 6.7 %collective-permute-start.5 = (bf16[1,256,256]{2,1,0:T(8,128)(2,1)S(1)}, bf16[1,256,256]{2,1,0:T(8,128)(2,1)S(1)}, u32[]{:S(2)}, u32[]{:S(2)}) collective-permute-start(bf16[1,256,256]{2,1,0:T(8,128)(2,1)S(1)} %copy-done), channel_id=1, source_target_pairs={{0,24},{8,0},{16,8},{24,16},{1,25},{9,1},{17,9},{25,17},{2,26},{10... | collective-permute-start | bytes 393224 | tf_op jit(solution)/shard_map/ppermute | solution.py:263
  11.0 10.9 %collective-permute-start.2 = (bf16[2320,128]{1,0:T(8,128)(2,1)S(1)}, bf16[2320,128]{1,0:T(8,128)(2,1)S(1)}, u32[]{:S(2)}, u32[]{:S(2)}) collective-permute-start(bf16[2320,128]{1,0:T(8,128)(2,1)S(1)} %pack.1.refs_0_), channel_id=1, source_target_pairs={{0,7},{1,2},{2,1},{3,4},{4,3},{5,6},{6,5},{7,0},{8,15},{9,10},{10,... | collective-permute-start | bytes 1781768 | tf_op jit(solution)/shard_map/ppermute | solution.py:268
  16.7 10.4 %collective-permute-start.6 = (bf16[2320,128]{1,0:T(8,128)(2,1)S(1)}, bf16[2320,128]{1,0:T(8,128)(2,1)S(1)}, u32[]{:S(2)}, u32[]{:S(2)}) collective-permute-start(bf16[2320,128]{1,0:T(8,128)(2,1)S(1)} %collective-permute-done.1.refs_2_), channel_id=1, source_target_pairs={{0,2},{1,7},{2,4},{3,1},{4,6},{5,3},{6,0},{7,5},{8,10},{9,15},{10,... | collective-permute-start | bytes 1781768 | tf_op jit(solution)/shard_map/ppermute | solution.py:255
  16.7 13.2 %collective-permute-start = (bf16[2320,128]{1,0:T(8,128)(2,1)S(1)}, bf16[2320,128]{1,0:T(8,128)(2,1)S(1)}, u32[]{:S(2)}, u32[]{:S(2)}) collective-permute-start(bf16[2320,128]{1,0:T(8,128)(2,1)S(1)} %pack.1.refs_0_), channel_id=1, source_target_pairs={{0,1},{1,0},{2,3},{3,2},{4,5},{5,4},{6,7},{7,6},{8,9},{9,8},{10,11... | collective-permute-start | bytes 1781768 | tf_op jit(solution)/shard_map/ppermute | solution.py:259
  18.4 11.4 %collective-permute-start.9 = (bf16[2320,128]{1,0:T(8,128)(2,1)S(1)}, bf16[2320,128]{1,0:T(8,128)(2,1)S(1)}, u32[]{:S(2)}, u32[]{:S(2)}) collective-permute-start(bf16[2320,128]{1,0:T(8,128)(2,1)S(1)} %collective-permute-done.1.refs_2_), channel_id=1, source_target_pairs={{0,1},{1,0},{2,3},{3,2},{4,5},{5,4},{6,7},{7,6},{8,9},{9,8},{10,11... | collective-permute-start | bytes 1781768 | tf_op jit(solution)/shard_map/ppermute | solution.py:259
  21.9 8.0 %collective-permute-start.8 = (bf16[2320,128]{1,0:T(8,128)(2,1)S(1)}, bf16[2320,128]{1,0:T(8,128)(2,1)S(1)}, u32[]{:S(2)}, u32[]{:S(2)}) collective-permute-start(bf16[2320,128]{1,0:T(8,128)(2,1)S(1)} %collective-permute-done.2.refs_3_), channel_id=1, source_target_pairs={{0,1},{1,0},{2,3},{3,2},{4,5},{5,4},{6,7},{7,6},{8,9},{9,8},{10,11... | collective-permute-start | bytes 1781768 | tf_op jit(solution)/shard_map/ppermute | solution.py:259
  27.0 4.4 %collective-permute-start.7 = (bf16[2320,128]{1,0:T(8,128)(2,1)S(1)}, bf16[2320,128]{1,0:T(8,128)(2,1)S(1)}, u32[]{:S(2)}, u32[]{:S(2)}) collective-permute-start(bf16[2320,128]{1,0:T(8,128)(2,1)S(1)} %collective-permute-done.6.refs_4_), channel_id=1, source_target_pairs={{0,1},{1,0},{2,3},{3,2},{4,5},{5,4},{6,7},{7,6},{8,9},{9,8},{10,11... | collective-permute-start | bytes 1781768 | tf_op jit(solution)/shard_map/ppermute | solution.py:259
  46.9 4.1 %collective-permute-start.10 = (bf16[64,256]{1,0:T(8,128)(2,1)S(1)}, bf16[64,256]{1,0:T(8,128)(2,1)S(1)}, u32[]{:S(2)}, u32[]{:S(2)}) collective-permute-start(bf16[64,256]{1,0:T(8,128)(2,1)S(1)} %get-tuple-element.20), channel_id=1, source_target_pairs={{0,8},{8,16},{16,24},{24,0},{1,9},{9,17},{17,25},{25,1},{2,10},{10... | collective-permute-start | bytes 98312 | tf_op jit(solution)/shard_map/ppermute | solution.py:263
  46.9 4.9 %collective-permute-start.11 = (bf16[64,256]{1,0:T(8,128)(2,1)S(1)}, bf16[64,256]{1,0:T(8,128)(2,1)S(1)}, u32[]{:S(2)}, u32[]{:S(2)}) collective-permute-start(bf16[64,256]{1,0:T(8,128)(2,1)S(1)} %get-tuple-element.22), channel_id=1, source_target_pairs={{0,16},{8,24},{16,0},{24,8},{1,17},{9,25},{17,1},{25,9},{2,18},{10... | collective-permute-start | bytes 98312 | tf_op jit(solution)/shard_map/ppermute | solution.py:263
  50.1 2.8 %collective-permute-start.12 = (bf16[64,256]{1,0:T(8,128)(2,1)S(1)}, bf16[64,256]{1,0:T(8,128)(2,1)S(1)}, u32[]{:S(2)}, u32[]{:S(2)}) collective-permute-start(bf16[64,256]{1,0:T(8,128)(2,1)S(1)} %get-tuple-element.21), channel_id=1, source_target_pairs={{0,24},{8,0},{16,8},{24,16},{1,25},{9,1},{17,9},{25,17},{2,26},{10... | collective-permute-start | bytes 98312 | tf_op jit(solution)/shard_map/ppermute | solution.py:263
  70.3 3.2 %collective-permute-start.13 = (f32[64,256]{1,0:T(8,128)S(1)}, f32[64,256]{1,0:T(8,128)S(1)}, u32[]{:S(2)}, u32[]{:S(2)}) collective-permute-start(f32[64,256]{1,0:T(8,128)S(1)} %convert_reduce_fusion), channel_id=1, source_target_pairs={{0,2},{1,3},{2,0},{3,1},{4,6},{5,7},{6,4},{7,5},{8,10},{9,11},{10,... | collective-permute-start | bytes 196616 | tf_op jit(solution)/shard_map/ppermute | solution.py:299
  73.6 5.6 %collective-permute-start.14 = (f32[128,256]{1,0:T(8,128)S(1)}, f32[128,256]{1,0:T(8,128)S(1)}, u32[]{:S(2)}, u32[]{:S(2)}) collective-permute-start(f32[128,256]{1,0:T(8,128)S(1)} %bitcast.23), channel_id=1, source_target_pairs={{0,1},{1,0},{2,3},{3,2},{4,5},{5,4},{6,7},{7,6},{8,9},{9,8},{10,11... | collective-permute-start | bytes 393224 | tf_op jit(solution)/shard_map/ppermute | solution.py:299

commit v7 on v6

--- a/solution.py
+++ b/solution.py
@@ -295,12 +295,14 @@
     mine = jnp.broadcast_to(mine[None], (8,) + mine.shape)
     mine = jnp.sum(lax.all_to_all(mine, "dp", 0, 0, tiled=True).astype(F32), axis=0)
     dom = lax.axis_index("dom")
-    for bit in (2, 1):
-        other = lax.ppermute(mine, "dom", [(i, i ^ bit) for i in range(8)])
-        odd = lax.bitwise_and(dom, bit) != 0
-        both = jnp.stack([jnp.where(odd, other, mine), jnp.where(odd, mine, other)])
-        mine = both.reshape(-1, both.shape[-1])
-    return grad_initial, mine.reshape(1, 256, 256)
+    held = [mine] + [lax.ppermute(mine, "dom", [(i, i ^ n) for i in range(8)]) for n in (2, 3, 1)]
+    by_bits = {0: held[0], 2: held[1], 3: held[2], 1: held[3]}
+    far_chip, far_core = lax.bitwise_and(dom, 2) != 0, lax.bitwise_and(dom, 1) != 0
+    rows = []
+    for quarter in (0, 2, 1, 3):
+        chip = [jnp.where(far_chip, by_bits[quarter ^ 2 ^ n], by_bits[quarter ^ n]) for n in (0, 1)]
+        rows.append(jnp.where(far_core, chip[1], chip[0]))
+    return grad_initial, jnp.concatenate(rows, axis=0)[None]
 
 
 def solution(mesh):

time: 80.1 us -> 79.4 us (level)
    ppermute x2 -> x3, waiting for transfers between devices: 4.08 us -> 3.3 us  [local(): lax.ppermute(mine, 'dom', [(i, i ^ n) for i in range(8)])]
    ppermute x2 -> x3, starting transfers between devices: 4.73 us -> 4.84 us  [local(): lax.ppermute(mine, 'dom', [(i, i ^ n) for i in range(8)])]
  transfers between devices with their start and end apart: 15 -> 16, of which waited for: 9 -> 8; matrix products, arithmetic and copies ran while one was open for 0% -> 0% of each run, Pallas kernels for 0% -> 0%
where the time goes in v7:
time: 79.4 us; the launch traced here: 79.2 us
  starting transfers between devices  25 us (31%)
  waiting for transfers between devices  18 us (23%)
  Pallas kernels  17.4 us (22%)
  blocking collectives  17.3 us (22%)
  other arithmetic  0.8 us (1%)
    all_to_all x1, blocking collectives, local(): lax.all_to_all(mine, 'dp', 0, 0, tiled=True).astype(F32)  17.3 us
    pallas_call x1, Pallas kernels, run_layers(): pl.pallas_call(functools.partial(layers_kernel, scale, betas), in_specs=[...  15.4 us
    ppermute x6, starting transfers between devices, to_phase(): return lax.ppermute(v, 'phase', [(i, (i + n) % 4) for i in range(4)])  8.78 us
    ppermute x4, starting transfers between devices, other_core(): return lax.ppermute(v, 'dom', [(i, i ^ 1) for i in range(8)])  6.32 us
    ppermute x6, waiting for transfers between devices, to_phase(): return lax.ppermute(v, 'phase', [(i, (i + n) % 4) for i in range(4)])  6.28 us
    ppermute x3, starting transfers between devices, local(): lax.ppermute(mine, 'dom', [(i, i ^ n) for i in range(8)])  4.84 us
    ppermute x1, waiting for transfers between devices, across(): return lax.ppermute(v, 'dom', route)  3.49 us
    ppermute x2, starting transfers between devices, onward(): return lax.ppermute(v, 'dom', route)  3.39 us
  transfers between devices with their start and end apart: 16, of which 8 were waited for; matrix products, arithmetic and copies ran while one was open for 0% of the time, Pallas kernels for 0%

profile of v7, /device:TPU:1, one launch (start us, length us, event | category | flops | bytes accessed | tf_op | source)
XLA Modules:
  0.0 79.2 jit_solution(13321650675969600547)
XLA Ops:
  0.6 0.0 copy-start
  0.6 2.0 %pack.1.refs_0_ = bf16[2320,128]{1,0:T(8,128)(2,1)S(1)} custom-call(bf16[4,1280,128]{2,1,0:T(8,128)(2,1)} %bitcast.12, bf16[4,256,256]{2,1,0:T(8,128)(2,1)} %initial.1, bf16[4,256,256]{2,1,0:T(8,128)(2,1)} %cotangent.1, s32[4,2,5]{2,1,0:T(2,128)} %cols.1), custom_call_target="tpu_custom_call" | custom-call | tf_op jit(solution)/shard_map/pack/pallas_call | solution.py:61
  2.6 3.4 %collective-permute-start.1 = (bf16[2320,128]{1,0:T(8,128)(2,1)S(1)}, bf16[2320,128]{1,0:T(8,128)(2,1)S(1)}, u32[]{:S(2)}, u32[]{:S(2)}) collective-permute-start(bf16[2320,128]{1,0:T(8,128)(2,1)S(1)} %pack.1.refs_0_), channel_id=1, source_target_pairs={{0,2},{1,7},{2,4},{3,1},{4,6},{5,3},{6,0},{7,5},{8,10},{9,15},{10,... | collective-permute-start | bytes 1781768 | tf_op jit(solution)/shard_map/ppermute | solution.py:255
  6.0 0.0 copy-done
  6.0 1.3 %collective-permute-start.3 = (bf16[1,256,256]{2,1,0:T(8,128)(2,1)S(1)}, bf16[1,256,256]{2,1,0:T(8,128)(2,1)S(1)}, u32[]{:S(2)}, u32[]{:S(2)}) collective-permute-start(bf16[1,256,256]{2,1,0:T(8,128)(2,1)S(1)} %copy-done), channel_id=1, source_target_pairs={{0,8},{8,16},{16,24},{24,0},{1,9},{9,17},{17,25},{25,1},{2,10},{10... | collective-permute-start | bytes 393224 | tf_op jit(solution)/shard_map/ppermute | solution.py:263
  7.3 2.6 %collective-permute-start.4 = (bf16[1,256,256]{2,1,0:T(8,128)(2,1)S(1)}, bf16[1,256,256]{2,1,0:T(8,128)(2,1)S(1)}, u32[]{:S(2)}, u32[]{:S(2)}) collective-permute-start(bf16[1,256,256]{2,1,0:T(8,128)(2,1)S(1)} %copy-done), channel_id=1, source_target_pairs={{0,16},{8,24},{16,0},{24,8},{1,17},{9,25},{17,1},{25,9},{2,18},{10... | collective-permute-start | bytes 393224 | tf_op jit(solution)/shard_map/ppermute | solution.py:263
  10.0 1.1 %collective-permute-start.5 = (bf16[1,256,256]{2,1,0:T(8,128)(2,1)S(1)}, bf16[1,256,256]{2,1,0:T(8,128)(2,1)S(1)}, u32[]{:S(2)}, u32[]{:S(2)}) collective-permute-start(bf16[1,256,256]{2,1,0:T(8,128)(2,1)S(1)} %copy-done), channel_id=1, source_target_pairs={{0,24},{8,0},{16,8},{24,16},{1,25},{9,1},{17,9},{25,17},{2,26},{10... | collective-permute-start | bytes 393224 | tf_op jit(solution)/shard_map/ppermute | solution.py:263
  11.0 1.6 %collective-permute-start.2 = (bf16[2320,128]{1,0:T(8,128)(2,1)S(1)}, bf16[2320,128]{1,0:T(8,128)(2,1)S(1)}, u32[]{:S(2)}, u32[]{:S(2)}) collective-permute-start(bf16[2320,128]{1,0:T(8,128)(2,1)S(1)} %pack.1.refs_0_), channel_id=1, source_target_pairs={{0,7},{1,2},{2,1},{3,4},{4,3},{5,6},{6,5},{7,0},{8,15},{9,10},{10,... | collective-permute-start | bytes 1781768 | tf_op jit(solution)/shard_map/ppermute | solution.py:268
  12.6 0.0 collective-permute-done.3.refs_9_
  12.6 4.0 %collective-permute-done.4.refs_10_ = bf16[1,256,256]{2,1,0:T(8,128)(2,1)S(1)} collective-permute-done((bf16[1,256,256]{2,1,0:T(8,128)(2,1)S(1)}, bf16[1,256,256]{2,1,0:T(8,128)(2,1)S(1)}, u32[]{:S(2)}, u32[]{:S(2)}) %collective-permute-start.4) | collective-permute-done | bytes 131104 | tf_op jit(solution)/shard_map/ppermute | solution.py:263
  16.7 0.0 collective-permute-done.5.refs_11_
  16.7 0.0 collective-permute-done.1.refs_2_
  16.7 0.0 collective-permute-start.6
  16.7 1.7 %collective-permute-start = (bf16[2320,128]{1,0:T(8,128)(2,1)S(1)}, bf16[2320,128]{1,0:T(8,128)(2,1)S(1)}, u32[]{:S(2)}, u32[]{:S(2)}) collective-permute-start(bf16[2320,128]{1,0:T(8,128)(2,1)S(1)} %pack.1.refs_0_), channel_id=1, source_target_pairs={{0,1},{1,0},{2,3},{3,2},{4,5},{5,4},{6,7},{7,6},{8,9},{9,8},{10,11... | collective-permute-start | bytes 1781768 | tf_op jit(solution)/shard_map/ppermute | solution.py:259
  18.4 0.0 collective-permute-start.9
  18.4 3.5 %collective-permute-done.2.refs_3_ = bf16[2320,128]{1,0:T(8,128)(2,1)S(1)} collective-permute-done((bf16[2320,128]{1,0:T(8,128)(2,1)S(1)}, bf16[2320,128]{1,0:T(8,128)(2,1)S(1)}, u32[]{:S(2)}, u32[]{:S(2)}) %collective-permute-start.2) | collective-permute-done | bytes 593952 | tf_op jit(solution)/shard_map/ppermute | solution.py:268
  21.9 1.8 %collective-permute-start.8 = (bf16[2320,128]{1,0:T(8,128)(2,1)S(1)}, bf16[2320,128]{1,0:T(8,128)(2,1)S(1)}, u32[]{:S(2)}, u32[]{:S(2)}) collective-permute-start(bf16[2320,128]{1,0:T(8,128)(2,1)S(1)} %collective-permute-done.2.refs_3_), channel_id=1, source_target_pairs={{0,1},{1,0},{2,3},{3,2},{4,5},{5,4},{6,7},{7,6},{8,9},{9,8},{10,11... | collective-permute-start | bytes 1781768 | tf_op jit(solution)/shard_map/ppermute | solution.py:259
  23.7 3.3 %collective-permute-done.6.refs_4_ = bf16[2320,128]{1,0:T(8,128)(2,1)S(1)} collective-permute-done((bf16[2320,128]{1,0:T(8,128)(2,1)S(1)}, bf16[2320,128]{1,0:T(8,128)(2,1)S(1)}, u32[]{:S(2)}, u32[]{:S(2)}) %collective-permute-start.6) | collective-permute-done | bytes 593952 | tf_op jit(solution)/shard_map/ppermute | solution.py:255
  27.0 2.8 %collective-permute-start.7 = (bf16[2320,128]{1,0:T(8,128)(2,1)S(1)}, bf16[2320,128]{1,0:T(8,128)(2,1)S(1)}, u32[]{:S(2)}, u32[]{:S(2)}) collective-permute-start(bf16[2320,128]{1,0:T(8,128)(2,1)S(1)} %collective-permute-done.6.refs_4_), channel_id=1, source_target_pairs={{0,1},{1,0},{2,3},{3,2},{4,5},{5,4},{6,7},{7,6},{8,9},{9,8},{10,11... | collective-permute-start | bytes 1781768 | tf_op jit(solution)/shard_map/ppermute | solution.py:259
  29.8 0.0 collective-permute-done.refs_1_
  29.8 0.0 collective-permute-done.9.refs_7_
  29.8 0.0 collective-permute-done.8.refs_6_
  29.8 1.6 %collective-permute-done.7.refs_5_ = bf16[2320,128]{1,0:T(8,128)(2,1)S(1)} collective-permute-done((bf16[2320,128]{1,0:T(8,128)(2,1)S(1)}, bf16[2320,128]{1,0:T(8,128)(2,1)S(1)}, u32[]{:S(2)}, u32[]{:S(2)}) %collective-permute-start.7) | collective-permute-done | bytes 593952 | tf_op jit(solution)/shard_map/ppermute | solution.py:259
  31.5 15.4 %layers.1 = (f32[1,256,256]{2,1,0:T(8,128)}, bf16[4,64,256]{2,1,0:T(8,128)(2,1)S(1)}) custom-call(bf16[2320,128]{1,0:T(8,128)(2,1)S(1)} %pack.1.refs_0_, bf16[2320,128]{1,0:T(8,128)(2,1)S(1)} %collective-permute-done.refs_1_, bf16[2320,128]{1,0:T(8,128)(2,1)S(1)} %collective-permute-done.1.refs_2_, bf16[2320,128]{1,0:T(8,128)(2,1)S(1)} %collective-permute-done.2.refs_3_, ...), custom_call_target="tpu_custom_call" | custom-call | flops 8999999488 | bytes 6000000 | tf_op jit(solution)/shard_map/layers/pallas_call | solution.py:226
  46.9 0.1 collective-permute-start.10
  46.9 3.1 %collective-permute-start.11 = (bf16[64,256]{1,0:T(8,128)(2,1)S(1)}, bf16[64,256]{1,0:T(8,128)(2,1)S(1)}, u32[]{:S(2)}, u32[]{:S(2)}) collective-permute-start(bf16[64,256]{1,0:T(8,128)(2,1)S(1)} %get-tuple-element.22), channel_id=1, source_target_pairs={{0,16},{8,24},{16,0},{24,8},{1,17},{9,25},{17,1},{25,9},{2,18},{10... | collective-permute-start | bytes 98312 | tf_op jit(solution)/shard_map/ppermute | solution.py:263
  50.1 0.6 collective-permute-start.12
  50.7 0.2 collective-permute-done.10
  50.9 0.9 %collective-permute-done.11 = bf16[64,256]{1,0:T(8,128)(2,1)S(1)} collective-permute-done((bf16[64,256]{1,0:T(8,128)(2,1)S(1)}, bf16[64,256]{1,0:T(8,128)(2,1)S(1)}, u32[]{:S(2)}, u32[]{:S(2)}) %collective-permute-start.11) | collective-permute-done | bytes 32800 | tf_op jit(solution)/shard_map/ppermute | solution.py:263
  51.8 1.1 %collective-permute-done.12 = bf16[64,256]{1,0:T(8,128)(2,1)S(1)} collective-permute-done((bf16[64,256]{1,0:T(8,128)(2,1)S(1)}, bf16[64,256]{1,0:T(8,128)(2,1)S(1)}, u32[]{:S(2)}, u32[]{:S(2)}) %collective-permute-start.12) | collective-permute-done | bytes 32800 | tf_op jit(solution)/shard_map/ppermute | solution.py:263
  53.0 17.3 %all_to_all.5 = bf16[8,64,256]{2,1,0:T(8,128)(2,1)S(1)} all-to-all(bf16[8,64,256]{2,1,0:T(8,128)(2,1)S(1)} %broadcast_in_dim.4), channel_id=1, replica_groups=mesh['dp'=8,'phase'=4,'dom'=8] {'dp'}, dimensions={0} | all-to-all | bytes 524288 | tf_op jit(solution)/shard_map/all_to_all | solution.py:296
  70.3 2.7 %collective-permute-start.13 = (f32[64,256]{1,0:T(8,128)S(1)}, f32[64,256]{1,0:T(8,128)S(1)}, u32[]{:S(2)}, u32[]{:S(2)}) collective-permute-start(f32[64,256]{1,0:T(8,128)S(1)} %convert_reduce_fusion), channel_id=1, source_target_pairs={{0,3},{1,2},{2,1},{3,0},{4,7},{5,6},{6,5},{7,4},{8,11},{9,10},{10,... | collective-permute-start | bytes 196616 | tf_op jit(solution)/shard_map/ppermute | solution.py:298
  73.0 0.9 %collective-permute-start.14 = (f32[64,256]{1,0:T(8,128)S(1)}, f32[64,256]{1,0:T(8,128)S(1)}, u32[]{:S(2)}, u32[]{:S(2)}) collective-permute-start(f32[64,256]{1,0:T(8,128)S(1)} %convert_reduce_fusion), channel_id=1, source_target_pairs={{0,1},{1,0},{2,3},{3,2},{4,5},{5,4},{6,7},{7,6},{8,9},{9,8},{10,11... | collective-permute-start | bytes 196616 | tf_op jit(solution)/shard_map/ppermute | solution.py:298
  73.9 1.3 %collective-permute-start.15 = (f32[64,256]{1,0:T(8,128)S(1)}, f32[64,256]{1,0:T(8,128)S(1)}, u32[]{:S(2)}, u32[]{:S(2)}) collective-permute-start(f32[64,256]{1,0:T(8,128)S(1)} %convert_reduce_fusion), channel_id=1, source_target_pairs={{0,2},{1,3},{2,0},{3,1},{4,6},{5,7},{6,4},{7,5},{8,10},{9,11},{10,... | collective-permute-start | bytes 196616 | tf_op jit(solution)/shard_map/ppermute | solution.py:298
  75.2 0.0 collective-permute-done.13
  75.2 0.0 collective-permute-done.14
  75.2 3.3 %collective-permute-done.15 = f32[64,256]{1,0:T(8,128)S(1)} collective-permute-done((f32[64,256]{1,0:T(8,128)S(1)}, f32[64,256]{1,0:T(8,128)S(1)}, u32[]{:S(2)}, u32[]{:S(2)}) %collective-permute-start.15) | collective-permute-done | bytes 65568 | tf_op jit(solution)/shard_map/ppermute | solution.py:298
  78.5 0.7 maximum_bitcast_fusion
  (5 shorter events, 0.1 us)
Async XLA Ops:
  0.6 5.4 %copy-start = (bf16[1,256,256]{2,1,0:T(8,128)(2,1)S(1)}, bf16[1,256,256]{2,1,0:T(8,128)(2,1)}, u32[]{:S(2)}) copy-start(bf16[1,256,256]{2,1,0:T(8,128)(2,1)} %refs_8_) | copy-start | bytes 393220
  2.6 14.0 %collective-permute-start.1 = (bf16[2320,128]{1,0:T(8,128)(2,1)S(1)}, bf16[2320,128]{1,0:T(8,128)(2,1)S(1)}, u32[]{:S(2)}, u32[]{:S(2)}) collective-permute-start(bf16[2320,128]{1,0:T(8,128)(2,1)S(1)} %pack.1.refs_0_), channel_id=1, source_target_pairs={{0,2},{1,7},{2,4},{3,1},{4,6},{5,3},{6,0},{7,5},{8,10},{9,15},{10,... | collective-permute-start | bytes 1781768 | tf_op jit(solution)/shard_map/ppermute | solution.py:255
  6.0 6.6 %collective-permute-start.3 = (bf16[1,256,256]{2,1,0:T(8,128)(2,1)S(1)}, bf16[1,256,256]{2,1,0:T(8,128)(2,1)S(1)}, u32[]{:S(2)}, u32[]{:S(2)}) collective-permute-start(bf16[1,256,256]{2,1,0:T(8,128)(2,1)S(1)} %copy-done), channel_id=1, source_target_pairs={{0,8},{8,16},{16,24},{24,0},{1,9},{9,17},{17,25},{25,1},{2,10},{10... | collective-permute-start | bytes 393224 | tf_op jit(solution)/shard_map/ppermute | solution.py:263
  7.3 9.3 %collective-permute-start.4 = (bf16[1,256,256]{2,1,0:T(8,128)(2,1)S(1)}, bf16[1,256,256]{2,1,0:T(8,128)(2,1)S(1)}, u32[]{:S(2)}, u32[]{:S(2)}) collective-permute-start(bf16[1,256,256]{2,1,0:T(8,128)(2,1)S(1)} %copy-done), channel_id=1, source_target_pairs={{0,16},{8,24},{16,0},{24,8},{1,17},{9,25},{17,1},{25,9},{2,18},{10... | collective-permute-start | bytes 393224 | tf_op jit(solution)/shard_map/ppermute | solution.py:263
  10.0 6.7 %collective-permute-start.5 = (bf16[1,256,256]{2,1,0:T(8,128)(2,1)S(1)}, bf16[1,256,256]{2,1,0:T(8,128)(2,1)S(1)}, u32[]{:S(2)}, u32[]{:S(2)}) collective-permute-start(bf16[1,256,256]{2,1,0:T(8,128)(2,1)S(1)} %copy-done), channel_id=1, source_target_pairs={{0,24},{8,0},{16,8},{24,16},{1,25},{9,1},{17,9},{25,17},{2,26},{10... | collective-permute-start | bytes 393224 | tf_op jit(solution)/shard_map/ppermute | solution.py:263
  11.0 10.9 %collective-permute-start.2 = (bf16[2320,128]{1,0:T(8,128)(2,1)S(1)}, bf16[2320,128]{1,0:T(8,128)(2,1)S(1)}, u32[]{:S(2)}, u32[]{:S(2)}) collective-permute-start(bf16[2320,128]{1,0:T(8,128)(2,1)S(1)} %pack.1.refs_0_), channel_id=1, source_target_pairs={{0,7},{1,2},{2,1},{3,4},{4,3},{5,6},{6,5},{7,0},{8,15},{9,10},{10,... | collective-permute-start | bytes 1781768 | tf_op jit(solution)/shard_map/ppermute | solution.py:268
  16.7 10.4 %collective-permute-start.6 = (bf16[2320,128]{1,0:T(8,128)(2,1)S(1)}, bf16[2320,128]{1,0:T(8,128)(2,1)S(1)}, u32[]{:S(2)}, u32[]{:S(2)}) collective-permute-start(bf16[2320,128]{1,0:T(8,128)(2,1)S(1)} %collective-permute-done.1.refs_2_), channel_id=1, source_target_pairs={{0,2},{1,7},{2,4},{3,1},{4,6},{5,3},{6,0},{7,5},{8,10},{9,15},{10,... | collective-permute-start | bytes 1781768 | tf_op jit(solution)/shard_map/ppermute | solution.py:255
  16.7 13.2 %collective-permute-start = (bf16[2320,128]{1,0:T(8,128)(2,1)S(1)}, bf16[2320,128]{1,0:T(8,128)(2,1)S(1)}, u32[]{:S(2)}, u32[]{:S(2)}) collective-permute-start(bf16[2320,128]{1,0:T(8,128)(2,1)S(1)} %pack.1.refs_0_), channel_id=1, source_target_pairs={{0,1},{1,0},{2,3},{3,2},{4,5},{5,4},{6,7},{7,6},{8,9},{9,8},{10,11... | collective-permute-start | bytes 1781768 | tf_op jit(solution)/shard_map/ppermute | solution.py:259
  18.4 11.4 %collective-permute-start.9 = (bf16[2320,128]{1,0:T(8,128)(2,1)S(1)}, bf16[2320,128]{1,0:T(8,128)(2,1)S(1)}, u32[]{:S(2)}, u32[]{:S(2)}) collective-permute-start(bf16[2320,128]{1,0:T(8,128)(2,1)S(1)} %collective-permute-done.1.refs_2_), channel_id=1, source_target_pairs={{0,1},{1,0},{2,3},{3,2},{4,5},{5,4},{6,7},{7,6},{8,9},{9,8},{10,11... | collective-permute-start | bytes 1781768 | tf_op jit(solution)/shard_map/ppermute | solution.py:259
  21.9 8.0 %collective-permute-start.8 = (bf16[2320,128]{1,0:T(8,128)(2,1)S(1)}, bf16[2320,128]{1,0:T(8,128)(2,1)S(1)}, u32[]{:S(2)}, u32[]{:S(2)}) collective-permute-start(bf16[2320,128]{1,0:T(8,128)(2,1)S(1)} %collective-permute-done.2.refs_3_), channel_id=1, source_target_pairs={{0,1},{1,0},{2,3},{3,2},{4,5},{5,4},{6,7},{7,6},{8,9},{9,8},{10,11... | collective-permute-start | bytes 1781768 | tf_op jit(solution)/shard_map/ppermute | solution.py:259
  27.0 4.4 %collective-permute-start.7 = (bf16[2320,128]{1,0:T(8,128)(2,1)S(1)}, bf16[2320,128]{1,0:T(8,128)(2,1)S(1)}, u32[]{:S(2)}, u32[]{:S(2)}) collective-permute-start(bf16[2320,128]{1,0:T(8,128)(2,1)S(1)} %collective-permute-done.6.refs_4_), channel_id=1, source_target_pairs={{0,1},{1,0},{2,3},{3,2},{4,5},{5,4},{6,7},{7,6},{8,9},{9,8},{10,11... | collective-permute-start | bytes 1781768 | tf_op jit(solution)/shard_map/ppermute | solution.py:259
  46.9 4.1 %collective-permute-start.10 = (bf16[64,256]{1,0:T(8,128)(2,1)S(1)}, bf16[64,256]{1,0:T(8,128)(2,1)S(1)}, u32[]{:S(2)}, u32[]{:S(2)}) collective-permute-start(bf16[64,256]{1,0:T(8,128)(2,1)S(1)} %get-tuple-element.20), channel_id=1, source_target_pairs={{0,8},{8,16},{16,24},{24,0},{1,9},{9,17},{17,25},{25,1},{2,10},{10... | collective-permute-start | bytes 98312 | tf_op jit(solution)/shard_map/ppermute | solution.py:263
  46.9 4.9 %collective-permute-start.11 = (bf16[64,256]{1,0:T(8,128)(2,1)S(1)}, bf16[64,256]{1,0:T(8,128)(2,1)S(1)}, u32[]{:S(2)}, u32[]{:S(2)}) collective-permute-start(bf16[64,256]{1,0:T(8,128)(2,1)S(1)} %get-tuple-element.22), channel_id=1, source_target_pairs={{0,16},{8,24},{16,0},{24,8},{1,17},{9,25},{17,1},{25,9},{2,18},{10... | collective-permute-start | bytes 98312 | tf_op jit(solution)/shard_map/ppermute | solution.py:263
  50.1 2.8 %collective-permute-start.12 = (bf16[64,256]{1,0:T(8,128)(2,1)S(1)}, bf16[64,256]{1,0:T(8,128)(2,1)S(1)}, u32[]{:S(2)}, u32[]{:S(2)}) collective-permute-start(bf16[64,256]{1,0:T(8,128)(2,1)S(1)} %get-tuple-element.21), channel_id=1, source_target_pairs={{0,24},{8,0},{16,8},{24,16},{1,25},{9,1},{17,9},{25,17},{2,26},{10... | collective-permute-start | bytes 98312 | tf_op jit(solution)/shard_map/ppermute | solution.py:263
  70.3 4.8 %collective-permute-start.13 = (f32[64,256]{1,0:T(8,128)S(1)}, f32[64,256]{1,0:T(8,128)S(1)}, u32[]{:S(2)}, u32[]{:S(2)}) collective-permute-start(f32[64,256]{1,0:T(8,128)S(1)} %convert_reduce_fusion), channel_id=1, source_target_pairs={{0,3},{1,2},{2,1},{3,0},{4,7},{5,6},{6,5},{7,4},{8,11},{9,10},{10,... | collective-permute-start | bytes 196616 | tf_op jit(solution)/shard_map/ppermute | solution.py:298
  73.0 2.2 %collective-permute-start.14 = (f32[64,256]{1,0:T(8,128)S(1)}, f32[64,256]{1,0:T(8,128)S(1)}, u32[]{:S(2)}, u32[]{:S(2)}) collective-permute-start(f32[64,256]{1,0:T(8,128)S(1)} %convert_reduce_fusion), channel_id=1, source_target_pairs={{0,1},{1,0},{2,3},{3,2},{4,5},{5,4},{6,7},{7,6},{8,9},{9,8},{10,11... | collective-permute-start | bytes 196616 | tf_op jit(solution)/shard_map/ppermute | solution.py:298
  73.9 4.6 %collective-permute-start.15 = (f32[64,256]{1,0:T(8,128)S(1)}, f32[64,256]{1,0:T(8,128)S(1)}, u32[]{:S(2)}, u32[]{:S(2)}) collective-permute-start(f32[64,256]{1,0:T(8,128)S(1)} %convert_reduce_fusion), channel_id=1, source_target_pairs={{0,2},{1,3},{2,0},{3,1},{4,6},{5,7},{6,4},{7,5},{8,10},{9,11},{10,... | collective-permute-start | bytes 196616 | tf_op jit(solution)/shard_map/ppermute | solution.py:298

commit v8 on v7

--- a/solution.py
+++ b/solution.py
@@ -295,7 +295,9 @@
     mine = jnp.broadcast_to(mine[None], (8,) + mine.shape)
     mine = jnp.sum(lax.all_to_all(mine, "dp", 0, 0, tiled=True).astype(F32), axis=0)
     dom = lax.axis_index("dom")
-    held = [mine] + [lax.ppermute(mine, "dom", [(i, i ^ n) for i in range(8)]) for n in (2, 3, 1)]
+    sent = mine.astype(BF16)
+    held = [lax.ppermute(sent, "dom", [(i, i ^ n) for i in range(8)]).astype(F32) for n in (2, 3, 1)]
+    held = [mine] + held
     by_bits = {0: held[0], 2: held[1], 3: held[2], 1: held[3]}
     far_chip, far_core = lax.bitwise_and(dom, 2) != 0, lax.bitwise_and(dom, 1) != 0
     rows = []

time: 79.4 us -> 77.8 us (0.980)
  waiting for transfers between devices: 18 us -> 16.4 us
    ppermute x3, waiting for transfers between devices: 3.3 us -> 1.65 us  [local(): lax.ppermute(sent, 'dom', [(i, i ^ n) for i in range(8)]).astype(F32)]
where the time goes in v8:
time: 77.8 us; the launch traced here: 77.6 us
  starting transfers between devices  25 us (32%)
  Pallas kernels  17.4 us (22%)
  blocking collectives  17.3 us (22%)
  waiting for transfers between devices  16.4 us (21%)
  other arithmetic  0.81 us (1%)
    all_to_all x1, blocking collectives, local(): lax.all_to_all(mine, 'dp', 0, 0, tiled=True).astype(F32)  17.3 us
    pallas_call x1, Pallas kernels, run_layers(): pl.pallas_call(functools.partial(layers_kernel, scale, betas), in_specs=[...  15.4 us
    ppermute x6, starting transfers between devices, to_phase(): return lax.ppermute(v, 'phase', [(i, (i + n) % 4) for i in range(4)])  8.78 us
    ppermute x4, starting transfers between devices, other_core(): return lax.ppermute(v, 'dom', [(i, i ^ 1) for i in range(8)])  6.32 us
    ppermute x6, waiting for transfers between devices, to_phase(): return lax.ppermute(v, 'phase', [(i, (i + n) % 4) for i in range(4)])  6.27 us
    ppermute x3, starting transfers between devices, local(): lax.ppermute(sent, 'dom', [(i, i ^ n) for i in range(8)]).astype(F32)  4.84 us
    ppermute x1, waiting for transfers between devices, across(): return lax.ppermute(v, 'dom', route)  3.49 us
    ppermute x2, starting transfers between devices, onward(): return lax.ppermute(v, 'dom', route)  3.39 us
  transfers between devices with their start and end apart: 16, of which 8 were waited for; matrix products, arithmetic and copies ran while one was open for 0% of the time, Pallas kernels for 0%

profile of v8, /device:TPU:1, one launch (start us, length us, event | category | flops | bytes accessed | tf_op | source)
XLA Modules:
  0.0 77.6 jit_solution(4193554807244532209)
XLA Ops:
  0.6 0.0 copy-start
  0.6 2.0 %pack.1.refs_0_ = bf16[2320,128]{1,0:T(8,128)(2,1)S(1)} custom-call(bf16[4,1280,128]{2,1,0:T(8,128)(2,1)} %bitcast.12, bf16[4,256,256]{2,1,0:T(8,128)(2,1)} %initial.1, bf16[4,256,256]{2,1,0:T(8,128)(2,1)} %cotangent.1, s32[4,2,5]{2,1,0:T(2,128)} %cols.1), custom_call_target="tpu_custom_call" | custom-call | tf_op jit(solution)/shard_map/pack/pallas_call | solution.py:61
  2.6 3.4 %collective-permute-start.1 = (bf16[2320,128]{1,0:T(8,128)(2,1)S(1)}, bf16[2320,128]{1,0:T(8,128)(2,1)S(1)}, u32[]{:S(2)}, u32[]{:S(2)}) collective-permute-start(bf16[2320,128]{1,0:T(8,128)(2,1)S(1)} %pack.1.refs_0_), channel_id=1, source_target_pairs={{0,2},{1,7},{2,4},{3,1},{4,6},{5,3},{6,0},{7,5},{8,10},{9,15},{10,... | collective-permute-start | bytes 1781768 | tf_op jit(solution)/shard_map/ppermute | solution.py:255
  6.0 0.0 copy-done
  6.0 1.3 %collective-permute-start.3 = (bf16[1,256,256]{2,1,0:T(8,128)(2,1)S(1)}, bf16[1,256,256]{2,1,0:T(8,128)(2,1)S(1)}, u32[]{:S(2)}, u32[]{:S(2)}) collective-permute-start(bf16[1,256,256]{2,1,0:T(8,128)(2,1)S(1)} %copy-done), channel_id=1, source_target_pairs={{0,8},{8,16},{16,24},{24,0},{1,9},{9,17},{17,25},{25,1},{2,10},{10... | collective-permute-start | bytes 393224 | tf_op jit(solution)/shard_map/ppermute | solution.py:263
  7.3 2.6 %collective-permute-start.4 = (bf16[1,256,256]{2,1,0:T(8,128)(2,1)S(1)}, bf16[1,256,256]{2,1,0:T(8,128)(2,1)S(1)}, u32[]{:S(2)}, u32[]{:S(2)}) collective-permute-start(bf16[1,256,256]{2,1,0:T(8,128)(2,1)S(1)} %copy-done), channel_id=1, source_target_pairs={{0,16},{8,24},{16,0},{24,8},{1,17},{9,25},{17,1},{25,9},{2,18},{10... | collective-permute-start | bytes 393224 | tf_op jit(solution)/shard_map/ppermute | solution.py:263
  10.0 1.1 %collective-permute-start.5 = (bf16[1,256,256]{2,1,0:T(8,128)(2,1)S(1)}, bf16[1,256,256]{2,1,0:T(8,128)(2,1)S(1)}, u32[]{:S(2)}, u32[]{:S(2)}) collective-permute-start(bf16[1,256,256]{2,1,0:T(8,128)(2,1)S(1)} %copy-done), channel_id=1, source_target_pairs={{0,24},{8,0},{16,8},{24,16},{1,25},{9,1},{17,9},{25,17},{2,26},{10... | collective-permute-start | bytes 393224 | tf_op jit(solution)/shard_map/ppermute | solution.py:263
  11.0 1.6 %collective-permute-start.2 = (bf16[2320,128]{1,0:T(8,128)(2,1)S(1)}, bf16[2320,128]{1,0:T(8,128)(2,1)S(1)}, u32[]{:S(2)}, u32[]{:S(2)}) collective-permute-start(bf16[2320,128]{1,0:T(8,128)(2,1)S(1)} %pack.1.refs_0_), channel_id=1, source_target_pairs={{0,7},{1,2},{2,1},{3,4},{4,3},{5,6},{6,5},{7,0},{8,15},{9,10},{10,... | collective-permute-start | bytes 1781768 | tf_op jit(solution)/shard_map/ppermute | solution.py:268
  12.6 0.0 collective-permute-done.3.refs_9_
  12.6 4.0 %collective-permute-done.4.refs_10_ = bf16[1,256,256]{2,1,0:T(8,128)(2,1)S(1)} collective-permute-done((bf16[1,256,256]{2,1,0:T(8,128)(2,1)S(1)}, bf16[1,256,256]{2,1,0:T(8,128)(2,1)S(1)}, u32[]{:S(2)}, u32[]{:S(2)}) %collective-permute-start.4) | collective-permute-done | bytes 131104 | tf_op jit(solution)/shard_map/ppermute | solution.py:263
  16.7 0.0 collective-permute-done.5.refs_11_
  16.7 0.0 collective-permute-done.1.refs_2_
  16.7 0.0 collective-permute-start.6
  16.7 1.7 %collective-permute-start = (bf16[2320,128]{1,0:T(8,128)(2,1)S(1)}, bf16[2320,128]{1,0:T(8,128)(2,1)S(1)}, u32[]{:S(2)}, u32[]{:S(2)}) collective-permute-start(bf16[2320,128]{1,0:T(8,128)(2,1)S(1)} %pack.1.refs_0_), channel_id=1, source_target_pairs={{0,1},{1,0},{2,3},{3,2},{4,5},{5,4},{6,7},{7,6},{8,9},{9,8},{10,11... | collective-permute-start | bytes 1781768 | tf_op jit(solution)/shard_map/ppermute | solution.py:259
  18.4 0.0 collective-permute-start.9
  18.4 3.5 %collective-permute-done.2.refs_3_ = bf16[2320,128]{1,0:T(8,128)(2,1)S(1)} collective-permute-done((bf16[2320,128]{1,0:T(8,128)(2,1)S(1)}, bf16[2320,128]{1,0:T(8,128)(2,1)S(1)}, u32[]{:S(2)}, u32[]{:S(2)}) %collective-permute-start.2) | collective-permute-done | bytes 593952 | tf_op jit(solution)/shard_map/ppermute | solution.py:268
  21.9 1.8 %collective-permute-start.8 = (bf16[2320,128]{1,0:T(8,128)(2,1)S(1)}, bf16[2320,128]{1,0:T(8,128)(2,1)S(1)}, u32[]{:S(2)}, u32[]{:S(2)}) collective-permute-start(bf16[2320,128]{1,0:T(8,128)(2,1)S(1)} %collective-permute-done.2.refs_3_), channel_id=1, source_target_pairs={{0,1},{1,0},{2,3},{3,2},{4,5},{5,4},{6,7},{7,6},{8,9},{9,8},{10,11... | collective-permute-start | bytes 1781768 | tf_op jit(solution)/shard_map/ppermute | solution.py:259
  23.7 3.3 %collective-permute-done.6.refs_4_ = bf16[2320,128]{1,0:T(8,128)(2,1)S(1)} collective-permute-done((bf16[2320,128]{1,0:T(8,128)(2,1)S(1)}, bf16[2320,128]{1,0:T(8,128)(2,1)S(1)}, u32[]{:S(2)}, u32[]{:S(2)}) %collective-permute-start.6) | collective-permute-done | bytes 593952 | tf_op jit(solution)/shard_map/ppermute | solution.py:255
  27.0 2.8 %collective-permute-start.7 = (bf16[2320,128]{1,0:T(8,128)(2,1)S(1)}, bf16[2320,128]{1,0:T(8,128)(2,1)S(1)}, u32[]{:S(2)}, u32[]{:S(2)}) collective-permute-start(bf16[2320,128]{1,0:T(8,128)(2,1)S(1)} %collective-permute-done.6.refs_4_), channel_id=1, source_target_pairs={{0,1},{1,0},{2,3},{3,2},{4,5},{5,4},{6,7},{7,6},{8,9},{9,8},{10,11... | collective-permute-start | bytes 1781768 | tf_op jit(solution)/shard_map/ppermute | solution.py:259
  29.8 0.0 collective-permute-done.refs_1_
  29.8 0.0 collective-permute-done.9.refs_7_
  29.8 0.0 collective-permute-done.8.refs_6_
  29.8 1.6 %collective-permute-done.7.refs_5_ = bf16[2320,128]{1,0:T(8,128)(2,1)S(1)} collective-permute-done((bf16[2320,128]{1,0:T(8,128)(2,1)S(1)}, bf16[2320,128]{1,0:T(8,128)(2,1)S(1)}, u32[]{:S(2)}, u32[]{:S(2)}) %collective-permute-start.7) | collective-permute-done | bytes 593952 | tf_op jit(solution)/shard_map/ppermute | solution.py:259
  31.5 15.4 %layers.1 = (f32[1,256,256]{2,1,0:T(8,128)}, bf16[4,64,256]{2,1,0:T(8,128)(2,1)S(1)}) custom-call(bf16[2320,128]{1,0:T(8,128)(2,1)S(1)} %pack.1.refs_0_, bf16[2320,128]{1,0:T(8,128)(2,1)S(1)} %collective-permute-done.refs_1_, bf16[2320,128]{1,0:T(8,128)(2,1)S(1)} %collective-permute-done.1.refs_2_, bf16[2320,128]{1,0:T(8,128)(2,1)S(1)} %collective-permute-done.2.refs_3_, ...), custom_call_target="tpu_custom_call" | custom-call | flops 8999999488 | bytes 6000000 | tf_op jit(solution)/shard_map/layers/pallas_call | solution.py:226
  46.9 0.1 collective-permute-start.10
  46.9 3.1 %collective-permute-start.11 = (bf16[64,256]{1,0:T(8,128)(2,1)S(1)}, bf16[64,256]{1,0:T(8,128)(2,1)S(1)}, u32[]{:S(2)}, u32[]{:S(2)}) collective-permute-start(bf16[64,256]{1,0:T(8,128)(2,1)S(1)} %get-tuple-element.22), channel_id=1, source_target_pairs={{0,16},{8,24},{16,0},{24,8},{1,17},{9,25},{17,1},{25,9},{2,18},{10... | collective-permute-start | bytes 98312 | tf_op jit(solution)/shard_map/ppermute | solution.py:263
  50.1 0.6 collective-permute-start.12
  50.7 0.2 collective-permute-done.10
  50.9 0.9 %collective-permute-done.11 = bf16[64,256]{1,0:T(8,128)(2,1)S(1)} collective-permute-done((bf16[64,256]{1,0:T(8,128)(2,1)S(1)}, bf16[64,256]{1,0:T(8,128)(2,1)S(1)}, u32[]{:S(2)}, u32[]{:S(2)}) %collective-permute-start.11) | collective-permute-done | bytes 32800 | tf_op jit(solution)/shard_map/ppermute | solution.py:263
  51.8 1.1 %collective-permute-done.12 = bf16[64,256]{1,0:T(8,128)(2,1)S(1)} collective-permute-done((bf16[64,256]{1,0:T(8,128)(2,1)S(1)}, bf16[64,256]{1,0:T(8,128)(2,1)S(1)}, u32[]{:S(2)}, u32[]{:S(2)}) %collective-permute-start.12) | collective-permute-done | bytes 32800 | tf_op jit(solution)/shard_map/ppermute | solution.py:263
  53.0 17.3 %all_to_all.5 = bf16[8,64,256]{2,1,0:T(8,128)(2,1)S(1)} all-to-all(bf16[8,64,256]{2,1,0:T(8,128)(2,1)S(1)} %broadcast_in_dim.4), channel_id=1, replica_groups=mesh['dp'=8,'phase'=4,'dom'=8] {'dp'}, dimensions={0} | all-to-all | bytes 524288 | tf_op jit(solution)/shard_map/all_to_all | solution.py:296
  70.4 2.7 %collective-permute-start.13 = (bf16[64,256]{1,0:T(8,128)(2,1)S(1)}, bf16[64,256]{1,0:T(8,128)(2,1)S(1)}, u32[]{:S(2)}, u32[]{:S(2)}) collective-permute-start(bf16[64,256]{1,0:T(8,128)(2,1)S(1)} %convert_element_type.40), channel_id=1, source_target_pairs={{0,3},{1,2},{2,1},{3,0},{4,7},{5,6},{6,5},{7,4},{8,11},{9,10},{10,... | collective-permute-start | bytes 98312 | tf_op jit(solution)/shard_map/ppermute | solution.py:299
  73.0 0.9 %collective-permute-start.14 = (bf16[64,256]{1,0:T(8,128)(2,1)S(1)}, bf16[64,256]{1,0:T(8,128)(2,1)S(1)}, u32[]{:S(2)}, u32[]{:S(2)}) collective-permute-start(bf16[64,256]{1,0:T(8,128)(2,1)S(1)} %convert_element_type.40), channel_id=1, source_target_pairs={{0,1},{1,0},{2,3},{3,2},{4,5},{5,4},{6,7},{7,6},{8,9},{9,8},{10,11... | collective-permute-start | bytes 98312 | tf_op jit(solution)/shard_map/ppermute | solution.py:299
  73.9 1.3 %collective-permute-start.15 = (bf16[64,256]{1,0:T(8,128)(2,1)S(1)}, bf16[64,256]{1,0:T(8,128)(2,1)S(1)}, u32[]{:S(2)}, u32[]{:S(2)}) collective-permute-start(bf16[64,256]{1,0:T(8,128)(2,1)S(1)} %convert_element_type.40), channel_id=1, source_target_pairs={{0,2},{1,3},{2,0},{3,1},{4,6},{5,7},{6,4},{7,5},{8,10},{9,11},{10,... | collective-permute-start | bytes 98312 | tf_op jit(solution)/shard_map/ppermute | solution.py:299
  75.2 0.0 collective-permute-done.13
  75.2 0.0 collective-permute-done.14
  75.2 1.6 %collective-permute-done.15 = bf16[64,256]{1,0:T(8,128)(2,1)S(1)} collective-permute-done((bf16[64,256]{1,0:T(8,128)(2,1)S(1)}, bf16[64,256]{1,0:T(8,128)(2,1)S(1)}, u32[]{:S(2)}, u32[]{:S(2)}) %collective-permute-start.15) | collective-permute-done | bytes 32800 | tf_op jit(solution)/shard_map/ppermute | solution.py:299
  76.9 0.7 maximum_bitcast_fusion
  (6 shorter events, 0.1 us)
Async XLA Ops:
  0.6 5.4 %copy-start = (bf16[1,256,256]{2,1,0:T(8,128)(2,1)S(1)}, bf16[1,256,256]{2,1,0:T(8,128)(2,1)}, u32[]{:S(2)}) copy-start(bf16[1,256,256]{2,1,0:T(8,128)(2,1)} %refs_8_) | copy-start | bytes 393220
  2.6 14.0 %collective-permute-start.1 = (bf16[2320,128]{1,0:T(8,128)(2,1)S(1)}, bf16[2320,128]{1,0:T(8,128)(2,1)S(1)}, u32[]{:S(2)}, u32[]{:S(2)}) collective-permute-start(bf16[2320,128]{1,0:T(8,128)(2,1)S(1)} %pack.1.refs_0_), channel_id=1, source_target_pairs={{0,2},{1,7},{2,4},{3,1},{4,6},{5,3},{6,0},{7,5},{8,10},{9,15},{10,... | collective-permute-start | bytes 1781768 | tf_op jit(solution)/shard_map/ppermute | solution.py:255
  6.0 6.6 %collective-permute-start.3 = (bf16[1,256,256]{2,1,0:T(8,128)(2,1)S(1)}, bf16[1,256,256]{2,1,0:T(8,128)(2,1)S(1)}, u32[]{:S(2)}, u32[]{:S(2)}) collective-permute-start(bf16[1,256,256]{2,1,0:T(8,128)(2,1)S(1)} %copy-done), channel_id=1, source_target_pairs={{0,8},{8,16},{16,24},{24,0},{1,9},{9,17},{17,25},{25,1},{2,10},{10... | collective-permute-start | bytes 393224 | tf_op jit(solution)/shard_map/ppermute | solution.py:263
  7.3 9.3 %collective-permute-start.4 = (bf16[1,256,256]{2,1,0:T(8,128)(2,1)S(1)}, bf16[1,256,256]{2,1,0:T(8,128)(2,1)S(1)}, u32[]{:S(2)}, u32[]{:S(2)}) collective-permute-start(bf16[1,256,256]{2,1,0:T(8,128)(2,1)S(1)} %copy-done), channel_id=1, source_target_pairs={{0,16},{8,24},{16,0},{24,8},{1,17},{9,25},{17,1},{25,9},{2,18},{10... | collective-permute-start | bytes 393224 | tf_op jit(solution)/shard_map/ppermute | solution.py:263
  10.0 6.7 %collective-permute-start.5 = (bf16[1,256,256]{2,1,0:T(8,128)(2,1)S(1)}, bf16[1,256,256]{2,1,0:T(8,128)(2,1)S(1)}, u32[]{:S(2)}, u32[]{:S(2)}) collective-permute-start(bf16[1,256,256]{2,1,0:T(8,128)(2,1)S(1)} %copy-done), channel_id=1, source_target_pairs={{0,24},{8,0},{16,8},{24,16},{1,25},{9,1},{17,9},{25,17},{2,26},{10... | collective-permute-start | bytes 393224 | tf_op jit(solution)/shard_map/ppermute | solution.py:263
  11.0 10.9 %collective-permute-start.2 = (bf16[2320,128]{1,0:T(8,128)(2,1)S(1)}, bf16[2320,128]{1,0:T(8,128)(2,1)S(1)}, u32[]{:S(2)}, u32[]{:S(2)}) collective-permute-start(bf16[2320,128]{1,0:T(8,128)(2,1)S(1)} %pack.1.refs_0_), channel_id=1, source_target_pairs={{0,7},{1,2},{2,1},{3,4},{4,3},{5,6},{6,5},{7,0},{8,15},{9,10},{10,... | collective-permute-start | bytes 1781768 | tf_op jit(solution)/shard_map/ppermute | solution.py:268
  16.7 10.4 %collective-permute-start.6 = (bf16[2320,128]{1,0:T(8,128)(2,1)S(1)}, bf16[2320,128]{1,0:T(8,128)(2,1)S(1)}, u32[]{:S(2)}, u32[]{:S(2)}) collective-permute-start(bf16[2320,128]{1,0:T(8,128)(2,1)S(1)} %collective-permute-done.1.refs_2_), channel_id=1, source_target_pairs={{0,2},{1,7},{2,4},{3,1},{4,6},{5,3},{6,0},{7,5},{8,10},{9,15},{10,... | collective-permute-start | bytes 1781768 | tf_op jit(solution)/shard_map/ppermute | solution.py:255
  16.7 13.2 %collective-permute-start = (bf16[2320,128]{1,0:T(8,128)(2,1)S(1)}, bf16[2320,128]{1,0:T(8,128)(2,1)S(1)}, u32[]{:S(2)}, u32[]{:S(2)}) collective-permute-start(bf16[2320,128]{1,0:T(8,128)(2,1)S(1)} %pack.1.refs_0_), channel_id=1, source_target_pairs={{0,1},{1,0},{2,3},{3,2},{4,5},{5,4},{6,7},{7,6},{8,9},{9,8},{10,11... | collective-permute-start | bytes 1781768 | tf_op jit(solution)/shard_map/ppermute | solution.py:259
  18.4 11.4 %collective-permute-start.9 = (bf16[2320,128]{1,0:T(8,128)(2,1)S(1)}, bf16[2320,128]{1,0:T(8,128)(2,1)S(1)}, u32[]{:S(2)}, u32[]{:S(2)}) collective-permute-start(bf16[2320,128]{1,0:T(8,128)(2,1)S(1)} %collective-permute-done.1.refs_2_), channel_id=1, source_target_pairs={{0,1},{1,0},{2,3},{3,2},{4,5},{5,4},{6,7},{7,6},{8,9},{9,8},{10,11... | collective-permute-start | bytes 1781768 | tf_op jit(solution)/shard_map/ppermute | solution.py:259
  21.9 8.0 %collective-permute-start.8 = (bf16[2320,128]{1,0:T(8,128)(2,1)S(1)}, bf16[2320,128]{1,0:T(8,128)(2,1)S(1)}, u32[]{:S(2)}, u32[]{:S(2)}) collective-permute-start(bf16[2320,128]{1,0:T(8,128)(2,1)S(1)} %collective-permute-done.2.refs_3_), channel_id=1, source_target_pairs={{0,1},{1,0},{2,3},{3,2},{4,5},{5,4},{6,7},{7,6},{8,9},{9,8},{10,11... | collective-permute-start | bytes 1781768 | tf_op jit(solution)/shard_map/ppermute | solution.py:259
  27.0 4.4 %collective-permute-start.7 = (bf16[2320,128]{1,0:T(8,128)(2,1)S(1)}, bf16[2320,128]{1,0:T(8,128)(2,1)S(1)}, u32[]{:S(2)}, u32[]{:S(2)}) collective-permute-start(bf16[2320,128]{1,0:T(8,128)(2,1)S(1)} %collective-permute-done.6.refs_4_), channel_id=1, source_target_pairs={{0,1},{1,0},{2,3},{3,2},{4,5},{5,4},{6,7},{7,6},{8,9},{9,8},{10,11... | collective-permute-start | bytes 1781768 | tf_op jit(solution)/shard_map/ppermute | solution.py:259
  46.9 4.1 %collective-permute-start.10 = (bf16[64,256]{1,0:T(8,128)(2,1)S(1)}, bf16[64,256]{1,0:T(8,128)(2,1)S(1)}, u32[]{:S(2)}, u32[]{:S(2)}) collective-permute-start(bf16[64,256]{1,0:T(8,128)(2,1)S(1)} %get-tuple-element.20), channel_id=1, source_target_pairs={{0,8},{8,16},{16,24},{24,0},{1,9},{9,17},{17,25},{25,1},{2,10},{10... | collective-permute-start | bytes 98312 | tf_op jit(solution)/shard_map/ppermute | solution.py:263
  46.9 4.9 %collective-permute-start.11 = (bf16[64,256]{1,0:T(8,128)(2,1)S(1)}, bf16[64,256]{1,0:T(8,128)(2,1)S(1)}, u32[]{:S(2)}, u32[]{:S(2)}) collective-permute-start(bf16[64,256]{1,0:T(8,128)(2,1)S(1)} %get-tuple-element.22), channel_id=1, source_target_pairs={{0,16},{8,24},{16,0},{24,8},{1,17},{9,25},{17,1},{25,9},{2,18},{10... | collective-permute-start | bytes 98312 | tf_op jit(solution)/shard_map/ppermute | solution.py:263
  50.1 2.8 %collective-permute-start.12 = (bf16[64,256]{1,0:T(8,128)(2,1)S(1)}, bf16[64,256]{1,0:T(8,128)(2,1)S(1)}, u32[]{:S(2)}, u32[]{:S(2)}) collective-permute-start(bf16[64,256]{1,0:T(8,128)(2,1)S(1)} %get-tuple-element.21), channel_id=1, source_target_pairs={{0,24},{8,0},{16,8},{24,16},{1,25},{9,1},{17,9},{25,17},{2,26},{10... | collective-permute-start | bytes 98312 | tf_op jit(solution)/shard_map/ppermute | solution.py:263
  70.4 4.8 %collective-permute-start.13 = (bf16[64,256]{1,0:T(8,128)(2,1)S(1)}, bf16[64,256]{1,0:T(8,128)(2,1)S(1)}, u32[]{:S(2)}, u32[]{:S(2)}) collective-permute-start(bf16[64,256]{1,0:T(8,128)(2,1)S(1)} %convert_element_type.40), channel_id=1, source_target_pairs={{0,3},{1,2},{2,1},{3,0},{4,7},{5,6},{6,5},{7,4},{8,11},{9,10},{10,... | collective-permute-start | bytes 98312 | tf_op jit(solution)/shard_map/ppermute | solution.py:299
  73.0 2.2 %collective-permute-start.14 = (bf16[64,256]{1,0:T(8,128)(2,1)S(1)}, bf16[64,256]{1,0:T(8,128)(2,1)S(1)}, u32[]{:S(2)}, u32[]{:S(2)}) collective-permute-start(bf16[64,256]{1,0:T(8,128)(2,1)S(1)} %convert_element_type.40), channel_id=1, source_target_pairs={{0,1},{1,0},{2,3},{3,2},{4,5},{5,4},{6,7},{7,6},{8,9},{9,8},{10,11... | collective-permute-start | bytes 98312 | tf_op jit(solution)/shard_map/ppermute | solution.py:299
  73.9 2.9 %collective-permute-start.15 = (bf16[64,256]{1,0:T(8,128)(2,1)S(1)}, bf16[64,256]{1,0:T(8,128)(2,1)S(1)}, u32[]{:S(2)}, u32[]{:S(2)}) collective-permute-start(bf16[64,256]{1,0:T(8,128)(2,1)S(1)} %convert_element_type.40), channel_id=1, source_target_pairs={{0,2},{1,3},{2,0},{3,1},{4,6},{5,7},{6,4},{7,5},{8,10},{9,11},{10,... | collective-permute-start | bytes 98312 | tf_op jit(solution)/shard_map/ppermute | solution.py:299

commit v9 on v8

--- a/solution.py
+++ b/solution.py
@@ -295,9 +295,9 @@
     mine = jnp.broadcast_to(mine[None], (8,) + mine.shape)
     mine = jnp.sum(lax.all_to_all(mine, "dp", 0, 0, tiled=True).astype(F32), axis=0)
     dom = lax.axis_index("dom")
-    sent = mine.astype(BF16)
+    sent = lax.optimization_barrier(mine.astype(BF16))
     held = [lax.ppermute(sent, "dom", [(i, i ^ n) for i in range(8)]).astype(F32) for n in (2, 3, 1)]
-    held = [mine] + held
+    held = [sent.astype(F32)] + held
     by_bits = {0: held[0], 2: held[1], 3: held[2], 1: held[3]}
     far_chip, far_core = lax.bitwise_and(dom, 2) != 0, lax.bitwise_and(dom, 1) != 0
     rows = []

time: 77.8 us -> 77.8 us (level)
  no operation moved by 1% of the time
where the time goes in v9:
time: 77.8 us; the launch traced here: 77.6 us
  starting transfers between devices  25 us (32%)
  Pallas kernels  17.4 us (22%)
  blocking collectives  17.4 us (22%)
  waiting for transfers between devices  16.4 us (21%)
  other arithmetic  0.81 us (1%)
    all_to_all x1, blocking collectives, local(): lax.all_to_all(mine, 'dp', 0, 0, tiled=True).astype(F32)  17.4 us
    pallas_call x1, Pallas kernels, run_layers(): pl.pallas_call(functools.partial(layers_kernel, scale, betas), in_specs=[...  15.4 us
    ppermute x6, starting transfers between devices, to_phase(): return lax.ppermute(v, 'phase', [(i, (i + n) % 4) for i in range(4)])  8.78 us
    ppermute x4, starting transfers between devices, other_core(): return lax.ppermute(v, 'dom', [(i, i ^ 1) for i in range(8)])  6.32 us
    ppermute x6, waiting for transfers between devices, to_phase(): return lax.ppermute(v, 'phase', [(i, (i + n) % 4) for i in range(4)])  6.28 us
    ppermute x3, starting transfers between devices, local(): lax.ppermute(sent, 'dom', [(i, i ^ n) for i in range(8)]).astype(F32)  4.84 us
    ppermute x1, waiting for transfers between devices, across(): return lax.ppermute(v, 'dom', route)  3.49 us
    ppermute x2, starting transfers between devices, onward(): return lax.ppermute(v, 'dom', route)  3.39 us
  transfers between devices with their start and end apart: 16, of which 8 were waited for; matrix products, arithmetic and copies ran while one was open for 0% of the time, Pallas kernels for 0%

profile of v9, /device:TPU:1, one launch (start us, length us, event | category | flops | bytes accessed | tf_op | source)
XLA Modules:
  0.0 77.6 jit_solution(3251796215069190065)
XLA Ops:
  0.6 0.0 copy-start
  0.6 2.0 %pack.1.refs_0_ = bf16[2320,128]{1,0:T(8,128)(2,1)S(1)} custom-call(bf16[4,1280,128]{2,1,0:T(8,128)(2,1)} %bitcast.12, bf16[4,256,256]{2,1,0:T(8,128)(2,1)} %initial.1, bf16[4,256,256]{2,1,0:T(8,128)(2,1)} %cotangent.1, s32[4,2,5]{2,1,0:T(2,128)} %cols.1), custom_call_target="tpu_custom_call" | custom-call | tf_op jit(solution)/shard_map/pack/pallas_call | solution.py:61
  2.6 3.4 %collective-permute-start.1 = (bf16[2320,128]{1,0:T(8,128)(2,1)S(1)}, bf16[2320,128]{1,0:T(8,128)(2,1)S(1)}, u32[]{:S(2)}, u32[]{:S(2)}) collective-permute-start(bf16[2320,128]{1,0:T(8,128)(2,1)S(1)} %pack.1.refs_0_), channel_id=1, source_target_pairs={{0,2},{1,7},{2,4},{3,1},{4,6},{5,3},{6,0},{7,5},{8,10},{9,15},{10,... | collective-permute-start | bytes 1781768 | tf_op jit(solution)/shard_map/ppermute | solution.py:255
  6.0 0.0 copy-done
  6.0 1.3 %collective-permute-start.3 = (bf16[1,256,256]{2,1,0:T(8,128)(2,1)S(1)}, bf16[1,256,256]{2,1,0:T(8,128)(2,1)S(1)}, u32[]{:S(2)}, u32[]{:S(2)}) collective-permute-start(bf16[1,256,256]{2,1,0:T(8,128)(2,1)S(1)} %copy-done), channel_id=1, source_target_pairs={{0,8},{8,16},{16,24},{24,0},{1,9},{9,17},{17,25},{25,1},{2,10},{10... | collective-permute-start | bytes 393224 | tf_op jit(solution)/shard_map/ppermute | solution.py:263
  7.3 2.6 %collective-permute-start.4 = (bf16[1,256,256]{2,1,0:T(8,128)(2,1)S(1)}, bf16[1,256,256]{2,1,0:T(8,128)(2,1)S(1)}, u32[]{:S(2)}, u32[]{:S(2)}) collective-permute-start(bf16[1,256,256]{2,1,0:T(8,128)(2,1)S(1)} %copy-done), channel_id=1, source_target_pairs={{0,16},{8,24},{16,0},{24,8},{1,17},{9,25},{17,1},{25,9},{2,18},{10... | collective-permute-start | bytes 393224 | tf_op jit(solution)/shard_map/ppermute | solution.py:263
  10.0 1.1 %collective-permute-start.5 = (bf16[1,256,256]{2,1,0:T(8,128)(2,1)S(1)}, bf16[1,256,256]{2,1,0:T(8,128)(2,1)S(1)}, u32[]{:S(2)}, u32[]{:S(2)}) collective-permute-start(bf16[1,256,256]{2,1,0:T(8,128)(2,1)S(1)} %copy-done), channel_id=1, source_target_pairs={{0,24},{8,0},{16,8},{24,16},{1,25},{9,1},{17,9},{25,17},{2,26},{10... | collective-permute-start | bytes 393224 | tf_op jit(solution)/shard_map/ppermute | solution.py:263
  11.0 1.6 %collective-permute-start.2 = (bf16[2320,128]{1,0:T(8,128)(2,1)S(1)}, bf16[2320,128]{1,0:T(8,128)(2,1)S(1)}, u32[]{:S(2)}, u32[]{:S(2)}) collective-permute-start(bf16[2320,128]{1,0:T(8,128)(2,1)S(1)} %pack.1.refs_0_), channel_id=1, source_target_pairs={{0,7},{1,2},{2,1},{3,4},{4,3},{5,6},{6,5},{7,0},{8,15},{9,10},{10,... | collective-permute-start | bytes 1781768 | tf_op jit(solution)/shard_map/ppermute | solution.py:268
  12.6 0.0 collective-permute-done.3.refs_9_
  12.6 4.0 %collective-permute-done.4.refs_10_ = bf16[1,256,256]{2,1,0:T(8,128)(2,1)S(1)} collective-permute-done((bf16[1,256,256]{2,1,0:T(8,128)(2,1)S(1)}, bf16[1,256,256]{2,1,0:T(8,128)(2,1)S(1)}, u32[]{:S(2)}, u32[]{:S(2)}) %collective-permute-start.4) | collective-permute-done | bytes 131104 | tf_op jit(solution)/shard_map/ppermute | solution.py:263
  16.7 0.0 collective-permute-done.5.refs_11_
  16.7 0.0 collective-permute-done.1.refs_2_
  16.7 0.0 collective-permute-start.6
  16.7 1.7 %collective-permute-start = (bf16[2320,128]{1,0:T(8,128)(2,1)S(1)}, bf16[2320,128]{1,0:T(8,128)(2,1)S(1)}, u32[]{:S(2)}, u32[]{:S(2)}) collective-permute-start(bf16[2320,128]{1,0:T(8,128)(2,1)S(1)} %pack.1.refs_0_), channel_id=1, source_target_pairs={{0,1},{1,0},{2,3},{3,2},{4,5},{5,4},{6,7},{7,6},{8,9},{9,8},{10,11... | collective-permute-start | bytes 1781768 | tf_op jit(solution)/shard_map/ppermute | solution.py:259
  18.4 0.0 collective-permute-start.9
  18.4 3.5 %collective-permute-done.2.refs_3_ = bf16[2320,128]{1,0:T(8,128)(2,1)S(1)} collective-permute-done((bf16[2320,128]{1,0:T(8,128)(2,1)S(1)}, bf16[2320,128]{1,0:T(8,128)(2,1)S(1)}, u32[]{:S(2)}, u32[]{:S(2)}) %collective-permute-start.2) | collective-permute-done | bytes 593952 | tf_op jit(solution)/shard_map/ppermute | solution.py:268
  21.9 1.8 %collective-permute-start.8 = (bf16[2320,128]{1,0:T(8,128)(2,1)S(1)}, bf16[2320,128]{1,0:T(8,128)(2,1)S(1)}, u32[]{:S(2)}, u32[]{:S(2)}) collective-permute-start(bf16[2320,128]{1,0:T(8,128)(2,1)S(1)} %collective-permute-done.2.refs_3_), channel_id=1, source_target_pairs={{0,1},{1,0},{2,3},{3,2},{4,5},{5,4},{6,7},{7,6},{8,9},{9,8},{10,11... | collective-permute-start | bytes 1781768 | tf_op jit(solution)/shard_map/ppermute | solution.py:259
  23.7 3.3 %collective-permute-done.6.refs_4_ = bf16[2320,128]{1,0:T(8,128)(2,1)S(1)} collective-permute-done((bf16[2320,128]{1,0:T(8,128)(2,1)S(1)}, bf16[2320,128]{1,0:T(8,128)(2,1)S(1)}, u32[]{:S(2)}, u32[]{:S(2)}) %collective-permute-start.6) | collective-permute-done | bytes 593952 | tf_op jit(solution)/shard_map/ppermute | solution.py:255
  27.0 2.8 %collective-permute-start.7 = (bf16[2320,128]{1,0:T(8,128)(2,1)S(1)}, bf16[2320,128]{1,0:T(8,128)(2,1)S(1)}, u32[]{:S(2)}, u32[]{:S(2)}) collective-permute-start(bf16[2320,128]{1,0:T(8,128)(2,1)S(1)} %collective-permute-done.6.refs_4_), channel_id=1, source_target_pairs={{0,1},{1,0},{2,3},{3,2},{4,5},{5,4},{6,7},{7,6},{8,9},{9,8},{10,11... | collective-permute-start | bytes 1781768 | tf_op jit(solution)/shard_map/ppermute | solution.py:259
  29.8 0.0 collective-permute-done.refs_1_
  29.8 0.0 collective-permute-done.9.refs_7_
  29.8 0.0 collective-permute-done.8.refs_6_
  29.8 1.6 %collective-permute-done.7.refs_5_ = bf16[2320,128]{1,0:T(8,128)(2,1)S(1)} collective-permute-done((bf16[2320,128]{1,0:T(8,128)(2,1)S(1)}, bf16[2320,128]{1,0:T(8,128)(2,1)S(1)}, u32[]{:S(2)}, u32[]{:S(2)}) %collective-permute-start.7) | collective-permute-done | bytes 593952 | tf_op jit(solution)/shard_map/ppermute | solution.py:259
  31.5 15.4 %layers.1 = (f32[1,256,256]{2,1,0:T(8,128)}, bf16[4,64,256]{2,1,0:T(8,128)(2,1)S(1)}) custom-call(bf16[2320,128]{1,0:T(8,128)(2,1)S(1)} %pack.1.refs_0_, bf16[2320,128]{1,0:T(8,128)(2,1)S(1)} %collective-permute-done.refs_1_, bf16[2320,128]{1,0:T(8,128)(2,1)S(1)} %collective-permute-done.1.refs_2_, bf16[2320,128]{1,0:T(8,128)(2,1)S(1)} %collective-permute-done.2.refs_3_, ...), custom_call_target="tpu_custom_call" | custom-call | flops 8999999488 | bytes 6000000 | tf_op jit(solution)/shard_map/layers/pallas_call | solution.py:226
  46.9 0.1 collective-permute-start.10
  46.9 3.1 %collective-permute-start.11 = (bf16[64,256]{1,0:T(8,128)(2,1)S(1)}, bf16[64,256]{1,0:T(8,128)(2,1)S(1)}, u32[]{:S(2)}, u32[]{:S(2)}) collective-permute-start(bf16[64,256]{1,0:T(8,128)(2,1)S(1)} %get-tuple-element.22), channel_id=1, source_target_pairs={{0,16},{8,24},{16,0},{24,8},{1,17},{9,25},{17,1},{25,9},{2,18},{10... | collective-permute-start | bytes 98312 | tf_op jit(solution)/shard_map/ppermute | solution.py:263
  50.1 0.6 collective-permute-start.12
  50.7 0.3 collective-permute-done.10
  50.9 0.9 %collective-permute-done.11 = bf16[64,256]{1,0:T(8,128)(2,1)S(1)} collective-permute-done((bf16[64,256]{1,0:T(8,128)(2,1)S(1)}, bf16[64,256]{1,0:T(8,128)(2,1)S(1)}, u32[]{:S(2)}, u32[]{:S(2)}) %collective-permute-start.11) | collective-permute-done | bytes 32800 | tf_op jit(solution)/shard_map/ppermute | solution.py:263
  51.8 1.1 %collective-permute-done.12 = bf16[64,256]{1,0:T(8,128)(2,1)S(1)} collective-permute-done((bf16[64,256]{1,0:T(8,128)(2,1)S(1)}, bf16[64,256]{1,0:T(8,128)(2,1)S(1)}, u32[]{:S(2)}, u32[]{:S(2)}) %collective-permute-start.12) | collective-permute-done | bytes 32800 | tf_op jit(solution)/shard_map/ppermute | solution.py:263
  53.0 17.4 %all_to_all.5 = bf16[8,64,256]{2,1,0:T(8,128)(2,1)S(1)} all-to-all(bf16[8,64,256]{2,1,0:T(8,128)(2,1)S(1)} %broadcast_in_dim.4), channel_id=1, replica_groups=mesh['dp'=8,'phase'=4,'dom'=8] {'dp'}, dimensions={0} | all-to-all | bytes 524288 | tf_op jit(solution)/shard_map/all_to_all | solution.py:296
  70.4 2.7 %collective-permute-start.13 = (bf16[64,256]{1,0:T(8,128)(2,1)S(1)}, bf16[64,256]{1,0:T(8,128)(2,1)S(1)}, u32[]{:S(2)}, u32[]{:S(2)}) collective-permute-start(bf16[64,256]{1,0:T(8,128)(2,1)S(1)} %reduce_sum.12), channel_id=1, source_target_pairs={{0,3},{1,2},{2,1},{3,0},{4,7},{5,6},{6,5},{7,4},{8,11},{9,10},{10,... | collective-permute-start | bytes 98312 | tf_op jit(solution)/shard_map/ppermute | solution.py:299
  73.0 0.9 %collective-permute-start.14 = (bf16[64,256]{1,0:T(8,128)(2,1)S(1)}, bf16[64,256]{1,0:T(8,128)(2,1)S(1)}, u32[]{:S(2)}, u32[]{:S(2)}) collective-permute-start(bf16[64,256]{1,0:T(8,128)(2,1)S(1)} %reduce_sum.12), channel_id=1, source_target_pairs={{0,1},{1,0},{2,3},{3,2},{4,5},{5,4},{6,7},{7,6},{8,9},{9,8},{10,11... | collective-permute-start | bytes 98312 | tf_op jit(solution)/shard_map/ppermute | solution.py:299
  73.9 1.3 %collective-permute-start.15 = (bf16[64,256]{1,0:T(8,128)(2,1)S(1)}, bf16[64,256]{1,0:T(8,128)(2,1)S(1)}, u32[]{:S(2)}, u32[]{:S(2)}) collective-permute-start(bf16[64,256]{1,0:T(8,128)(2,1)S(1)} %reduce_sum.12), channel_id=1, source_target_pairs={{0,2},{1,3},{2,0},{3,1},{4,6},{5,7},{6,4},{7,5},{8,10},{9,11},{10,... | collective-permute-start | bytes 98312 | tf_op jit(solution)/shard_map/ppermute | solution.py:299
  75.2 0.0 collective-permute-done.13
  75.2 0.0 collective-permute-done.14
  75.2 1.6 %collective-permute-done.15 = bf16[64,256]{1,0:T(8,128)(2,1)S(1)} collective-permute-done((bf16[64,256]{1,0:T(8,128)(2,1)S(1)}, bf16[64,256]{1,0:T(8,128)(2,1)S(1)}, u32[]{:S(2)}, u32[]{:S(2)}) %collective-permute-start.15) | collective-permute-done | bytes 32800 | tf_op jit(solution)/shard_map/ppermute | solution.py:299
  76.9 0.7 maximum_bitcast_fusion
  (5 shorter events, 0.1 us)
Async XLA Ops:
  0.6 5.4 %copy-start = (bf16[1,256,256]{2,1,0:T(8,128)(2,1)S(1)}, bf16[1,256,256]{2,1,0:T(8,128)(2,1)}, u32[]{:S(2)}) copy-start(bf16[1,256,256]{2,1,0:T(8,128)(2,1)} %refs_8_) | copy-start | bytes 393220
  2.6 14.0 %collective-permute-start.1 = (bf16[2320,128]{1,0:T(8,128)(2,1)S(1)}, bf16[2320,128]{1,0:T(8,128)(2,1)S(1)}, u32[]{:S(2)}, u32[]{:S(2)}) collective-permute-start(bf16[2320,128]{1,0:T(8,128)(2,1)S(1)} %pack.1.refs_0_), channel_id=1, source_target_pairs={{0,2},{1,7},{2,4},{3,1},{4,6},{5,3},{6,0},{7,5},{8,10},{9,15},{10,... | collective-permute-start | bytes 1781768 | tf_op jit(solution)/shard_map/ppermute | solution.py:255
  6.0 6.6 %collective-permute-start.3 = (bf16[1,256,256]{2,1,0:T(8,128)(2,1)S(1)}, bf16[1,256,256]{2,1,0:T(8,128)(2,1)S(1)}, u32[]{:S(2)}, u32[]{:S(2)}) collective-permute-start(bf16[1,256,256]{2,1,0:T(8,128)(2,1)S(1)} %copy-done), channel_id=1, source_target_pairs={{0,8},{8,16},{16,24},{24,0},{1,9},{9,17},{17,25},{25,1},{2,10},{10... | collective-permute-start | bytes 393224 | tf_op jit(solution)/shard_map/ppermute | solution.py:263
  7.3 9.3 %collective-permute-start.4 = (bf16[1,256,256]{2,1,0:T(8,128)(2,1)S(1)}, bf16[1,256,256]{2,1,0:T(8,128)(2,1)S(1)}, u32[]{:S(2)}, u32[]{:S(2)}) collective-permute-start(bf16[1,256,256]{2,1,0:T(8,128)(2,1)S(1)} %copy-done), channel_id=1, source_target_pairs={{0,16},{8,24},{16,0},{24,8},{1,17},{9,25},{17,1},{25,9},{2,18},{10... | collective-permute-start | bytes 393224 | tf_op jit(solution)/shard_map/ppermute | solution.py:263
  10.0 6.7 %collective-permute-start.5 = (bf16[1,256,256]{2,1,0:T(8,128)(2,1)S(1)}, bf16[1,256,256]{2,1,0:T(8,128)(2,1)S(1)}, u32[]{:S(2)}, u32[]{:S(2)}) collective-permute-start(bf16[1,256,256]{2,1,0:T(8,128)(2,1)S(1)} %copy-done), channel_id=1, source_target_pairs={{0,24},{8,0},{16,8},{24,16},{1,25},{9,1},{17,9},{25,17},{2,26},{10... | collective-permute-start | bytes 393224 | tf_op jit(solution)/shard_map/ppermute | solution.py:263
  11.0 10.9 %collective-permute-start.2 = (bf16[2320,128]{1,0:T(8,128)(2,1)S(1)}, bf16[2320,128]{1,0:T(8,128)(2,1)S(1)}, u32[]{:S(2)}, u32[]{:S(2)}) collective-permute-start(bf16[2320,128]{1,0:T(8,128)(2,1)S(1)} %pack.1.refs_0_), channel_id=1, source_target_pairs={{0,7},{1,2},{2,1},{3,4},{4,3},{5,6},{6,5},{7,0},{8,15},{9,10},{10,... | collective-permute-start | bytes 1781768 | tf_op jit(solution)/shard_map/ppermute | solution.py:268
  16.7 10.4 %collective-permute-start.6 = (bf16[2320,128]{1,0:T(8,128)(2,1)S(1)}, bf16[2320,128]{1,0:T(8,128)(2,1)S(1)}, u32[]{:S(2)}, u32[]{:S(2)}) collective-permute-start(bf16[2320,128]{1,0:T(8,128)(2,1)S(1)} %collective-permute-done.1.refs_2_), channel_id=1, source_target_pairs={{0,2},{1,7},{2,4},{3,1},{4,6},{5,3},{6,0},{7,5},{8,10},{9,15},{10,... | collective-permute-start | bytes 1781768 | tf_op jit(solution)/shard_map/ppermute | solution.py:255
  16.7 13.2 %collective-permute-start = (bf16[2320,128]{1,0:T(8,128)(2,1)S(1)}, bf16[2320,128]{1,0:T(8,128)(2,1)S(1)}, u32[]{:S(2)}, u32[]{:S(2)}) collective-permute-start(bf16[2320,128]{1,0:T(8,128)(2,1)S(1)} %pack.1.refs_0_), channel_id=1, source_target_pairs={{0,1},{1,0},{2,3},{3,2},{4,5},{5,4},{6,7},{7,6},{8,9},{9,8},{10,11... | collective-permute-start | bytes 1781768 | tf_op jit(solution)/shard_map/ppermute | solution.py:259
  18.4 11.4 %collective-permute-start.9 = (bf16[2320,128]{1,0:T(8,128)(2,1)S(1)}, bf16[2320,128]{1,0:T(8,128)(2,1)S(1)}, u32[]{:S(2)}, u32[]{:S(2)}) collective-permute-start(bf16[2320,128]{1,0:T(8,128)(2,1)S(1)} %collective-permute-done.1.refs_2_), channel_id=1, source_target_pairs={{0,1},{1,0},{2,3},{3,2},{4,5},{5,4},{6,7},{7,6},{8,9},{9,8},{10,11... | collective-permute-start | bytes 1781768 | tf_op jit(solution)/shard_map/ppermute | solution.py:259
  21.9 8.0 %collective-permute-start.8 = (bf16[2320,128]{1,0:T(8,128)(2,1)S(1)}, bf16[2320,128]{1,0:T(8,128)(2,1)S(1)}, u32[]{:S(2)}, u32[]{:S(2)}) collective-permute-start(bf16[2320,128]{1,0:T(8,128)(2,1)S(1)} %collective-permute-done.2.refs_3_), channel_id=1, source_target_pairs={{0,1},{1,0},{2,3},{3,2},{4,5},{5,4},{6,7},{7,6},{8,9},{9,8},{10,11... | collective-permute-start | bytes 1781768 | tf_op jit(solution)/shard_map/ppermute | solution.py:259
  27.0 4.4 %collective-permute-start.7 = (bf16[2320,128]{1,0:T(8,128)(2,1)S(1)}, bf16[2320,128]{1,0:T(8,128)(2,1)S(1)}, u32[]{:S(2)}, u32[]{:S(2)}) collective-permute-start(bf16[2320,128]{1,0:T(8,128)(2,1)S(1)} %collective-permute-done.6.refs_4_), channel_id=1, source_target_pairs={{0,1},{1,0},{2,3},{3,2},{4,5},{5,4},{6,7},{7,6},{8,9},{9,8},{10,11... | collective-permute-start | bytes 1781768 | tf_op jit(solution)/shard_map/ppermute | solution.py:259
  46.9 4.1 %collective-permute-start.10 = (bf16[64,256]{1,0:T(8,128)(2,1)S(1)}, bf16[64,256]{1,0:T(8,128)(2,1)S(1)}, u32[]{:S(2)}, u32[]{:S(2)}) collective-permute-start(bf16[64,256]{1,0:T(8,128)(2,1)S(1)} %get-tuple-element.20), channel_id=1, source_target_pairs={{0,8},{8,16},{16,24},{24,0},{1,9},{9,17},{17,25},{25,1},{2,10},{10... | collective-permute-start | bytes 98312 | tf_op jit(solution)/shard_map/ppermute | solution.py:263
  46.9 4.9 %collective-permute-start.11 = (bf16[64,256]{1,0:T(8,128)(2,1)S(1)}, bf16[64,256]{1,0:T(8,128)(2,1)S(1)}, u32[]{:S(2)}, u32[]{:S(2)}) collective-permute-start(bf16[64,256]{1,0:T(8,128)(2,1)S(1)} %get-tuple-element.22), channel_id=1, source_target_pairs={{0,16},{8,24},{16,0},{24,8},{1,17},{9,25},{17,1},{25,9},{2,18},{10... | collective-permute-start | bytes 98312 | tf_op jit(solution)/shard_map/ppermute | solution.py:263
  50.1 2.8 %collective-permute-start.12 = (bf16[64,256]{1,0:T(8,128)(2,1)S(1)}, bf16[64,256]{1,0:T(8,128)(2,1)S(1)}, u32[]{:S(2)}, u32[]{:S(2)}) collective-permute-start(bf16[64,256]{1,0:T(8,128)(2,1)S(1)} %get-tuple-element.21), channel_id=1, source_target_pairs={{0,24},{8,0},{16,8},{24,16},{1,25},{9,1},{17,9},{25,17},{2,26},{10... | collective-permute-start | bytes 98312 | tf_op jit(solution)/shard_map/ppermute | solution.py:263
  70.4 4.8 %collective-permute-start.13 = (bf16[64,256]{1,0:T(8,128)(2,1)S(1)}, bf16[64,256]{1,0:T(8,128)(2,1)S(1)}, u32[]{:S(2)}, u32[]{:S(2)}) collective-permute-start(bf16[64,256]{1,0:T(8,128)(2,1)S(1)} %reduce_sum.12), channel_id=1, source_target_pairs={{0,3},{1,2},{2,1},{3,0},{4,7},{5,6},{6,5},{7,4},{8,11},{9,10},{10,... | collective-permute-start | bytes 98312 | tf_op jit(solution)/shard_map/ppermute | solution.py:299
  73.0 2.2 %collective-permute-start.14 = (bf16[64,256]{1,0:T(8,128)(2,1)S(1)}, bf16[64,256]{1,0:T(8,128)(2,1)S(1)}, u32[]{:S(2)}, u32[]{:S(2)}) collective-permute-start(bf16[64,256]{1,0:T(8,128)(2,1)S(1)} %reduce_sum.12), channel_id=1, source_target_pairs={{0,1},{1,0},{2,3},{3,2},{4,5},{5,4},{6,7},{7,6},{8,9},{9,8},{10,11... | collective-permute-start | bytes 98312 | tf_op jit(solution)/shard_map/ppermute | solution.py:299
  73.9 2.9 %collective-permute-start.15 = (bf16[64,256]{1,0:T(8,128)(2,1)S(1)}, bf16[64,256]{1,0:T(8,128)(2,1)S(1)}, u32[]{:S(2)}, u32[]{:S(2)}) collective-permute-start(bf16[64,256]{1,0:T(8,128)(2,1)S(1)} %reduce_sum.12), channel_id=1, source_target_pairs={{0,2},{1,3},{2,0},{3,1},{4,6},{5,7},{6,4},{7,5},{8,10},{9,11},{10,... | collective-permute-start | bytes 98312 | tf_op jit(solution)/shard_map/ppermute | solution.py:299
